TPU v7x, 256 devices: a whole 4x4x8 slice. The times are simulated.
256 devices in a mesh: ctx: 64 (over x, y, z_hi, core), tp: 4 (over z_lo).
Axes of the slice: x: 4, y: 4, z: 8 (z_hi: 2, z_lo: 4; z = z_hi * 4 + z_lo), core: 2. Of those that a mesh axis runs over, the one named last changes fastest.
Arguments:
- stream: bfloat16 [4096, 8192], P('ctx', 'tp'), may hold values from -20 to 20
- se_pregate: bfloat16 [4096, 8192], P('ctx', 'tp'), may hold values from -6 to 6
- se_postgate: bfloat16 [4096, 8192], P('ctx', 'tp'), may hold values from -6 to 6
- se_taps: bfloat16 [8192, 7], P('tp'), may hold values from -2 to 2
- mr_pregate: bfloat16 [4096, 8192], P('ctx', 'tp'), may hold values from -6 to 6
- mr_postgate: bfloat16 [4096, 8192], P('ctx', 'tp'), may hold values from -6 to 6
- mr_taps: bfloat16 [16, 128], P('tp'), may hold values from -0.5 to 0.5
- query_rows: bfloat16 [4096, 4096], P('ctx', 'tp'), may hold values from -120 to 120
- key_rows: bfloat16 [4096, 4096], P('ctx', 'tp'), may hold values from -6 to 6
- value_rows: bfloat16 [4096, 4096], P('ctx', 'tp'), may hold values from -6 to 6
- block_owner: int32 [128, 1], replicated, may hold values from 0 to 63; in each aligned block of 128 rows (0 to 127, 128 to 255, ...) at most 4 rows name the same one
Outputs:
- hyena_stream: bfloat16 [4096, 8192], P('ctx', 'tp')
- attention_out: bfloat16 [4096, 4096], P('ctx', 'tp')
- decode_cache: bfloat16 [8192, 2, 4096], P('ctx', None, 'tp')
- filter_state: bfloat16 [8192, 8192], P('ctx', 'tp')
Inputs may be any that keep to these rules, and one draw needn't show every extreme that they name: `block_owner`: no owner is named by more than 4 tiles; some owner is named by exactly 4.
All inputs are finite; a program needn't handle non-finite values.
Results may differ from a plain program's by a relative error of at most 0.007.
Values may be sent and summed in bfloat16 or wider, within the bound.
No kernel may reach another device: no remote copies, remote signals or barrier semaphores. Data moves between devices by JAX's collectives and lax.ppermute only.
A program may use at most 192 MiB of HBM per device.

v0:
```python
import math

import jax
import jax.numpy as jnp
from jax import lax
from jax.sharding import PartitionSpec as P

HEAD_DIM = 128
CAP = 4


NEG_FILL = -1e30
EPS_NORM = 1e-06


def from_behind(array, axis, by):
    devices = lax.axis_size(axis)
    pairs = [(i, i + by) for i in range(devices) if 0 <= i + by < devices]
    return lax.ppermute(array, axis, pairs)


def shifted(block, axis, distance):
    devices = range(lax.axis_size(axis))
    route = [((i - distance) % len(devices), i) for i in devices]
    return lax.ppermute(block, axis, route)


def mirror_place(rows, start, tok_dev, count):
    rowid = start + jnp.arange(rows, dtype=jnp.int32)
    device = rowid // tok_dev
    within = rowid % tok_dev
    half_rows = tok_dev // 2
    early = device * half_rows + within
    late = (2 * count - 1 - device) * half_rows + within - half_rows
    return jnp.where(within < half_rows, early, late)


def row_scale(signal):
    partial_value = jnp.sum(jnp.square(signal.astype(jnp.float32)), axis=1)
    total = lax.psum(partial_value, "tp")
    width = signal.shape[1] * lax.axis_size("tp")
    return lax.rsqrt(total / width + EPS_NORM)


def short_conv(previous, tiles, taps_in):
    extended = jnp.concatenate([previous, tiles], axis=1).astype(jnp.float32)
    taps = taps_in.astype(jnp.float32)
    depth = taps.shape[1] - 1
    half_rows = tiles.shape[1]
    result = jnp.zeros(tiles.shape, jnp.float32)
    for tap_index in range(depth + 1):
        lower = depth - tap_index
        result = (
            result + taps[:, tap_index][None, None, :] * extended[:, lower : lower + half_rows, :]
        )
    return result


def long_conv(previous, tiles, filters):
    depth = filters.shape[1] - 1
    half_rows = tiles.shape[1]
    group_count = filters.shape[0]
    channels = tiles.shape[2]
    extended = jnp.concatenate([previous, tiles], axis=1)
    row_ids = jnp.arange(half_rows, dtype=jnp.int32)[:, None]
    col_ids = jnp.arange(half_rows + depth, dtype=jnp.int32)[None, :]
    offset = depth + row_ids - col_ids
    valid = (offset >= 0) & (offset <= depth)
    picked = jnp.take(filters, jnp.clip(offset, 0, depth), axis=1)
    toeplitz = jnp.where(valid[None, :, :], picked, jnp.zeros_like(picked))
    grouped = extended.reshape(2, half_rows + depth, group_count, channels // group_count)
    result = jnp.einsum("gts,hsgc->htgc", toeplitz, grouped, preferred_element_type=jnp.float32)
    return result.reshape(2, half_rows, channels)


def context_shifts(early, late, depth, my_index, ctx_count):
    half_rows = early.shape[0]
    reach = -(-depth // half_rows)
    before = []
    for step in range(1, reach + 1):
        before.append(from_behind(early, "ctx", step))
    early_prev = jnp.concatenate(before[::-1], axis=0)[reach * half_rows - depth :]
    own_stack = jnp.stack(before[: reach - 1][::-1] + [early], axis=0)
    payload = jnp.concatenate([own_stack, late[None]], axis=0)
    turned = own_stack
    received_late = []
    for step in range(1, reach + 1):
        received = from_behind(payload, "ctx", -step)
        received_late.append(received[reach])
        turned = jnp.where(my_index == ctx_count - 1 - step, received[:reach], turned)
    after = []
    for step in range(1, reach + 1):
        where_at = jnp.clip(ctx_count - 1 - my_index - step + reach, 0, reach - 1)
        crossing = lax.dynamic_index_in_dim(turned, where_at, 0, keepdims=False)
        after.append(jnp.where(my_index + step <= ctx_count - 1, received_late[step - 1], crossing))
    late_prev = jnp.concatenate(after[::-1], axis=0)[reach * half_rows - depth :]
    return (early_prev, late_prev)


def body(
    stream,
    se_pregate,
    se_postgate,
    se_taps,
    mr_pregate,
    mr_postgate,
    mr_taps,
    query_rows,
    key_rows,
    value_rows,
    block_owner,
):
    ctx_count = lax.axis_size("ctx")
    my_index = lax.axis_index("ctx")
    tok_dev, channels = stream.shape
    half_rows = tok_dev // 2
    scale_one = row_scale(stream)
    se_input = (
        se_pregate.astype(jnp.float32) * stream.astype(jnp.float32) * scale_one[:, None]
    ).astype(jnp.bfloat16)
    se_depth = se_taps.shape[1] - 1
    early_se = se_input[:half_rows]
    late_se = se_input[half_rows:]
    from_before = from_behind(early_se[half_rows - se_depth :], "ctx", 1)
    from_after = from_behind(late_se[half_rows - se_depth :], "ctx", -1)
    late_before = jnp.where(my_index == ctx_count - 1, early_se[half_rows - se_depth :], from_after)
    se_out = short_conv(
        jnp.stack([from_before, late_before]), jnp.stack([early_se, late_se]), se_taps
    )
    mixed = (
        stream.astype(jnp.float32)
        + se_postgate.astype(jnp.float32) * se_out.reshape(tok_dev, channels)
    ).astype(jnp.bfloat16)
    scale_two = row_scale(mixed)
    mr_input = (
        mr_pregate.astype(jnp.float32) * mixed.astype(jnp.float32) * scale_two[:, None]
    ).astype(jnp.bfloat16)
    depth = mr_taps.shape[1] - 1
    early_mr = mr_input[:half_rows]
    late_mr = mr_input[half_rows:]
    early_prev, late_prev = context_shifts(early_mr, late_mr, depth, my_index, ctx_count)
    mr_out = long_conv(jnp.stack([early_prev, late_prev]), jnp.stack([early_mr, late_mr]), mr_taps)
    hyena_stream = (
        mixed.astype(jnp.float32)
        + mr_postgate.astype(jnp.float32) * mr_out.reshape(tok_dev, channels)
    ).astype(jnp.bfloat16)
    tail_rows = jnp.concatenate([late_prev, late_mr], axis=0)[half_rows - 1 :]
    filter_state = jnp.where(my_index == 0, tail_rows, jnp.zeros_like(tail_rows))
    head_cols = query_rows.shape[1]
    heads_here = head_cols // HEAD_DIM
    scale = 1.0 / math.sqrt(HEAD_DIM)
    queries = query_rows.reshape(tok_dev, heads_here, HEAD_DIM)
    query_place = mirror_place(tok_dev, my_index * tok_dev, tok_dev, ctx_count)
    tiles_all = 2 * ctx_count
    tile_ids = jnp.arange(tiles_all, dtype=jnp.int32)
    owners = block_owner[:, 0]
    earlier = tile_ids[:, None] > tile_ids[None, :]
    same = owners[:, None] == owners[None, :]
    ranks = jnp.sum((earlier & same).astype(jnp.int32), axis=1)
    slot_rows = CAP * half_rows
    packed = jnp.stack([key_rows, value_rows], axis=1)

    def attend(carry, piece, start):
        top, total, summed, cache = carry
        rows = piece.shape[0]
        key_place = mirror_place(rows, start, tok_dev, ctx_count)
        keys_here = piece[:, 0].reshape(rows, heads_here, HEAD_DIM)
        values_here = piece[:, 1].reshape(rows, heads_here, HEAD_DIM)
        scores = (
            jnp.einsum("qhd,khd->hqk", queries, keys_here, preferred_element_type=jnp.float32)
            * scale
        )
        allowed = key_place[None, None, :] <= query_place[None, :, None]
        scores = jnp.where(allowed, scores, NEG_FILL)
        new_top = jnp.maximum(top, jnp.max(scores, axis=2))
        weights = jnp.where(allowed, jnp.exp(scores - new_top[:, :, None]), 0.0)
        fade = jnp.exp(top - new_top)
        total = total * fade + jnp.sum(weights, axis=2)
        summed = summed * fade[:, :, None] + jnp.einsum(
            "hqk,khd->hqd",
            weights.astype(jnp.bfloat16),
            values_here,
            preferred_element_type=jnp.float32,
        )
        tile_of = key_place // half_rows
        match = tile_of[:, None] == tile_ids[None, :]
        owner_of = jnp.sum(jnp.where(match, owners[None, :], 0), axis=1)
        rank_of = jnp.sum(jnp.where(match, ranks[None, :], 0), axis=1)
        target = jnp.where(
            owner_of == my_index, rank_of * half_rows + key_place % half_rows, slot_rows
        )
        cache = cache.at[target].set(piece, mode="drop")
        return (new_top, total, summed, cache)

    initial = (
        jnp.full((heads_here, tok_dev), NEG_FILL, jnp.float32),
        jnp.zeros((heads_here, tok_dev), jnp.float32),
        jnp.zeros((heads_here, tok_dev, HEAD_DIM), jnp.float32),
        jnp.zeros((slot_rows, 2, head_cols), jnp.bfloat16),
    )
    first = attend(initial, packed, my_index * tok_dev)

    def pass_on(step, state):
        running, current = state
        current = shifted(current, "ctx", 1)
        source = (my_index - step) % ctx_count
        return (attend(running, current, source * tok_dev), current)

    final, _ = lax.fori_loop(1, ctx_count, pass_on, (first, packed))
    top, total, summed, decode_cache = final
    attention_out = (
        (summed / total[:, :, None])
        .transpose(1, 0, 2)
        .reshape(tok_dev, head_cols)
        .astype(jnp.bfloat16)
    )
    return (hyena_stream, attention_out, decode_cache, filter_state)


def solution(mesh):
    in_specs = (
        P("ctx", "tp"),
        P("ctx", "tp"),
        P("ctx", "tp"),
        P("tp", None),
        P("ctx", "tp"),
        P("ctx", "tp"),
        P("tp", None),
        P("ctx", "tp"),
        P("ctx", "tp"),
        P("ctx", "tp"),
        P(),
    )
    out_specs = (P("ctx", "tp"), P("ctx", "tp"), P("ctx", None, "tp"), P("ctx", "tp"))
    return jax.shard_map(body, mesh=mesh, in_specs=in_specs, out_specs=out_specs, check_vma=False)
```

profile of v0, /device:TPU:8, one launch (start us, length us, event | category | flops | bytes accessed | tf_op | source)
XLA Modules:
  0.0 1268.3 jit_solution(8451829971691901141)
XLA Ops:
  26.5 15.4 %gather_fusion = bf16[5088,4]{1,0:T(8,128)(2,1)S(1)} fusion(bf16[4,128]{0,1:T(8,128)(2,1)S(1)} %copy.54, s32[5120]{0:T(1024)S(1)} %pad_clamp_fusion), kind=kCustom, calls=%fused_computation | custom fusion | bytes 101760 | tf_op jit(solution)/shard_map/jit(_take)/gather | solution.py:69
  89.8 1124.3 %while.25 = (s32[]{:T(128)}, f32[8,64]{1,0:T(8,128)S(1)}, f32[8,64]{1,0:T(8,128)S(1)}, f32[8,64,128]{2,1,0:T(8,128)S(1)}, bf16[128,2,1024]{2,1,0:T(2,128)(2,1)S(...) while((s32[]{:T(128)}, f32[8,64]{1,0:T(8,128)S(1)}, ...), condition=%wide.region_16.17_spmd.clone, body=%wide.region_10.16_spmd.clone.sunk | while | flops 17256656 | bytes 5296458 | solution.py:209
  90.4 33.9 %collective-permute-done = bf16[64,2,1024]{2,0,1:T(8,128)(2,1)S(1)} collective-permute-done((bf16[64,2,1024]{2,0,1:T(8,128)(2,1)S(1)}, bf16[64,2,1024]{2,0,1:T(8,128)(2,1)S(1)}, u32[]{:S(2)}, u32[]{:S(2)}) %collective-permute-start) | collective-permute-done | bytes 262176 | tf_op jit(solution)/shard_map/while/body/eval_jaxpr/ppermute | solution.py:25
  142.3 13.9 %collective-permute-start = (bf16[64,2,1024]{2,0,1:T(8,128)(2,1)S(1)}, bf16[64,2,1024]{2,0,1:T(8,128)(2,1)S(1)}, u32[]{:S(2)}, u32[]{:S(2)}) collective-permute-start(bf16[64,2,1024]{2,0,1:T(8,128)(2,1)S(1)} %get-tuple-element.577), channel_id=1, source_target_pairs={{252,0},{0,4},{4,8},{8,12},{12,16},{16,20},{20,24},{24,28},{28,32}... | collective-permute-start | bytes 786440 | tf_op jit(solution)/shard_map/while/body/eval_jaxpr/ppermute | solution.py:25
  245.7 13.7 %collective-permute-done = bf16[64,2,1024]{2,0,1:T(8,128)(2,1)S(1)} collective-permute-done((bf16[64,2,1024]{2,0,1:T(8,128)(2,1)S(1)}, bf16[64,2,1024]{2,0,1:T(8,128)(2,1)S(1)}, u32[]{:S(2)}, u32[]{:S(2)}) %collective-permute-start) | collective-permute-done | bytes 262176 | tf_op jit(solution)/shard_map/while/body/eval_jaxpr/ppermute | solution.py:25
  263.4 14.0 %collective-permute-done = bf16[64,2,1024]{2,0,1:T(8,128)(2,1)S(1)} collective-permute-done((bf16[64,2,1024]{2,0,1:T(8,128)(2,1)S(1)}, bf16[64,2,1024]{2,0,1:T(8,128)(2,1)S(1)}, u32[]{:S(2)}, u32[]{:S(2)}) %collective-permute-start) | collective-permute-done | bytes 262176 | tf_op jit(solution)/shard_map/while/body/eval_jaxpr/ppermute | solution.py:25
  281.5 14.0 %collective-permute-done = bf16[64,2,1024]{2,0,1:T(8,128)(2,1)S(1)} collective-permute-done((bf16[64,2,1024]{2,0,1:T(8,128)(2,1)S(1)}, bf16[64,2,1024]{2,0,1:T(8,128)(2,1)S(1)}, u32[]{:S(2)}, u32[]{:S(2)}) %collective-permute-start) | collective-permute-done | bytes 262176 | tf_op jit(solution)/shard_map/while/body/eval_jaxpr/ppermute | solution.py:25
  299.6 13.9 %collective-permute-done = bf16[64,2,1024]{2,0,1:T(8,128)(2,1)S(1)} collective-permute-done((bf16[64,2,1024]{2,0,1:T(8,128)(2,1)S(1)}, bf16[64,2,1024]{2,0,1:T(8,128)(2,1)S(1)}, u32[]{:S(2)}, u32[]{:S(2)}) %collective-permute-start) | collective-permute-done | bytes 262176 | tf_op jit(solution)/shard_map/while/body/eval_jaxpr/ppermute | solution.py:25
  351.3 13.6 %collective-permute-done = bf16[64,2,1024]{2,0,1:T(8,128)(2,1)S(1)} collective-permute-done((bf16[64,2,1024]{2,0,1:T(8,128)(2,1)S(1)}, bf16[64,2,1024]{2,0,1:T(8,128)(2,1)S(1)}, u32[]{:S(2)}, u32[]{:S(2)}) %collective-permute-start) | collective-permute-done | bytes 262176 | tf_op jit(solution)/shard_map/while/body/eval_jaxpr/ppermute | solution.py:25
  369.0 13.6 %collective-permute-done = bf16[64,2,1024]{2,0,1:T(8,128)(2,1)S(1)} collective-permute-done((bf16[64,2,1024]{2,0,1:T(8,128)(2,1)S(1)}, bf16[64,2,1024]{2,0,1:T(8,128)(2,1)S(1)}, u32[]{:S(2)}, u32[]{:S(2)}) %collective-permute-start) | collective-permute-done | bytes 262176 | tf_op jit(solution)/shard_map/while/body/eval_jaxpr/ppermute | solution.py:25
  386.7 14.0 %collective-permute-done = bf16[64,2,1024]{2,0,1:T(8,128)(2,1)S(1)} collective-permute-done((bf16[64,2,1024]{2,0,1:T(8,128)(2,1)S(1)}, bf16[64,2,1024]{2,0,1:T(8,128)(2,1)S(1)}, u32[]{:S(2)}, u32[]{:S(2)}) %collective-permute-start) | collective-permute-done | bytes 262176 | tf_op jit(solution)/shard_map/while/body/eval_jaxpr/ppermute | solution.py:25
  404.7 14.0 %collective-permute-done = bf16[64,2,1024]{2,0,1:T(8,128)(2,1)S(1)} collective-permute-done((bf16[64,2,1024]{2,0,1:T(8,128)(2,1)S(1)}, bf16[64,2,1024]{2,0,1:T(8,128)(2,1)S(1)}, u32[]{:S(2)}, u32[]{:S(2)}) %collective-permute-start) | collective-permute-done | bytes 262176 | tf_op jit(solution)/shard_map/while/body/eval_jaxpr/ppermute | solution.py:25
  422.8 13.9 %collective-permute-done = bf16[64,2,1024]{2,0,1:T(8,128)(2,1)S(1)} collective-permute-done((bf16[64,2,1024]{2,0,1:T(8,128)(2,1)S(1)}, bf16[64,2,1024]{2,0,1:T(8,128)(2,1)S(1)}, u32[]{:S(2)}, u32[]{:S(2)}) %collective-permute-start) | collective-permute-done | bytes 262176 | tf_op jit(solution)/shard_map/while/body/eval_jaxpr/ppermute | solution.py:25
  474.7 13.6 %collective-permute-done = bf16[64,2,1024]{2,0,1:T(8,128)(2,1)S(1)} collective-permute-done((bf16[64,2,1024]{2,0,1:T(8,128)(2,1)S(1)}, bf16[64,2,1024]{2,0,1:T(8,128)(2,1)S(1)}, u32[]{:S(2)}, u32[]{:S(2)}) %collective-permute-start) | collective-permute-done | bytes 262176 | tf_op jit(solution)/shard_map/while/body/eval_jaxpr/ppermute | solution.py:25
  492.3 13.6 %collective-permute-done = bf16[64,2,1024]{2,0,1:T(8,128)(2,1)S(1)} collective-permute-done((bf16[64,2,1024]{2,0,1:T(8,128)(2,1)S(1)}, bf16[64,2,1024]{2,0,1:T(8,128)(2,1)S(1)}, u32[]{:S(2)}, u32[]{:S(2)}) %collective-permute-start) | collective-permute-done | bytes 262176 | tf_op jit(solution)/shard_map/while/body/eval_jaxpr/ppermute | solution.py:25
  509.9 13.6 %collective-permute-done = bf16[64,2,1024]{2,0,1:T(8,128)(2,1)S(1)} collective-permute-done((bf16[64,2,1024]{2,0,1:T(8,128)(2,1)S(1)}, bf16[64,2,1024]{2,0,1:T(8,128)(2,1)S(1)}, u32[]{:S(2)}, u32[]{:S(2)}) %collective-permute-start) | collective-permute-done | bytes 262176 | tf_op jit(solution)/shard_map/while/body/eval_jaxpr/ppermute | solution.py:25
  545.1 13.6 %collective-permute-done = bf16[64,2,1024]{2,0,1:T(8,128)(2,1)S(1)} collective-permute-done((bf16[64,2,1024]{2,0,1:T(8,128)(2,1)S(1)}, bf16[64,2,1024]{2,0,1:T(8,128)(2,1)S(1)}, u32[]{:S(2)}, u32[]{:S(2)}) %collective-permute-start) | collective-permute-done | bytes 262176 | tf_op jit(solution)/shard_map/while/body/eval_jaxpr/ppermute | solution.py:25
  562.8 13.6 %collective-permute-done = bf16[64,2,1024]{2,0,1:T(8,128)(2,1)S(1)} collective-permute-done((bf16[64,2,1024]{2,0,1:T(8,128)(2,1)S(1)}, bf16[64,2,1024]{2,0,1:T(8,128)(2,1)S(1)}, u32[]{:S(2)}, u32[]{:S(2)}) %collective-permute-start) | collective-permute-done | bytes 262176 | tf_op jit(solution)/shard_map/while/body/eval_jaxpr/ppermute | solution.py:25
  580.4 13.6 %collective-permute-done = bf16[64,2,1024]{2,0,1:T(8,128)(2,1)S(1)} collective-permute-done((bf16[64,2,1024]{2,0,1:T(8,128)(2,1)S(1)}, bf16[64,2,1024]{2,0,1:T(8,128)(2,1)S(1)}, u32[]{:S(2)}, u32[]{:S(2)}) %collective-permute-start) | collective-permute-done | bytes 262176 | tf_op jit(solution)/shard_map/while/body/eval_jaxpr/ppermute | solution.py:25
  598.0 13.6 %collective-permute-done = bf16[64,2,1024]{2,0,1:T(8,128)(2,1)S(1)} collective-permute-done((bf16[64,2,1024]{2,0,1:T(8,128)(2,1)S(1)}, bf16[64,2,1024]{2,0,1:T(8,128)(2,1)S(1)}, u32[]{:S(2)}, u32[]{:S(2)}) %collective-permute-start) | collective-permute-done | bytes 262176 | tf_op jit(solution)/shard_map/while/body/eval_jaxpr/ppermute | solution.py:25
  615.6 13.6 %collective-permute-done = bf16[64,2,1024]{2,0,1:T(8,128)(2,1)S(1)} collective-permute-done((bf16[64,2,1024]{2,0,1:T(8,128)(2,1)S(1)}, bf16[64,2,1024]{2,0,1:T(8,128)(2,1)S(1)}, u32[]{:S(2)}, u32[]{:S(2)}) %collective-permute-start) | collective-permute-done | bytes 262176 | tf_op jit(solution)/shard_map/while/body/eval_jaxpr/ppermute | solution.py:25
  633.3 13.6 %collective-permute-done = bf16[64,2,1024]{2,0,1:T(8,128)(2,1)S(1)} collective-permute-done((bf16[64,2,1024]{2,0,1:T(8,128)(2,1)S(1)}, bf16[64,2,1024]{2,0,1:T(8,128)(2,1)S(1)}, u32[]{:S(2)}, u32[]{:S(2)}) %collective-permute-start) | collective-permute-done | bytes 262176 | tf_op jit(solution)/shard_map/while/body/eval_jaxpr/ppermute | solution.py:25
  650.8 13.6 %collective-permute-done = bf16[64,2,1024]{2,0,1:T(8,128)(2,1)S(1)} collective-permute-done((bf16[64,2,1024]{2,0,1:T(8,128)(2,1)S(1)}, bf16[64,2,1024]{2,0,1:T(8,128)(2,1)S(1)}, u32[]{:S(2)}, u32[]{:S(2)}) %collective-permute-start) | collective-permute-done | bytes 262176 | tf_op jit(solution)/shard_map/while/body/eval_jaxpr/ppermute | solution.py:25
  668.4 13.6 %collective-permute-done = bf16[64,2,1024]{2,0,1:T(8,128)(2,1)S(1)} collective-permute-done((bf16[64,2,1024]{2,0,1:T(8,128)(2,1)S(1)}, bf16[64,2,1024]{2,0,1:T(8,128)(2,1)S(1)}, u32[]{:S(2)}, u32[]{:S(2)}) %collective-permute-start) | collective-permute-done | bytes 262176 | tf_op jit(solution)/shard_map/while/body/eval_jaxpr/ppermute | solution.py:25
  721.2 13.6 %collective-permute-done = bf16[64,2,1024]{2,0,1:T(8,128)(2,1)S(1)} collective-permute-done((bf16[64,2,1024]{2,0,1:T(8,128)(2,1)S(1)}, bf16[64,2,1024]{2,0,1:T(8,128)(2,1)S(1)}, u32[]{:S(2)}, u32[]{:S(2)}) %collective-permute-start) | collective-permute-done | bytes 262176 | tf_op jit(solution)/shard_map/while/body/eval_jaxpr/ppermute | solution.py:25
  738.9 13.6 %collective-permute-done = bf16[64,2,1024]{2,0,1:T(8,128)(2,1)S(1)} collective-permute-done((bf16[64,2,1024]{2,0,1:T(8,128)(2,1)S(1)}, bf16[64,2,1024]{2,0,1:T(8,128)(2,1)S(1)}, u32[]{:S(2)}, u32[]{:S(2)}) %collective-permute-start) | collective-permute-done | bytes 262176 | tf_op jit(solution)/shard_map/while/body/eval_jaxpr/ppermute | solution.py:25
  756.5 13.6 %collective-permute-done = bf16[64,2,1024]{2,0,1:T(8,128)(2,1)S(1)} collective-permute-done((bf16[64,2,1024]{2,0,1:T(8,128)(2,1)S(1)}, bf16[64,2,1024]{2,0,1:T(8,128)(2,1)S(1)}, u32[]{:S(2)}, u32[]{:S(2)}) %collective-permute-start) | collective-permute-done | bytes 262176 | tf_op jit(solution)/shard_map/while/body/eval_jaxpr/ppermute | solution.py:25
  791.7 13.6 %collective-permute-done = bf16[64,2,1024]{2,0,1:T(8,128)(2,1)S(1)} collective-permute-done((bf16[64,2,1024]{2,0,1:T(8,128)(2,1)S(1)}, bf16[64,2,1024]{2,0,1:T(8,128)(2,1)S(1)}, u32[]{:S(2)}, u32[]{:S(2)}) %collective-permute-start) | collective-permute-done | bytes 262176 | tf_op jit(solution)/shard_map/while/body/eval_jaxpr/ppermute | solution.py:25
  809.4 13.6 %collective-permute-done = bf16[64,2,1024]{2,0,1:T(8,128)(2,1)S(1)} collective-permute-done((bf16[64,2,1024]{2,0,1:T(8,128)(2,1)S(1)}, bf16[64,2,1024]{2,0,1:T(8,128)(2,1)S(1)}, u32[]{:S(2)}, u32[]{:S(2)}) %collective-permute-start) | collective-permute-done | bytes 262176 | tf_op jit(solution)/shard_map/while/body/eval_jaxpr/ppermute | solution.py:25
  827.0 13.6 %collective-permute-done = bf16[64,2,1024]{2,0,1:T(8,128)(2,1)S(1)} collective-permute-done((bf16[64,2,1024]{2,0,1:T(8,128)(2,1)S(1)}, bf16[64,2,1024]{2,0,1:T(8,128)(2,1)S(1)}, u32[]{:S(2)}, u32[]{:S(2)}) %collective-permute-start) | collective-permute-done | bytes 262176 | tf_op jit(solution)/shard_map/while/body/eval_jaxpr/ppermute | solution.py:25
  844.6 13.6 %collective-permute-done = bf16[64,2,1024]{2,0,1:T(8,128)(2,1)S(1)} collective-permute-done((bf16[64,2,1024]{2,0,1:T(8,128)(2,1)S(1)}, bf16[64,2,1024]{2,0,1:T(8,128)(2,1)S(1)}, u32[]{:S(2)}, u32[]{:S(2)}) %collective-permute-start) | collective-permute-done | bytes 262176 | tf_op jit(solution)/shard_map/while/body/eval_jaxpr/ppermute | solution.py:25
  862.2 13.6 %collective-permute-done = bf16[64,2,1024]{2,0,1:T(8,128)(2,1)S(1)} collective-permute-done((bf16[64,2,1024]{2,0,1:T(8,128)(2,1)S(1)}, bf16[64,2,1024]{2,0,1:T(8,128)(2,1)S(1)}, u32[]{:S(2)}, u32[]{:S(2)}) %collective-permute-start) | collective-permute-done | bytes 262176 | tf_op jit(solution)/shard_map/while/body/eval_jaxpr/ppermute | solution.py:25
  897.4 13.6 %collective-permute-done = bf16[64,2,1024]{2,0,1:T(8,128)(2,1)S(1)} collective-permute-done((bf16[64,2,1024]{2,0,1:T(8,128)(2,1)S(1)}, bf16[64,2,1024]{2,0,1:T(8,128)(2,1)S(1)}, u32[]{:S(2)}, u32[]{:S(2)}) %collective-permute-start) | collective-permute-done | bytes 262176 | tf_op jit(solution)/shard_map/while/body/eval_jaxpr/ppermute | solution.py:25
  932.5 13.6 %collective-permute-done = bf16[64,2,1024]{2,0,1:T(8,128)(2,1)S(1)} collective-permute-done((bf16[64,2,1024]{2,0,1:T(8,128)(2,1)S(1)}, bf16[64,2,1024]{2,0,1:T(8,128)(2,1)S(1)}, u32[]{:S(2)}, u32[]{:S(2)}) %collective-permute-start) | collective-permute-done | bytes 262176 | tf_op jit(solution)/shard_map/while/body/eval_jaxpr/ppermute | solution.py:25
  950.2 13.6 %collective-permute-done = bf16[64,2,1024]{2,0,1:T(8,128)(2,1)S(1)} collective-permute-done((bf16[64,2,1024]{2,0,1:T(8,128)(2,1)S(1)}, bf16[64,2,1024]{2,0,1:T(8,128)(2,1)S(1)}, u32[]{:S(2)}, u32[]{:S(2)}) %collective-permute-start) | collective-permute-done | bytes 262176 | tf_op jit(solution)/shard_map/while/body/eval_jaxpr/ppermute | solution.py:25
  967.9 13.6 %collective-permute-done = bf16[64,2,1024]{2,0,1:T(8,128)(2,1)S(1)} collective-permute-done((bf16[64,2,1024]{2,0,1:T(8,128)(2,1)S(1)}, bf16[64,2,1024]{2,0,1:T(8,128)(2,1)S(1)}, u32[]{:S(2)}, u32[]{:S(2)}) %collective-permute-start) | collective-permute-done | bytes 262176 | tf_op jit(solution)/shard_map/while/body/eval_jaxpr/ppermute | solution.py:25
  985.5 13.6 %collective-permute-done = bf16[64,2,1024]{2,0,1:T(8,128)(2,1)S(1)} collective-permute-done((bf16[64,2,1024]{2,0,1:T(8,128)(2,1)S(1)}, bf16[64,2,1024]{2,0,1:T(8,128)(2,1)S(1)}, u32[]{:S(2)}, u32[]{:S(2)}) %collective-permute-start) | collective-permute-done | bytes 262176 | tf_op jit(solution)/shard_map/while/body/eval_jaxpr/ppermute | solution.py:25
  1003.0 13.6 %collective-permute-done = bf16[64,2,1024]{2,0,1:T(8,128)(2,1)S(1)} collective-permute-done((bf16[64,2,1024]{2,0,1:T(8,128)(2,1)S(1)}, bf16[64,2,1024]{2,0,1:T(8,128)(2,1)S(1)}, u32[]{:S(2)}, u32[]{:S(2)}) %collective-permute-start) | collective-permute-done | bytes 262176 | tf_op jit(solution)/shard_map/while/body/eval_jaxpr/ppermute | solution.py:25
  1020.7 13.6 %collective-permute-done = bf16[64,2,1024]{2,0,1:T(8,128)(2,1)S(1)} collective-permute-done((bf16[64,2,1024]{2,0,1:T(8,128)(2,1)S(1)}, bf16[64,2,1024]{2,0,1:T(8,128)(2,1)S(1)}, u32[]{:S(2)}, u32[]{:S(2)}) %collective-permute-start) | collective-permute-done | bytes 262176 | tf_op jit(solution)/shard_map/while/body/eval_jaxpr/ppermute | solution.py:25
  1055.9 13.6 %collective-permute-done = bf16[64,2,1024]{2,0,1:T(8,128)(2,1)S(1)} collective-permute-done((bf16[64,2,1024]{2,0,1:T(8,128)(2,1)S(1)}, bf16[64,2,1024]{2,0,1:T(8,128)(2,1)S(1)}, u32[]{:S(2)}, u32[]{:S(2)}) %collective-permute-start) | collective-permute-done | bytes 262176 | tf_op jit(solution)/shard_map/while/body/eval_jaxpr/ppermute | solution.py:25
  1091.1 13.6 %collective-permute-done = bf16[64,2,1024]{2,0,1:T(8,128)(2,1)S(1)} collective-permute-done((bf16[64,2,1024]{2,0,1:T(8,128)(2,1)S(1)}, bf16[64,2,1024]{2,0,1:T(8,128)(2,1)S(1)}, u32[]{:S(2)}, u32[]{:S(2)}) %collective-permute-start) | collective-permute-done | bytes 262176 | tf_op jit(solution)/shard_map/while/body/eval_jaxpr/ppermute | solution.py:25
  1108.8 13.6 %collective-permute-done = bf16[64,2,1024]{2,0,1:T(8,128)(2,1)S(1)} collective-permute-done((bf16[64,2,1024]{2,0,1:T(8,128)(2,1)S(1)}, bf16[64,2,1024]{2,0,1:T(8,128)(2,1)S(1)}, u32[]{:S(2)}, u32[]{:S(2)}) %collective-permute-start) | collective-permute-done | bytes 262176 | tf_op jit(solution)/shard_map/while/body/eval_jaxpr/ppermute | solution.py:25
  1126.4 13.6 %collective-permute-done = bf16[64,2,1024]{2,0,1:T(8,128)(2,1)S(1)} collective-permute-done((bf16[64,2,1024]{2,0,1:T(8,128)(2,1)S(1)}, bf16[64,2,1024]{2,0,1:T(8,128)(2,1)S(1)}, u32[]{:S(2)}, u32[]{:S(2)}) %collective-permute-start) | collective-permute-done | bytes 262176 | tf_op jit(solution)/shard_map/while/body/eval_jaxpr/ppermute | solution.py:25
  1144.1 13.6 %collective-permute-done = bf16[64,2,1024]{2,0,1:T(8,128)(2,1)S(1)} collective-permute-done((bf16[64,2,1024]{2,0,1:T(8,128)(2,1)S(1)}, bf16[64,2,1024]{2,0,1:T(8,128)(2,1)S(1)}, u32[]{:S(2)}, u32[]{:S(2)}) %collective-permute-start) | collective-permute-done | bytes 262176 | tf_op jit(solution)/shard_map/while/body/eval_jaxpr/ppermute | solution.py:25
  1161.7 13.6 %collective-permute-done = bf16[64,2,1024]{2,0,1:T(8,128)(2,1)S(1)} collective-permute-done((bf16[64,2,1024]{2,0,1:T(8,128)(2,1)S(1)}, bf16[64,2,1024]{2,0,1:T(8,128)(2,1)S(1)}, u32[]{:S(2)}, u32[]{:S(2)}) %collective-permute-start) | collective-permute-done | bytes 262176 | tf_op jit(solution)/shard_map/while/body/eval_jaxpr/ppermute | solution.py:25
  1179.3 13.6 %collective-permute-done = bf16[64,2,1024]{2,0,1:T(8,128)(2,1)S(1)} collective-permute-done((bf16[64,2,1024]{2,0,1:T(8,128)(2,1)S(1)}, bf16[64,2,1024]{2,0,1:T(8,128)(2,1)S(1)}, u32[]{:S(2)}, u32[]{:S(2)}) %collective-permute-start) | collective-permute-done | bytes 262176 | tf_op jit(solution)/shard_map/while/body/eval_jaxpr/ppermute | solution.py:25
  1196.9 13.6 %collective-permute-done = bf16[64,2,1024]{2,0,1:T(8,128)(2,1)S(1)} collective-permute-done((bf16[64,2,1024]{2,0,1:T(8,128)(2,1)S(1)}, bf16[64,2,1024]{2,0,1:T(8,128)(2,1)S(1)}, u32[]{:S(2)}, u32[]{:S(2)}) %collective-permute-start) | collective-permute-done | bytes 262176 | tf_op jit(solution)/shard_map/while/body/eval_jaxpr/ppermute | solution.py:25
  1216.9 42.1 %collective-permute-done.3 = bf16[32,2048]{1,0:T(8,128)(2,1)S(1)} collective-permute-done((bf16[32,2048]{1,0:T(8,128)(2,1)S(1)}, bf16[32,2048]{1,0:T(8,128)(2,1)S(1)}, u32[]{:S(2)}, u32[]{:S(2)}) %collective-permute-start.3) | collective-permute-done | bytes 131104 | tf_op jit(solution)/shard_map/ppermute | solution.py:19
  (1258 shorter events, 566.9 us)
Async XLA Ops:
  21.7 24.7 %collective-permute-start.1 = (bf16[6,2048]{1,0:T(8,128)(2,1)S(1)}, bf16[6,2048]{1,0:T(8,128)(2,1)S(1)}, u32[]{:S(2)}, u32[]{:S(2)}) collective-permute-start(bf16[6,2048]{1,0:T(8,128)(2,1)S(1)} %get-tuple-element.451), channel_id=1, source_target_pairs={{0,4},{4,8},{8,12},{12,16},{16,20},{20,24},{24,28},{28,32},{32,36}... | collective-permute-start | bytes 73736 | tf_op jit(solution)/shard_map/ppermute | solution.py:19
  61.2 14.6 %collective-permute-start.5 = (bf16[32,2048]{1,0:T(8,128)(2,1)S(1)}, bf16[32,2048]{1,0:T(8,128)(2,1)S(1)}, u32[]{:S(2)}, u32[]{:S(2)}) collective-permute-start(bf16[32,2048]{1,0:T(8,128)(2,1)S(1)} %get-tuple-element.450), channel_id=1, source_target_pairs={{0,8},{4,12},{8,16},{12,20},{16,24},{20,28},{24,32},{28,36},{32,40... | collective-permute-start | bytes 393224 | tf_op jit(solution)/shard_map/ppermute | solution.py:19
  79.9 1179.3 %collective-permute-start.7 = (bf16[5,32,2048]{2,1,0:T(8,128)(2,1)}, bf16[5,32,2048]{2,1,0:T(8,128)(2,1)S(1)}, u32[]{:S(2)}, u32[]{:S(2)}) collective-permute-start(bf16[5,32,2048]{2,1,0:T(8,128)(2,1)} %constant_dynamic-update-slice_fusion), channel_id=1, source_target_pairs={{16,0},{20,4},{24,8},{28,12},{32,16},{36,20},{40,24},{44,28},{48,3... | collective-permute-start | bytes 1966088 | tf_op jit(solution)/shard_map/ppermute | solution.py:19
  81.8 1177.4 %collective-permute-start.10 = (bf16[5,32,2048]{2,1,0:T(8,128)(2,1)}, bf16[5,32,2048]{2,1,0:T(8,128)(2,1)}, u32[]{:S(2)}, u32[]{:S(2)}) collective-permute-start(bf16[5,32,2048]{2,1,0:T(8,128)(2,1)} %constant_dynamic-update-slice_fusion), channel_id=1, source_target_pairs={{4,0},{8,4},{12,8},{16,12},{20,16},{24,20},{28,24},{32,28},{36,32}... | collective-permute-start | bytes 1966088 | tf_op jit(solution)/shard_map/ppermute | solution.py:19
  84.3 1174.9 %collective-permute-start.9 = (bf16[5,32,2048]{2,1,0:T(8,128)(2,1)}, bf16[5,32,2048]{2,1,0:T(8,128)(2,1)}, u32[]{:S(2)}, u32[]{:S(2)}) collective-permute-start(bf16[5,32,2048]{2,1,0:T(8,128)(2,1)} %constant_dynamic-update-slice_fusion), channel_id=1, source_target_pairs={{8,0},{12,4},{16,8},{20,12},{24,16},{28,20},{32,24},{36,28},{40,32... | collective-permute-start | bytes 1966088 | tf_op jit(solution)/shard_map/ppermute | solution.py:19
  87.8 1171.4 %collective-permute-start.8 = (bf16[5,32,2048]{2,1,0:T(8,128)(2,1)}, bf16[5,32,2048]{2,1,0:T(8,128)(2,1)}, u32[]{:S(2)}, u32[]{:S(2)}) collective-permute-start(bf16[5,32,2048]{2,1,0:T(8,128)(2,1)} %constant_dynamic-update-slice_fusion), channel_id=1, source_target_pairs={{12,0},{16,4},{20,8},{24,12},{28,16},{32,20},{36,24},{40,28},{44,3... | collective-permute-start | bytes 1966088 | tf_op jit(solution)/shard_map/ppermute | solution.py:19
  89.8 34.6 %collective-permute-start = (bf16[64,2,1024]{2,0,1:T(8,128)(2,1)S(1)}, bf16[64,2,1024]{2,0,1:T(8,128)(2,1)S(1)}, u32[]{:S(2)}, u32[]{:S(2)}) collective-permute-start(bf16[64,2,1024]{2,0,1:T(8,128)(2,1)S(1)} %get-tuple-element.577), channel_id=1, source_target_pairs={{252,0},{0,4},{4,8},{8,12},{12,16},{16,20},{20,24},{24,28},{28,32}... | collective-permute-start | bytes 786440 | tf_op jit(solution)/shard_map/while/body/eval_jaxpr/ppermute | solution.py:25
  142.3 15.0 %collective-permute-start = (bf16[64,2,1024]{2,0,1:T(8,128)(2,1)S(1)}, bf16[64,2,1024]{2,0,1:T(8,128)(2,1)S(1)}, u32[]{:S(2)}, u32[]{:S(2)}) collective-permute-start(bf16[64,2,1024]{2,0,1:T(8,128)(2,1)S(1)} %get-tuple-element.577), channel_id=1, source_target_pairs={{252,0},{0,4},{4,8},{8,12},{12,16},{16,20},{20,24},{24,28},{28,32}... | collective-permute-start | bytes 786440 | tf_op jit(solution)/shard_map/while/body/eval_jaxpr/ppermute | solution.py:25
  209.1 14.9 %collective-permute-start = (bf16[64,2,1024]{2,0,1:T(8,128)(2,1)S(1)}, bf16[64,2,1024]{2,0,1:T(8,128)(2,1)S(1)}, u32[]{:S(2)}, u32[]{:S(2)}) collective-permute-start(bf16[64,2,1024]{2,0,1:T(8,128)(2,1)S(1)} %get-tuple-element.577), channel_id=1, source_target_pairs={{252,0},{0,4},{4,8},{8,12},{12,16},{16,20},{20,24},{24,28},{28,32}... | collective-permute-start | bytes 786440 | tf_op jit(solution)/shard_map/while/body/eval_jaxpr/ppermute | solution.py:25
  227.5 14.1 %collective-permute-start = (bf16[64,2,1024]{2,0,1:T(8,128)(2,1)S(1)}, bf16[64,2,1024]{2,0,1:T(8,128)(2,1)S(1)}, u32[]{:S(2)}, u32[]{:S(2)}) collective-permute-start(bf16[64,2,1024]{2,0,1:T(8,128)(2,1)S(1)} %get-tuple-element.577), channel_id=1, source_target_pairs={{252,0},{0,4},{4,8},{8,12},{12,16},{16,20},{20,24},{24,28},{28,32}... | collective-permute-start | bytes 786440 | tf_op jit(solution)/shard_map/while/body/eval_jaxpr/ppermute | solution.py:25
  245.3 14.1 %collective-permute-start = (bf16[64,2,1024]{2,0,1:T(8,128)(2,1)S(1)}, bf16[64,2,1024]{2,0,1:T(8,128)(2,1)S(1)}, u32[]{:S(2)}, u32[]{:S(2)}) collective-permute-start(bf16[64,2,1024]{2,0,1:T(8,128)(2,1)S(1)} %get-tuple-element.577), channel_id=1, source_target_pairs={{252,0},{0,4},{4,8},{8,12},{12,16},{16,20},{20,24},{24,28},{28,32}... | collective-permute-start | bytes 786440 | tf_op jit(solution)/shard_map/while/body/eval_jaxpr/ppermute | solution.py:25
  263.0 14.4 %collective-permute-start = (bf16[64,2,1024]{2,0,1:T(8,128)(2,1)S(1)}, bf16[64,2,1024]{2,0,1:T(8,128)(2,1)S(1)}, u32[]{:S(2)}, u32[]{:S(2)}) collective-permute-start(bf16[64,2,1024]{2,0,1:T(8,128)(2,1)S(1)} %get-tuple-element.577), channel_id=1, source_target_pairs={{252,0},{0,4},{4,8},{8,12},{12,16},{16,20},{20,24},{24,28},{28,32}... | collective-permute-start | bytes 786440 | tf_op jit(solution)/shard_map/while/body/eval_jaxpr/ppermute | solution.py:25
  281.1 14.4 %collective-permute-start = (bf16[64,2,1024]{2,0,1:T(8,128)(2,1)S(1)}, bf16[64,2,1024]{2,0,1:T(8,128)(2,1)S(1)}, u32[]{:S(2)}, u32[]{:S(2)}) collective-permute-start(bf16[64,2,1024]{2,0,1:T(8,128)(2,1)S(1)} %get-tuple-element.577), channel_id=1, source_target_pairs={{252,0},{0,4},{4,8},{8,12},{12,16},{16,20},{20,24},{24,28},{28,32}... | collective-permute-start | bytes 786440 | tf_op jit(solution)/shard_map/while/body/eval_jaxpr/ppermute | solution.py:25
  299.1 14.3 %collective-permute-start = (bf16[64,2,1024]{2,0,1:T(8,128)(2,1)S(1)}, bf16[64,2,1024]{2,0,1:T(8,128)(2,1)S(1)}, u32[]{:S(2)}, u32[]{:S(2)}) collective-permute-start(bf16[64,2,1024]{2,0,1:T(8,128)(2,1)S(1)} %get-tuple-element.577), channel_id=1, source_target_pairs={{252,0},{0,4},{4,8},{8,12},{12,16},{16,20},{20,24},{24,28},{28,32}... | collective-permute-start | bytes 786440 | tf_op jit(solution)/shard_map/while/body/eval_jaxpr/ppermute | solution.py:25
  350.9 14.0 %collective-permute-start = (bf16[64,2,1024]{2,0,1:T(8,128)(2,1)S(1)}, bf16[64,2,1024]{2,0,1:T(8,128)(2,1)S(1)}, u32[]{:S(2)}, u32[]{:S(2)}) collective-permute-start(bf16[64,2,1024]{2,0,1:T(8,128)(2,1)S(1)} %get-tuple-element.577), channel_id=1, source_target_pairs={{252,0},{0,4},{4,8},{8,12},{12,16},{16,20},{20,24},{24,28},{28,32}... | collective-permute-start | bytes 786440 | tf_op jit(solution)/shard_map/while/body/eval_jaxpr/ppermute | solution.py:25
  368.5 14.1 %collective-permute-start = (bf16[64,2,1024]{2,0,1:T(8,128)(2,1)S(1)}, bf16[64,2,1024]{2,0,1:T(8,128)(2,1)S(1)}, u32[]{:S(2)}, u32[]{:S(2)}) collective-permute-start(bf16[64,2,1024]{2,0,1:T(8,128)(2,1)S(1)} %get-tuple-element.577), channel_id=1, source_target_pairs={{252,0},{0,4},{4,8},{8,12},{12,16},{16,20},{20,24},{24,28},{28,32}... | collective-permute-start | bytes 786440 | tf_op jit(solution)/shard_map/while/body/eval_jaxpr/ppermute | solution.py:25
  386.2 14.4 %collective-permute-start = (bf16[64,2,1024]{2,0,1:T(8,128)(2,1)S(1)}, bf16[64,2,1024]{2,0,1:T(8,128)(2,1)S(1)}, u32[]{:S(2)}, u32[]{:S(2)}) collective-permute-start(bf16[64,2,1024]{2,0,1:T(8,128)(2,1)S(1)} %get-tuple-element.577), channel_id=1, source_target_pairs={{252,0},{0,4},{4,8},{8,12},{12,16},{16,20},{20,24},{24,28},{28,32}... | collective-permute-start | bytes 786440 | tf_op jit(solution)/shard_map/while/body/eval_jaxpr/ppermute | solution.py:25
  404.3 14.4 %collective-permute-start = (bf16[64,2,1024]{2,0,1:T(8,128)(2,1)S(1)}, bf16[64,2,1024]{2,0,1:T(8,128)(2,1)S(1)}, u32[]{:S(2)}, u32[]{:S(2)}) collective-permute-start(bf16[64,2,1024]{2,0,1:T(8,128)(2,1)S(1)} %get-tuple-element.577), channel_id=1, source_target_pairs={{252,0},{0,4},{4,8},{8,12},{12,16},{16,20},{20,24},{24,28},{28,32}... | collective-permute-start | bytes 786440 | tf_op jit(solution)/shard_map/while/body/eval_jaxpr/ppermute | solution.py:25
  422.4 14.3 %collective-permute-start = (bf16[64,2,1024]{2,0,1:T(8,128)(2,1)S(1)}, bf16[64,2,1024]{2,0,1:T(8,128)(2,1)S(1)}, u32[]{:S(2)}, u32[]{:S(2)}) collective-permute-start(bf16[64,2,1024]{2,0,1:T(8,128)(2,1)S(1)} %get-tuple-element.577), channel_id=1, source_target_pairs={{252,0},{0,4},{4,8},{8,12},{12,16},{16,20},{20,24},{24,28},{28,32}... | collective-permute-start | bytes 786440 | tf_op jit(solution)/shard_map/while/body/eval_jaxpr/ppermute | solution.py:25
  474.2 14.0 %collective-permute-start = (bf16[64,2,1024]{2,0,1:T(8,128)(2,1)S(1)}, bf16[64,2,1024]{2,0,1:T(8,128)(2,1)S(1)}, u32[]{:S(2)}, u32[]{:S(2)}) collective-permute-start(bf16[64,2,1024]{2,0,1:T(8,128)(2,1)S(1)} %get-tuple-element.577), channel_id=1, source_target_pairs={{252,0},{0,4},{4,8},{8,12},{12,16},{16,20},{20,24},{24,28},{28,32}... | collective-permute-start | bytes 786440 | tf_op jit(solution)/shard_map/while/body/eval_jaxpr/ppermute | solution.py:25
  509.5 14.0 %collective-permute-start = (bf16[64,2,1024]{2,0,1:T(8,128)(2,1)S(1)}, bf16[64,2,1024]{2,0,1:T(8,128)(2,1)S(1)}, u32[]{:S(2)}, u32[]{:S(2)}) collective-permute-start(bf16[64,2,1024]{2,0,1:T(8,128)(2,1)S(1)} %get-tuple-element.577), channel_id=1, source_target_pairs={{252,0},{0,4},{4,8},{8,12},{12,16},{16,20},{20,24},{24,28},{28,32}... | collective-permute-start | bytes 786440 | tf_op jit(solution)/shard_map/while/body/eval_jaxpr/ppermute | solution.py:25
  544.6 14.1 %collective-permute-start = (bf16[64,2,1024]{2,0,1:T(8,128)(2,1)S(1)}, bf16[64,2,1024]{2,0,1:T(8,128)(2,1)S(1)}, u32[]{:S(2)}, u32[]{:S(2)}) collective-permute-start(bf16[64,2,1024]{2,0,1:T(8,128)(2,1)S(1)} %get-tuple-element.577), channel_id=1, source_target_pairs={{252,0},{0,4},{4,8},{8,12},{12,16},{16,20},{20,24},{24,28},{28,32}... | collective-permute-start | bytes 786440 | tf_op jit(solution)/shard_map/while/body/eval_jaxpr/ppermute | solution.py:25
  562.3 14.0 %collective-permute-start = (bf16[64,2,1024]{2,0,1:T(8,128)(2,1)S(1)}, bf16[64,2,1024]{2,0,1:T(8,128)(2,1)S(1)}, u32[]{:S(2)}, u32[]{:S(2)}) collective-permute-start(bf16[64,2,1024]{2,0,1:T(8,128)(2,1)S(1)} %get-tuple-element.577), channel_id=1, source_target_pairs={{252,0},{0,4},{4,8},{8,12},{12,16},{16,20},{20,24},{24,28},{28,32}... | collective-permute-start | bytes 786440 | tf_op jit(solution)/shard_map/while/body/eval_jaxpr/ppermute | solution.py:25
  579.9 14.0 %collective-permute-start = (bf16[64,2,1024]{2,0,1:T(8,128)(2,1)S(1)}, bf16[64,2,1024]{2,0,1:T(8,128)(2,1)S(1)}, u32[]{:S(2)}, u32[]{:S(2)}) collective-permute-start(bf16[64,2,1024]{2,0,1:T(8,128)(2,1)S(1)} %get-tuple-element.577), channel_id=1, source_target_pairs={{252,0},{0,4},{4,8},{8,12},{12,16},{16,20},{20,24},{24,28},{28,32}... | collective-permute-start | bytes 786440 | tf_op jit(solution)/shard_map/while/body/eval_jaxpr/ppermute | solution.py:25
  597.6 14.0 %collective-permute-start = (bf16[64,2,1024]{2,0,1:T(8,128)(2,1)S(1)}, bf16[64,2,1024]{2,0,1:T(8,128)(2,1)S(1)}, u32[]{:S(2)}, u32[]{:S(2)}) collective-permute-start(bf16[64,2,1024]{2,0,1:T(8,128)(2,1)S(1)} %get-tuple-element.577), channel_id=1, source_target_pairs={{252,0},{0,4},{4,8},{8,12},{12,16},{16,20},{20,24},{24,28},{28,32}... | collective-permute-start | bytes 786440 | tf_op jit(solution)/shard_map/while/body/eval_jaxpr/ppermute | solution.py:25
  615.2 14.0 %collective-permute-start = (bf16[64,2,1024]{2,0,1:T(8,128)(2,1)S(1)}, bf16[64,2,1024]{2,0,1:T(8,128)(2,1)S(1)}, u32[]{:S(2)}, u32[]{:S(2)}) collective-permute-start(bf16[64,2,1024]{2,0,1:T(8,128)(2,1)S(1)} %get-tuple-element.577), channel_id=1, source_target_pairs={{252,0},{0,4},{4,8},{8,12},{12,16},{16,20},{20,24},{24,28},{28,32}... | collective-permute-start | bytes 786440 | tf_op jit(solution)/shard_map/while/body/eval_jaxpr/ppermute | solution.py:25
  650.3 14.0 %collective-permute-start = (bf16[64,2,1024]{2,0,1:T(8,128)(2,1)S(1)}, bf16[64,2,1024]{2,0,1:T(8,128)(2,1)S(1)}, u32[]{:S(2)}, u32[]{:S(2)}) collective-permute-start(bf16[64,2,1024]{2,0,1:T(8,128)(2,1)S(1)} %get-tuple-element.577), channel_id=1, source_target_pairs={{252,0},{0,4},{4,8},{8,12},{12,16},{16,20},{20,24},{24,28},{28,32}... | collective-permute-start | bytes 786440 | tf_op jit(solution)/shard_map/while/body/eval_jaxpr/ppermute | solution.py:25
  668.0 14.1 %collective-permute-start = (bf16[64,2,1024]{2,0,1:T(8,128)(2,1)S(1)}, bf16[64,2,1024]{2,0,1:T(8,128)(2,1)S(1)}, u32[]{:S(2)}, u32[]{:S(2)}) collective-permute-start(bf16[64,2,1024]{2,0,1:T(8,128)(2,1)S(1)} %get-tuple-element.577), channel_id=1, source_target_pairs={{252,0},{0,4},{4,8},{8,12},{12,16},{16,20},{20,24},{24,28},{28,32}... | collective-permute-start | bytes 786440 | tf_op jit(solution)/shard_map/while/body/eval_jaxpr/ppermute | solution.py:25
  720.7 14.1 %collective-permute-start = (bf16[64,2,1024]{2,0,1:T(8,128)(2,1)S(1)}, bf16[64,2,1024]{2,0,1:T(8,128)(2,1)S(1)}, u32[]{:S(2)}, u32[]{:S(2)}) collective-permute-start(bf16[64,2,1024]{2,0,1:T(8,128)(2,1)S(1)} %get-tuple-element.577), channel_id=1, source_target_pairs={{252,0},{0,4},{4,8},{8,12},{12,16},{16,20},{20,24},{24,28},{28,32}... | collective-permute-start | bytes 786440 | tf_op jit(solution)/shard_map/while/body/eval_jaxpr/ppermute | solution.py:25
  738.4 14.0 %collective-permute-start = (bf16[64,2,1024]{2,0,1:T(8,128)(2,1)S(1)}, bf16[64,2,1024]{2,0,1:T(8,128)(2,1)S(1)}, u32[]{:S(2)}, u32[]{:S(2)}) collective-permute-start(bf16[64,2,1024]{2,0,1:T(8,128)(2,1)S(1)} %get-tuple-element.577), channel_id=1, source_target_pairs={{252,0},{0,4},{4,8},{8,12},{12,16},{16,20},{20,24},{24,28},{28,32}... | collective-permute-start | bytes 786440 | tf_op jit(solution)/shard_map/while/body/eval_jaxpr/ppermute | solution.py:25
  756.1 14.0 %collective-permute-start = (bf16[64,2,1024]{2,0,1:T(8,128)(2,1)S(1)}, bf16[64,2,1024]{2,0,1:T(8,128)(2,1)S(1)}, u32[]{:S(2)}, u32[]{:S(2)}) collective-permute-start(bf16[64,2,1024]{2,0,1:T(8,128)(2,1)S(1)} %get-tuple-element.577), channel_id=1, source_target_pairs={{252,0},{0,4},{4,8},{8,12},{12,16},{16,20},{20,24},{24,28},{28,32}... | collective-permute-start | bytes 786440 | tf_op jit(solution)/shard_map/while/body/eval_jaxpr/ppermute | solution.py:25
  791.3 14.0 %collective-permute-start = (bf16[64,2,1024]{2,0,1:T(8,128)(2,1)S(1)}, bf16[64,2,1024]{2,0,1:T(8,128)(2,1)S(1)}, u32[]{:S(2)}, u32[]{:S(2)}) collective-permute-start(bf16[64,2,1024]{2,0,1:T(8,128)(2,1)S(1)} %get-tuple-element.577), channel_id=1, source_target_pairs={{252,0},{0,4},{4,8},{8,12},{12,16},{16,20},{20,24},{24,28},{28,32}... | collective-permute-start | bytes 786440 | tf_op jit(solution)/shard_map/while/body/eval_jaxpr/ppermute | solution.py:25
  808.9 14.0 %collective-permute-start = (bf16[64,2,1024]{2,0,1:T(8,128)(2,1)S(1)}, bf16[64,2,1024]{2,0,1:T(8,128)(2,1)S(1)}, u32[]{:S(2)}, u32[]{:S(2)}) collective-permute-start(bf16[64,2,1024]{2,0,1:T(8,128)(2,1)S(1)} %get-tuple-element.577), channel_id=1, source_target_pairs={{252,0},{0,4},{4,8},{8,12},{12,16},{16,20},{20,24},{24,28},{28,32}... | collective-permute-start | bytes 786440 | tf_op jit(solution)/shard_map/while/body/eval_jaxpr/ppermute | solution.py:25
  844.2 14.0 %collective-permute-start = (bf16[64,2,1024]{2,0,1:T(8,128)(2,1)S(1)}, bf16[64,2,1024]{2,0,1:T(8,128)(2,1)S(1)}, u32[]{:S(2)}, u32[]{:S(2)}) collective-permute-start(bf16[64,2,1024]{2,0,1:T(8,128)(2,1)S(1)} %get-tuple-element.577), channel_id=1, source_target_pairs={{252,0},{0,4},{4,8},{8,12},{12,16},{16,20},{20,24},{24,28},{28,32}... | collective-permute-start | bytes 786440 | tf_op jit(solution)/shard_map/while/body/eval_jaxpr/ppermute | solution.py:25
  861.8 14.0 %collective-permute-start = (bf16[64,2,1024]{2,0,1:T(8,128)(2,1)S(1)}, bf16[64,2,1024]{2,0,1:T(8,128)(2,1)S(1)}, u32[]{:S(2)}, u32[]{:S(2)}) collective-permute-start(bf16[64,2,1024]{2,0,1:T(8,128)(2,1)S(1)} %get-tuple-element.577), channel_id=1, source_target_pairs={{252,0},{0,4},{4,8},{8,12},{12,16},{16,20},{20,24},{24,28},{28,32}... | collective-permute-start | bytes 786440 | tf_op jit(solution)/shard_map/while/body/eval_jaxpr/ppermute | solution.py:25
  896.9 14.0 %collective-permute-start = (bf16[64,2,1024]{2,0,1:T(8,128)(2,1)S(1)}, bf16[64,2,1024]{2,0,1:T(8,128)(2,1)S(1)}, u32[]{:S(2)}, u32[]{:S(2)}) collective-permute-start(bf16[64,2,1024]{2,0,1:T(8,128)(2,1)S(1)} %get-tuple-element.577), channel_id=1, source_target_pairs={{252,0},{0,4},{4,8},{8,12},{12,16},{16,20},{20,24},{24,28},{28,32}... | collective-permute-start | bytes 786440 | tf_op jit(solution)/shard_map/while/body/eval_jaxpr/ppermute | solution.py:25
  932.1 14.1 %collective-permute-start = (bf16[64,2,1024]{2,0,1:T(8,128)(2,1)S(1)}, bf16[64,2,1024]{2,0,1:T(8,128)(2,1)S(1)}, u32[]{:S(2)}, u32[]{:S(2)}) collective-permute-start(bf16[64,2,1024]{2,0,1:T(8,128)(2,1)S(1)} %get-tuple-element.577), channel_id=1, source_target_pairs={{252,0},{0,4},{4,8},{8,12},{12,16},{16,20},{20,24},{24,28},{28,32}... | collective-permute-start | bytes 786440 | tf_op jit(solution)/shard_map/while/body/eval_jaxpr/ppermute | solution.py:25
  949.8 14.0 %collective-permute-start = (bf16[64,2,1024]{2,0,1:T(8,128)(2,1)S(1)}, bf16[64,2,1024]{2,0,1:T(8,128)(2,1)S(1)}, u32[]{:S(2)}, u32[]{:S(2)}) collective-permute-start(bf16[64,2,1024]{2,0,1:T(8,128)(2,1)S(1)} %get-tuple-element.577), channel_id=1, source_target_pairs={{252,0},{0,4},{4,8},{8,12},{12,16},{16,20},{20,24},{24,28},{28,32}... | collective-permute-start | bytes 786440 | tf_op jit(solution)/shard_map/while/body/eval_jaxpr/ppermute | solution.py:25
  985.0 14.0 %collective-permute-start = (bf16[64,2,1024]{2,0,1:T(8,128)(2,1)S(1)}, bf16[64,2,1024]{2,0,1:T(8,128)(2,1)S(1)}, u32[]{:S(2)}, u32[]{:S(2)}) collective-permute-start(bf16[64,2,1024]{2,0,1:T(8,128)(2,1)S(1)} %get-tuple-element.577), channel_id=1, source_target_pairs={{252,0},{0,4},{4,8},{8,12},{12,16},{16,20},{20,24},{24,28},{28,32}... | collective-permute-start | bytes 786440 | tf_op jit(solution)/shard_map/while/body/eval_jaxpr/ppermute | solution.py:25
  1002.6 14.1 %collective-permute-start = (bf16[64,2,1024]{2,0,1:T(8,128)(2,1)S(1)}, bf16[64,2,1024]{2,0,1:T(8,128)(2,1)S(1)}, u32[]{:S(2)}, u32[]{:S(2)}) collective-permute-start(bf16[64,2,1024]{2,0,1:T(8,128)(2,1)S(1)} %get-tuple-element.577), channel_id=1, source_target_pairs={{252,0},{0,4},{4,8},{8,12},{12,16},{16,20},{20,24},{24,28},{28,32}... | collective-permute-start | bytes 786440 | tf_op jit(solution)/shard_map/while/body/eval_jaxpr/ppermute | solution.py:25
  1020.3 14.0 %collective-permute-start = (bf16[64,2,1024]{2,0,1:T(8,128)(2,1)S(1)}, bf16[64,2,1024]{2,0,1:T(8,128)(2,1)S(1)}, u32[]{:S(2)}, u32[]{:S(2)}) collective-permute-start(bf16[64,2,1024]{2,0,1:T(8,128)(2,1)S(1)} %get-tuple-element.577), channel_id=1, source_target_pairs={{252,0},{0,4},{4,8},{8,12},{12,16},{16,20},{20,24},{24,28},{28,32}... | collective-permute-start | bytes 786440 | tf_op jit(solution)/shard_map/while/body/eval_jaxpr/ppermute | solution.py:25
  1055.4 14.1 %collective-permute-start = (bf16[64,2,1024]{2,0,1:T(8,128)(2,1)S(1)}, bf16[64,2,1024]{2,0,1:T(8,128)(2,1)S(1)}, u32[]{:S(2)}, u32[]{:S(2)}) collective-permute-start(bf16[64,2,1024]{2,0,1:T(8,128)(2,1)S(1)} %get-tuple-element.577), channel_id=1, source_target_pairs={{252,0},{0,4},{4,8},{8,12},{12,16},{16,20},{20,24},{24,28},{28,32}... | collective-permute-start | bytes 786440 | tf_op jit(solution)/shard_map/while/body/eval_jaxpr/ppermute | solution.py:25
  1090.7 14.1 %collective-permute-start = (bf16[64,2,1024]{2,0,1:T(8,128)(2,1)S(1)}, bf16[64,2,1024]{2,0,1:T(8,128)(2,1)S(1)}, u32[]{:S(2)}, u32[]{:S(2)}) collective-permute-start(bf16[64,2,1024]{2,0,1:T(8,128)(2,1)S(1)} %get-tuple-element.577), channel_id=1, source_target_pairs={{252,0},{0,4},{4,8},{8,12},{12,16},{16,20},{20,24},{24,28},{28,32}... | collective-permute-start | bytes 786440 | tf_op jit(solution)/shard_map/while/body/eval_jaxpr/ppermute | solution.py:25
  1126.0 14.0 %collective-permute-start = (bf16[64,2,1024]{2,0,1:T(8,128)(2,1)S(1)}, bf16[64,2,1024]{2,0,1:T(8,128)(2,1)S(1)}, u32[]{:S(2)}, u32[]{:S(2)}) collective-permute-start(bf16[64,2,1024]{2,0,1:T(8,128)(2,1)S(1)} %get-tuple-element.577), channel_id=1, source_target_pairs={{252,0},{0,4},{4,8},{8,12},{12,16},{16,20},{20,24},{24,28},{28,32}... | collective-permute-start | bytes 786440 | tf_op jit(solution)/shard_map/while/body/eval_jaxpr/ppermute | solution.py:25
  1143.6 14.0 %collective-permute-start = (bf16[64,2,1024]{2,0,1:T(8,128)(2,1)S(1)}, bf16[64,2,1024]{2,0,1:T(8,128)(2,1)S(1)}, u32[]{:S(2)}, u32[]{:S(2)}) collective-permute-start(bf16[64,2,1024]{2,0,1:T(8,128)(2,1)S(1)} %get-tuple-element.577), channel_id=1, source_target_pairs={{252,0},{0,4},{4,8},{8,12},{12,16},{16,20},{20,24},{24,28},{28,32}... | collective-permute-start | bytes 786440 | tf_op jit(solution)/shard_map/while/body/eval_jaxpr/ppermute | solution.py:25
  1161.2 14.0 %collective-permute-start = (bf16[64,2,1024]{2,0,1:T(8,128)(2,1)S(1)}, bf16[64,2,1024]{2,0,1:T(8,128)(2,1)S(1)}, u32[]{:S(2)}, u32[]{:S(2)}) collective-permute-start(bf16[64,2,1024]{2,0,1:T(8,128)(2,1)S(1)} %get-tuple-element.577), channel_id=1, source_target_pairs={{252,0},{0,4},{4,8},{8,12},{12,16},{16,20},{20,24},{24,28},{28,32}... | collective-permute-start | bytes 786440 | tf_op jit(solution)/shard_map/while/body/eval_jaxpr/ppermute | solution.py:25
  1178.9 14.0 %collective-permute-start = (bf16[64,2,1024]{2,0,1:T(8,128)(2,1)S(1)}, bf16[64,2,1024]{2,0,1:T(8,128)(2,1)S(1)}, u32[]{:S(2)}, u32[]{:S(2)}) collective-permute-start(bf16[64,2,1024]{2,0,1:T(8,128)(2,1)S(1)} %get-tuple-element.577), channel_id=1, source_target_pairs={{252,0},{0,4},{4,8},{8,12},{12,16},{16,20},{20,24},{24,28},{28,32}... | collective-permute-start | bytes 786440 | tf_op jit(solution)/shard_map/while/body/eval_jaxpr/ppermute | solution.py:25
  1214.9 44.1 %collective-permute-start.3 = (bf16[32,2048]{1,0:T(8,128)(2,1)S(1)}, bf16[32,2048]{1,0:T(8,128)(2,1)S(1)}, u32[]{:S(2)}, u32[]{:S(2)}) collective-permute-start(bf16[32,2048]{1,0:T(8,128)(2,1)S(1)} %get-tuple-element.450), channel_id=1, source_target_pairs={{0,16},{4,20},{8,24},{12,28},{16,32},{20,36},{24,40},{28,44},{32,4... | collective-permute-start | bytes 393224 | tf_op jit(solution)/shard_map/ppermute | solution.py:19
  (41 other events, 1621.8 us)
where the time goes:
time: 1270 us
  waiting for transfers between devices  878 us (69%)
  local copies, waits for them, and re-layouts  213 us (17%)
  starting transfers between devices  77.8 us (6%)
  other arithmetic  34.9 us (3%)
  matrix products  33.6 us (3%)
  blocking collectives  21.5 us (2%)
    ppermute x63, waiting for transfers between devices, shifted(): return lax.ppermute(block, axis, route)  828 us
    scatter x64, local copies, waits for them, and re-layouts, attend(): cache = cache.at[target].set(piece, mode='drop')  165 us
    ppermute x10, waiting for transfers between devices, from_behind(): return lax.ppermute(array, axis, pairs)  50.2 us
    ppermute x63, starting transfers between devices, shifted(): return lax.ppermute(block, axis, route)  46.3 us
    ppermute x10, starting transfers between devices, from_behind(): return lax.ppermute(array, axis, pairs)  31.5 us
  transfers between devices with their start and end apart: 73, of which 66 were waited for; matrix products, arithmetic and copies ran while one was open for 21% of the time, Pallas kernels for 0%

commit v1 on v0

v1 whole, which is shorter than its diff:
```python
import functools
import math

import jax
import jax.numpy as jnp
from jax import lax
from jax.experimental import pallas as pl
from jax.experimental.pallas import tpu as pltpu
from jax.sharding import Mesh, PartitionSpec as P

HEAD_DIM = 128
CAP = 4
EPS_NORM = 1e-06
MASKED = -1e30
CTX = ("x", "y", "zh", "c")
F32 = jnp.float32
BF16 = jnp.bfloat16
LANES = 128
TILE = 32
TAPS = 7
PAIRS = tuple((a, b) for a in range(TAPS + 1) for b in range(a, TAPS + 1))


def ctx_route(array, target):
    pairs = [(i, target(i)) for i in range(64) if 0 <= target(i) < 64]
    return lax.ppermute(array, CTX, pairs)


def call(kernel, out_shape, scratch=(), in_spaces=None, flops=0, nbytes=0, name=None):
    specs = [pl.BlockSpec(memory_space=space) for space in in_spaces]
    if isinstance(out_shape, (list, tuple)):
        outs = [pl.BlockSpec(memory_space=pltpu.VMEM) for _ in out_shape]
    else:
        outs = pl.BlockSpec(memory_space=pltpu.VMEM)
    return pl.pallas_call(
        kernel,
        out_shape=out_shape,
        in_specs=specs,
        out_specs=outs,
        scratch_shapes=list(scratch),
        compiler_params=pltpu.CompilerParams(vmem_limit_bytes=40 * 1024 * 1024),
        cost_estimate=pl.CostEstimate(flops=flops, bytes_accessed=nbytes, transcendentals=0),
        name=name,
    )


V, S = pltpu.VMEM, pltpu.SMEM


def lanes_at(index, width):
    return pl.ds(pl.multiple_of(index * width, width), width)


def halo_products(meta, stream, pre, he, hl, cs):
    last = meta[0] == 63
    s = stream[:, cs].astype(F32)
    u = s * pre[:, cs].astype(F32)
    early = he[:, cs].astype(F32)
    late = hl[:, cs].astype(F32)
    early_u = early[0:8] * early[8:16]
    late_s = jnp.where(last, s[TILE - 8 : TILE], late[0:8])
    late_u = jnp.where(last, u[TILE - 8 : TILE], late[0:8] * late[8:16])
    return s, u, early[0:8], early_u, late_s, late_u


def stats_kernel(meta, stream, pre, post, taps, he, hl, out, us, sf, pf):
    def prepare(step, carry):
        acc_e, acc_l = carry
        cs = lanes_at(step, LANES)
        s, u, es, eu, ls, lu = halo_products(meta, stream, pre, he, hl, cs)
        sf[:, cs] = s
        pf[:, cs] = post[:, cs].astype(F32)
        us[0, 0:8, cs] = eu
        us[0, 8:40, cs] = u[0:TILE]
        us[1, 0:8, cs] = lu
        us[1, 8:40, cs] = u[TILE:]
        return acc_e + es * es, acc_l + ls * ls

    chunks = stream.shape[1] // LANES
    zero = jnp.zeros((8, LANES), F32)
    acc_e, acc_l = lax.fori_loop(0, chunks, prepare, (zero, zero))
    lane = lax.broadcasted_iota(jnp.int32, (8, LANES), 1)
    out[64:72, :] = jnp.where(lane == 0, jnp.sum(acc_e, axis=1, keepdims=True), 0.0)
    out[72:80, :] = jnp.where(lane == 0, jnp.sum(acc_l, axis=1, keepdims=True), 0.0)
    for tile in range(2):
        for group in range(TILE // 8):
            row = tile * TILE + group * 8

            def collect(step, sums, tile=tile, group=group, row=row):
                cs = lanes_at(step, LANES)
                gate = pf[row : row + 8, cs]
                terms = [sf[row : row + 8, cs]]
                for j in range(TAPS):
                    behind = us[tile, pl.ds(group * 8 + 8 - j, 8), cs]
                    terms.append(taps[j : j + 1, cs] * gate * behind)
                return tuple(t + terms[a] * terms[b] for t, (a, b) in zip(sums, PAIRS))

            sums = lax.fori_loop(0, chunks, collect, (zero,) * len(PAIRS))
            packed = zero
            for q, part in enumerate(sums):
                packed = jnp.where(lane == q, jnp.sum(part, axis=1, keepdims=True), packed)
            out[row : row + 8, :] = packed


def mix_kernel(meta, stream, pre, post, taps, he, hl, total, mrpre, mixed, early, late, sc, s2, xs):
    width = 1.0 / 8192.0
    scale = lax.rsqrt(total[:, 0:1] * width + EPS_NORM)
    wide = jnp.broadcast_to(scale, (80, LANES))
    sc[0, 0:8, :] = wide[64:72]
    sc[0, 8:40, :] = wide[0:TILE]
    sc[1, 0:8, :] = wide[72:80]
    sc[1, 8:40, :] = wide[TILE:64]
    lane = lax.broadcasted_iota(jnp.int32, (TILE, LANES), 1)
    for tile in range(2):
        factor = [jnp.ones((TILE, LANES), F32)]
        for j in range(TAPS):
            factor.append(sc[tile, pl.ds(8 - j, TILE), :])
        weight = jnp.zeros((TILE, LANES), F32)
        for q, (a, b) in enumerate(PAIRS):
            term = factor[a] * factor[b]
            weight = jnp.where(lane == q, term if a == b else term * 2.0, weight)
        rows = slice(tile * TILE, (tile + 1) * TILE)
        squares = jnp.sum(weight * total[rows, :], axis=1, keepdims=True)
        second = lax.rsqrt(jnp.maximum(squares, 0.0) * width + EPS_NORM)
        s2[rows, :] = jnp.broadcast_to(second, (TILE, LANES))

    def one(step, carry):
        cs = lanes_at(step, LANES)
        s, u, _, eu, _, lu = halo_products(meta, stream, pre, he, hl, cs)
        gate = post[:, cs].astype(F32)
        front = mrpre[:, cs].astype(F32)
        for tile, halo in enumerate((eu, lu)):
            rows = slice(tile * TILE, (tile + 1) * TILE)
            xs[tile, 0:8, :] = (halo * sc[tile, 0:8, :]).astype(BF16).astype(F32)
            xs[tile, 8:40, :] = (u[rows] * sc[tile, 8:40, :]).astype(BF16).astype(F32)
        for tile, target in enumerate((early, late)):
            rows = slice(tile * TILE, (tile + 1) * TILE)
            acc = jnp.zeros((TILE, LANES), F32)
            for j in range(TAPS):
                acc = acc + taps[j : j + 1, cs] * xs[tile, pl.ds(8 - j, TILE), :]
            value = (s[rows] + gate[rows] * acc).astype(BF16)
            mixed[rows, cs] = value
            target[:, cs] = (front[rows] * value.astype(F32) * s2[rows, :]).astype(BF16)
        return carry

    lax.fori_loop(0, stream.shape[1] // LANES, one, 0)


def conv_kernel(meta, taps, mixed, post, early, late, e2, e4, l2, l4, swapped, out, state, ext):
    first = meta[0] == 0
    ext[0, 0:32, :] = e4[...]
    ext[0, 32:64, :] = swapped[1]
    ext[0, 64:96, :] = e2[...]
    ext[0, 96:128, :] = swapped[0]
    ext[0, 128:160, :] = early[...]
    ext[1, 0:32, :] = l4[...]
    ext[1, 32:64, :] = swapped[3]
    ext[1, 64:96, :] = l2[...]
    ext[1, 96:128, :] = swapped[2]
    ext[1, 128:160, :] = late[...]
    group_width = out.shape[1] // taps.shape[0]
    for g in range(taps.shape[0]):
        row = jnp.broadcast_to(taps[g : g + 1, :], (TILE, 256))
        toeplitz = pltpu.roll(row, 0, 1, stride=1, stride_axis=0)[:, 0:160].astype(BF16)
        cols = slice(g * group_width, (g + 1) * group_width)
        for tile in range(2):
            rows = slice(tile * TILE, (tile + 1) * TILE)
            acc = jnp.dot(toeplitz, ext[tile, :, cols], preferred_element_type=F32)
            value = mixed[rows, cols].astype(F32) + post[rows, cols].astype(F32) * acc
            out[rows, cols] = value.astype(BF16)

    @pl.when(first)
    def _():
        state[...] = ext[1, 32:160, :]

    @pl.when(jnp.logical_not(first))
    def _():
        state[...] = jnp.zeros_like(state)


def pack_kernel(meta, k, v, kz, vz, q, out):
    half = meta[2]
    for a in range(8):
        cols = slice(a * LANES, (a + 1) * LANES)
        xa, y = a // 4, a % 4
        queries = (q[0:TILE, cols], q[TILE : 2 * TILE, cols])
        for xb in range(2):
            n = (xa * 2 + xb) * 4 + y
            out[n, 0:64, :] = k[:, cols]
            out[n, 64:128, :] = v[:, cols]
            out[n, 128:192, :] = kz[:, cols]
            out[n, 192:256, :] = vz[:, cols]
            for t in range(2):
                out[n, 256 + 16 * t : 272 + 16 * t, :] = queries[t][16 * xb : 16 * xb + 16]


def attend_kernel(meta, slots, mine, twin, out, scores):
    xb, zh, c = meta[2], meta[4], meta[5]
    log_scale = math.log2(math.e) / math.sqrt(HEAD_DIM)
    refs = (mine, twin)
    groups = []
    for which in range(2):
        for other in range(2):
            zg = zh if other == 0 else 1 - zh
            cg = c if which == 0 else 1 - c
            groups.append((refs[which], other * 128, zg, cg))

    def place(src, zg, cg, late, u):
        device = src * 4 + zg * 2 + cg
        return (127 - device if late else device) * TILE + u

    def columns(late):
        col = lax.broadcasted_iota(jnp.int32, (1, 512), 1)
        return [place(col // TILE, zg, cg, late, col % TILE) for _, _, zg, cg in groups]

    def tiles(ref, low, count):
        return ref[:, low : low + count, :].reshape(16 * count, LANES)

    block = 128
    places = (columns(False), columns(True))
    for late in range(2):
        for part in range(256 // block):
            src0 = part * (block // 16)
            query = mine[src0 : src0 + block // 16, 256 + 16 * late : 272 + 16 * late, :]
            query = query.reshape(block, LANES)
            row = lax.broadcasted_iota(jnp.int32, (block, 1), 0)
            spot = place(src0 + row // 16, zh, c, bool(late), xb * 16 + row % 16)
            top = jnp.full((block, LANES), MASKED, F32)
            jobs = []
            for key_late in range(late + 1):
                for g, (ref, low, _, _) in enumerate(groups):
                    jobs.append((len(jobs), key_late, g, ref, low + TILE * key_late))
            for n, key_late, g, ref, low in jobs:
                keys = tiles(ref, low, TILE)
                found = lax.dot_general(
                    query, keys, (((1,), (1,)), ((), ())), preferred_element_type=F32
                )
                if key_late == late:
                    found = jnp.where(places[key_late][g] <= spot, found, MASKED)
                scores[:, n * 512 : (n + 1) * 512] = found
                for k in range(4):
                    top = jnp.maximum(top, found[:, k * LANES : (k + 1) * LANES])
            top = jnp.max(top, axis=1, keepdims=True)
            total = jnp.zeros((block, LANES), F32)
            summed = jnp.zeros((block, LANES), F32)
            for n, key_late, g, ref, low in jobs:
                weights = jnp.exp2((scores[:, n * 512 : (n + 1) * 512] - top) * log_scale)
                for k in range(4):
                    total = total + weights[:, k * LANES : (k + 1) * LANES]
                values = tiles(ref, low + 64, TILE)
                summed = summed + jnp.dot(
                    weights.astype(BF16), values, preferred_element_type=F32
                )
            result = (summed / jnp.sum(total, axis=1, keepdims=True)).astype(BF16)
            out[src0 : src0 + block // 16, 16 * late : 16 * late + 16, :] = result.reshape(
                block // 16, 16, LANES
            )

    def cache(n, carry):
        for slot in range(2):
            tile = slots[n * 2 + slot]
            held = jnp.maximum(tile, 0)
            late = (held >= 64).astype(jnp.int32)
            device = jnp.where(held >= 64, 127 - held, held)
            src = device // 4
            zd, cd = (device // 2) % 2, device % 2
            low = pl.multiple_of(jnp.where(zd == zh, 0, 128) + late * TILE, TILE)
            there = jnp.where(tile >= 0, 1, 0)
            near = jnp.where(cd == c, 1, 0)
            for kv in range(2):
                a = mine[src, pl.ds(pl.multiple_of(low + 64 * kv, TILE), TILE), :]
                b = twin[src, pl.ds(pl.multiple_of(low + 64 * kv, TILE), TILE), :]
                value = jnp.where(near == 1, a, b)
                value = jnp.where(there == 1, value, jnp.zeros_like(value))
                first = 32 + (slot * 2 + kv) * TILE
                out[n, first : first + TILE, :] = value
        return carry

    lax.fori_loop(0, 16, cache, 0)


def unpack_kernel(came, att, keys, values):
    for n in range(16):
        xa, xb, y = n // 8, (n // 4) % 2, n % 4
        a = xa * 4 + y
        cols = slice(a * LANES, (a + 1) * LANES)
        att[16 * xb : 16 * xb + 16, cols] = came[n, 0:16, :]
        att[TILE + 16 * xb : TILE + 16 * xb + 16, cols] = came[n, 16:32, :]
        for slot in range(2):
            rows = slice((xb * 2 + slot) * TILE, (xb * 2 + slot + 1) * TILE)
            low = 32 + slot * 2 * TILE
            keys[rows, cols] = came[n, low : low + TILE, :]
            values[rows, cols] = came[n, low + TILE : low + 2 * TILE, :]


def shape(dims, dtype=BF16):
    return jax.ShapeDtypeStruct(dims, dtype)


def body(stream, se_pre, se_post, se_taps, mr_pre, mr_post, mr_taps, query, key, value, owner):
    x, y, zh, c = (lax.axis_index(name) for name in CTX)
    me = ((x * 4 + y) * 2 + zh) * 2 + c
    meta = jnp.stack([me, x // 2, x % 2, y, zh, c, c, c]).astype(jnp.int32)
    rows, channels = stream.shape

    early_raw = jnp.concatenate([stream[24:32], se_pre[24:32]], axis=0)
    late_raw = jnp.concatenate([stream[56:64], se_pre[56:64]], axis=0)
    halo_early = ctx_route(early_raw, lambda i: i + 1)
    halo_late = ctx_route(late_raw, lambda i: i - 1)
    key_z = lax.ppermute(key, "zh", [(0, 1), (1, 0)])
    value_z = lax.ppermute(value, "zh", [(0, 1), (1, 0)])

    taps = jnp.pad(se_taps.T.astype(F32), ((0, 1), (0, 0)))
    sums = call(
        stats_kernel,
        shape((80, LANES), F32),
        [pltpu.VMEM((2, 40, channels), F32), pltpu.VMEM((rows, channels), F32), pltpu.VMEM((rows, channels), F32)],
        [S, V, V, V, V, V, V],
        flops=20_000_000,
        nbytes=900_000,
        name="stats",
    )(meta, stream, se_pre, se_post, taps, halo_early, halo_late)
    total = lax.psum(sums, "tp")
    mixed, early, late = call(
        mix_kernel,
        [shape((rows, channels)), shape((TILE, channels)), shape((TILE, channels))],
        [pltpu.VMEM((2, 40, LANES), F32), pltpu.VMEM((64, LANES), F32), pltpu.VMEM((2, 40, LANES), F32)],
        [S, V, V, V, V, V, V, V, V],
        flops=8_000_000,
        nbytes=1_500_000,
        name="mix",
    )(meta, stream, se_pre, se_post, taps, halo_early, halo_late, total, mr_pre)

    e2 = ctx_route(early, lambda i: i + 2)
    l2 = ctx_route(late, lambda i: i - 2)
    e4 = ctx_route(early, lambda i: i + 4)
    l4 = ctx_route(late, lambda i: i - 4)
    turn2 = ctx_route(early, lambda i: 125 - i if i > 61 else -1)
    turn4 = ctx_route(early, lambda i: 123 - i if i > 59 else -1)
    l2 = jnp.where(me >= 62, turn2, l2)
    l4 = jnp.where(me >= 60, turn4, l4)
    even = c == 0
    swap = jnp.stack(
        [
            jnp.where(even, early, e2),
            jnp.where(even, e2, e4),
            jnp.where(even, l2, late),
            jnp.where(even, l4, l2),
        ]
    )
    swapped = lax.ppermute(swap, "c", [(0, 1), (1, 0)])

    packed = call(pack_kernel, shape((16, 288, LANES)), (), [S] + [V] * 5, nbytes=3_000_000, name="pack")(
        meta, key, value, key_z, value_z, query
    )
    mine = lax.all_to_all(packed, ("x", "y"), 0, 0, tiled=True)
    twin = lax.ppermute(mine, "c", [(0, 1), (1, 0)])

    owners = owner[:, 0]
    tile_ids = jnp.arange(128, dtype=jnp.int32)
    earlier = tile_ids[:, None] > tile_ids[None, :]
    ranks = jnp.sum((earlier & (owners[:, None] == owners[None, :])).astype(jnp.int32), axis=1)
    place_of = owners * CAP + ranks
    want = (jnp.arange(16, dtype=jnp.int32)[:, None] * 4 + zh * 2 + c) * CAP
    want = (want + (x % 2) * 2 + jnp.arange(2, dtype=jnp.int32)[None, :]).reshape(32)
    match = want[:, None] == place_of[None, :]
    slots = jnp.sum(jnp.where(match, tile_ids[None, :] + 1, 0), axis=1) - 1

    answered = call(
        attend_kernel,
        shape((16, 160, LANES)),
        [pltpu.VMEM((128, 4096), F32)],
        [S, S, V, V],
        flops=1_000_000_000,
        nbytes=3_000_000,
        name="attend",
    )(meta, slots.astype(jnp.int32), mine, twin)
    came = lax.all_to_all(answered, ("x", "y"), 0, 0, tiled=True)
    attention_out, cache_keys, cache_values = call(
        unpack_kernel,
        [shape((rows, 1024)), shape((128, 1024)), shape((128, 1024))],
        (),
        [V],
        nbytes=1_300_000,
        name="unpack",
    )(came)
    decode_cache = jnp.stack([cache_keys, cache_values], axis=1)

    reversed_taps = jnp.pad(mr_taps[:, ::-1].astype(F32), ((0, 0), (1, 127)))
    hyena_stream, filter_state = call(
        conv_kernel,
        [shape((rows, channels)), shape((128, channels))],
        [pltpu.VMEM((2, 160, channels), BF16)],
        [S] + [V] * 10,
        flops=100_000_000,
        nbytes=3_000_000,
        name="conv",
    )(meta, reversed_taps, mixed, mr_post, early, late, e2, e4, l2, l4, swapped)
    return hyena_stream, attention_out, decode_cache, filter_state


def solution(mesh):
    fine = Mesh(mesh.devices.reshape(4, 4, 2, 2, 4), (*CTX, "tp"))
    block = P(CTX, "tp")
    in_specs = (block, block, block, P("tp", None), block, block, P("tp", None), block, block, block, P())
    out_specs = (block, block, P(CTX, None, "tp"), block)
    return jax.shard_map(body, mesh=fine, in_specs=in_specs, out_specs=out_specs, check_vma=False)
```

time: 1270 us -> 114 us (0.09)
  the two profiles are of different devices: /device:TPU:8 before, /device:TPU:1 now
where the time goes in v1:
time: 114 us; the launch traced here: 113 us
  starting transfers between devices  63.4 us (56%)
  Pallas kernels  16.6 us (15%)
  blocking collectives  15.1 us (13%)
  waiting for transfers between devices  9.59 us (8%)
  local copies, waits for them, and re-layouts  5.18 us (5%)
  other arithmetic  2.08 us (2%)
    ppermute x8, starting transfers between devices, ctx_route(): return lax.ppermute(array, CTX, pairs)  27 us
    all_to_all x1, starting transfers between devices, body(): came = lax.all_to_all(answered, ('x', 'y'), 0, 0, tiled=True)  17.2 us
    psum x1, blocking collectives, body(): total = lax.psum(sums, 'tp')  15.1 us
    ppermute x1, starting transfers between devices, body(): value_z = lax.ppermute(value, 'zh', [(0, 1), (1, 0)])  7.83 us
    all_to_all x1, waiting for transfers between devices, body(): came = lax.all_to_all(answered, ('x', 'y'), 0, 0, tiled=True)  7.18 us
    all_to_all x1, starting transfers between devices, body(): mine = lax.all_to_all(packed, ('x', 'y'), 0, 0, tiled=True)  6.9 us
    pallas_call x1, Pallas kernels, body(): call(stats_kernel, shape((80, LANES), F32), [pltpu.VMEM((2, 40, channels)...  5.33 us
    pallas_call x1, Pallas kernels, body(): call(attend_kernel, shape((16, 160, LANES)), [pltpu.VMEM((128, 4096), F32...  5.22 us
  transfers between devices with their start and end apart: 14, of which 4 were waited for; matrix products, arithmetic and copies ran while one was open for 3% of the time, Pallas kernels for 9%

profile of v1, /device:TPU:1, one launch (start us, length us, event | category | flops | bytes accessed | tf_op | source)
XLA Modules:
  0.0 113.0 jit_solution(10789441175179928530)
XLA Ops:
  0.6 7.8 %collective-permute-start.10 = (bf16[64,1024]{1,0:T(8,128)(2,1)}, bf16[64,1024]{1,0:T(8,128)(2,1)S(1)}, u32[]{:S(2)}, u32[]{:S(2)}) collective-permute-start(bf16[64,1024]{1,0:T(8,128)(2,1)} %v.1), channel_id=1, source_target_pairs={{0,8},{8,0},{1,9},{9,1},{2,10},{10,2},{3,11},{11,3},{4,12},{12,4},... | collective-permute-start | bytes 393224 | tf_op jit(solution)/shard_map/ppermute | solution.py:311
  8.5 0.1 collective-permute-start.9
  8.6 0.8 fusion.1
  9.4 3.2 %collective-permute-start.1 = (bf16[16,2048]{1,0:T(8,128)(2,1)S(1)}, bf16[16,2048]{1,0:T(8,128)(2,1)S(1)}, u32[]{:S(2)}, u32[]{:S(2)}) collective-permute-start(bf16[16,2048]{1,0:T(8,128)(2,1)S(1)} %pad_maximum_fusion.3), channel_id=1, source_target_pairs={{4,0},{8,4},{12,8},{16,12},{20,16},{24,20},{28,24},{32,28},{36,32}... | collective-permute-start | bytes 196616 | tf_op jit(solution)/shard_map/ppermute | solution.py:26
  12.7 7.0 %collective-permute-start = (bf16[16,2048]{1,0:T(8,128)(2,1)S(1)}, bf16[16,2048]{1,0:T(8,128)(2,1)S(1)}, u32[]{:S(2)}, u32[]{:S(2)}) collective-permute-start(bf16[16,2048]{1,0:T(8,128)(2,1)S(1)} %pad_maximum_fusion.2), channel_id=1, source_target_pairs={{0,4},{4,8},{8,12},{12,16},{16,20},{20,24},{24,28},{28,32},{32,36}... | collective-permute-start | bytes 196616 | tf_op jit(solution)/shard_map/ppermute | solution.py:26
  19.7 0.1 stack.53.meta
  19.8 0.0 collective-permute-done.10.vz
  19.8 0.0 copy-start.5
  19.8 0.9 copy-done.5
  20.7 0.9 copy-done.6
  21.6 0.9 copy-done.7
  22.5 1.7 %pack.1 = bf16[16,288,128]{2,1,0:T(8,128)(2,1)} custom-call(s32[8]{0:T(128)S(1)} %stack.53.meta, bf16[64,1024]{1,0:T(8,128)(2,1)S(1)} %copy-done.5, bf16[64,1024]{1,0:T(8,128)(2,1)S(1)} %copy-done.6, bf16[64,1024]{1,0:T(8,128)(2,1)S(1)} %collective-permute-done.9.kz, bf16[64,1024]{1,0:T(8,128)(2,1)S(1)} %collective-permute-done.10.vz, ...), custom_call_target="tpu_custom_call" | custom-call | bytes 3000000 | tf_op jit(solution)/shard_map/pack/pallas_call | solution.py:353
  24.2 0.0 copy-start.2
  24.3 6.9 %all-to-all-start = ((bf16[16,288,128]{2,1,0:T(8,128)(2,1)}), bf16[16,288,128]{2,1,0:T(8,128)(2,1)S(1)}, u32[]{:S(2)}, u32[]{:S(2)}) async-start(bf16[16,288,128]{2,1,0:T(8,128)(2,1)} %pack.1), calls=%async_computation | async-start | bytes 2359296 | tf_op jit(solution)/shard_map/all_to_all | solution.py:356
  31.2 0.0 copy-start.3
  31.2 0.1 iota_add_fusion
  31.2 0.1 add.106
  31.4 0.2 convert_reduce_fusion
  31.6 0.2 select_reduce_fusion
  31.7 0.0 collective-permute-done.1.hl
  31.8 5.3 %stats.1 = f32[80,128]{1,0:T(8,128)S(1)} custom-call(s32[8]{0:T(128)S(1)} %stack.53.meta, bf16[64,2048]{1,0:T(8,128)(2,1)S(1)} %copy-done, bf16[64,2048]{1,0:T(8,128)(2,1)S(1)} %copy-done.1, bf16[64,2048]{1,0:T(8,128)(2,1)S(1)} %copy-done.2, f32[8,2048]{1,0:T(8,128)S(1)} %pad_convert_fusion.taps, bf16[16,2048]{1,0:T(8,128)(2,1)S(1)} %collective-permute-done.he, ...), custom_call_target="tpu_custom_call" | custom-call | flops 20000000 | bytes 900000 | tf_op jit(solution)/shard_map/stats/pallas_call | solution.py:314
  37.1 15.1 %psum.7.total = f32[80,128]{1,0:T(8,128)S(1)} all-reduce(f32[80,128]{1,0:T(8,128)S(1)} %stats.1), channel_id=1, replica_groups=mesh['x'=4,'y'=4,'zh'=2,'c'=2,'tp'=4] {'tp'}, use_global_device_ids=true, to_apply=%region_0.1 | all-reduce | flops 10240 | bytes 81920 | tf_op jit(solution)/shard_map/psum | solution.py:323
  52.3 1.6 %mix.1 = (bf16[64,2048]{1,0:T(8,128)(2,1)S(1)}, bf16[32,2048]{1,0:T(8,128)(2,1)S(1)}, bf16[32,2048]{1,0:T(8,128)(2,1)S(1)}) custom-call(s32[8]{0:T(128)S(1)} %stack.53.meta, bf16[64,2048]{1,0:T(8,128)(2,1)S(1)} %copy-done, bf16[64,2048]{1,0:T(8,128)(2,1)S(1)} %copy-done.1, bf16[64,2048]{1,0:T(8,128)(2,1)S(1)} %copy-done.2, ...), custom_call_target="tpu_custom_call" | custom-call | flops 8000000 | bytes 1500000 | tf_op jit(solution)/shard_map/mix/pallas_call | solution.py:324
  53.9 0.7 collective-permute-start.4
  54.6 1.3 %collective-permute-start.5 = (bf16[32,2048]{1,0:T(8,128)(2,1)S(1)}, bf16[32,2048]{1,0:T(8,128)(2,1)S(1)}, u32[]{:S(2)}, u32[]{:S(2)}) collective-permute-start(bf16[32,2048]{1,0:T(8,128)(2,1)S(1)} %get-tuple-element.14.late), channel_id=1, source_target_pairs={{8,0},{12,4},{16,8},{20,12},{24,16},{28,20},{32,24},{36,28},{40,32... | collective-permute-start | bytes 393224 | tf_op jit(solution)/shard_map/ppermute | solution.py:26
  55.9 9.8 %collective-permute-start.2 = (bf16[32,2048]{1,0:T(8,128)(2,1)S(1)}, bf16[32,2048]{1,0:T(8,128)(2,1)S(1)}, u32[]{:S(2)}, u32[]{:S(2)}) collective-permute-start(bf16[32,2048]{1,0:T(8,128)(2,1)S(1)} %get-tuple-element.13.early), channel_id=1, source_target_pairs={{0,8},{4,12},{8,16},{12,20},{16,24},{20,28},{24,32},{28,36},{32,40... | collective-permute-start | bytes 393224 | tf_op jit(solution)/shard_map/ppermute | solution.py:26
  65.7 3.1 %collective-permute-start.3 = (bf16[32,2048]{1,0:T(8,128)(2,1)S(1)}, bf16[32,2048]{1,0:T(8,128)(2,1)S(1)}, u32[]{:S(2)}, u32[]{:S(2)}) collective-permute-start(bf16[32,2048]{1,0:T(8,128)(2,1)S(1)} %get-tuple-element.13.early), channel_id=1, source_target_pairs={{0,16},{4,20},{8,24},{12,28},{16,32},{20,36},{24,40},{28,44},{32,4... | collective-permute-start | bytes 393224 | tf_op jit(solution)/shard_map/ppermute | solution.py:26
  68.8 0.7 collective-permute-start.6
  69.5 0.0 collective-permute-done.4
  69.5 1.3 %collective-permute-start.7 = (bf16[32,2048]{1,0:T(8,128)(2,1)S(1)}, bf16[32,2048]{1,0:T(8,128)(2,1)S(1)}, u32[]{:S(2)}, u32[]{:S(2)}) collective-permute-start(bf16[32,2048]{1,0:T(8,128)(2,1)S(1)} %get-tuple-element.14.late), channel_id=1, source_target_pairs={{16,0},{20,4},{24,8},{28,12},{32,16},{36,20},{40,24},{44,28},{48,3... | collective-permute-start | bytes 393224 | tf_op jit(solution)/shard_map/ppermute | solution.py:26
  70.8 3.6 %collective-permute-start.11 = (bf16[16,288,128]{2,1,0:T(8,128)(2,1)S(1)}, bf16[16,288,128]{2,1,0:T(8,128)(2,1)S(1)}, u32[]{:S(2)}, u32[]{:S(2)}) collective-permute-start(bf16[16,288,128]{2,1,0:T(8,128)(2,1)S(1)} %all-to-all-done.mine), channel_id=1, source_target_pairs={{0,4},{4,0},{1,5},{5,1},{2,6},{6,2},{3,7},{7,3},{8,12},{12,8},{9,1... | collective-permute-start | bytes 3538952 | tf_op jit(solution)/shard_map/ppermute | solution.py:357
  74.5 0.7 collective-permute-done.7
  75.2 0.7 select_bitcast_fusion
  75.9 0.7 select_bitcast_fusion.3
  76.6 0.3 collective-permute-done.11.twin
  76.9 5.2 %attend.1 = bf16[16,160,128]{2,1,0:T(8,128)(2,1)} custom-call(s32[8]{0:T(128)S(1)} %stack.53.meta, s32[32]{0:T(128)S(1)} %broadcast_add_fusion.slots, bf16[16,288,128]{2,1,0:T(8,128)(2,1)S(1)} %all-to-all-done.mine, bf16[16,288,128]{2,1,0:T(8,128)(2,1)S(1)} %collective-permute-done.11.twin), custom_call_target="tpu_custom_call" | custom-call | flops 1000000000 | bytes 3000000 | tf_op jit(solution)/shard_map/attend/pallas_call | solution.py:369
  82.1 0.0 copy-start.4
  82.2 17.2 %all-to-all-start.1 = ((bf16[16,160,128]{2,1,0:T(8,128)(2,1)}), bf16[16,160,128]{2,1,0:T(8,128)(2,1)S(1)}, u32[]{:S(2)}, u32[]{:S(2)}) async-start(bf16[16,160,128]{2,1,0:T(8,128)(2,1)} %attend.1), calls=%async_computation.1 | async-start | bytes 1310720 | tf_op jit(solution)/shard_map/all_to_all | solution.py:378
  99.4 0.1 pad_maximum_fusion
  99.5 0.7 collective-permute-start.8
  100.2 0.1 rev.3
  100.3 0.1 pad_convert_fusion.1.taps
  100.4 1.4 %collective-permute-done.8.swapped = bf16[4,32,2048]{2,1,0:T(8,128)(2,1)S(1)} collective-permute-done((bf16[4,32,2048]{2,1,0:T(8,128)(2,1)S(1)}, bf16[4,32,2048]{2,1,0:T(8,128)(2,1)S(1)}, u32[]{:S(2)}, u32[]{:S(2)}) %collective-permute-start.8) | collective-permute-done | bytes 524320 | tf_op jit(solution)/shard_map/ppermute | solution.py:351
  101.8 1.9 %conv.1 = (bf16[64,2048]{1,0:T(8,128)(2,1)}, bf16[128,2048]{1,0:T(8,128)(2,1)}) custom-call(s32[8]{0:T(128)S(1)} %stack.53.meta, f32[4,256]{1,0:T(4,128)S(1)} %pad_convert_fusion.1.taps, bf16[64,2048]{1,0:T(8,128)(2,1)S(1)} %get-tuple-element.12.mixed, bf16[64,2048]{1,0:T(8,128)(2,1)S(1)} %copy-done.4, bf16[32,2048]{1,0:T(8,128)(2,1)S(1)} %get-tuple-element.13.early, ...), custom_call_target="tpu_custom_call" | custom-call | flops 100000000 | bytes 3000000 | tf_op jit(solution)/shard_map/conv/pallas_call | solution.py:390
  103.6 7.2 %all-to-all-done.1.came = bf16[16,160,128]{2,1,0:T(8,128)(2,1)S(1)} async-done(((bf16[16,160,128]{2,1,0:T(8,128)(2,1)}), bf16[16,160,128]{2,1,0:T(8,128)(2,1)S(1)}, u32[]{:S(2)}, u32[]{:S(2)}) %all-to-all-start.1) | async-done | bytes 655392 | tf_op jit(solution)/shard_map/all_to_all | solution.py:378
  110.8 0.8 unpack.1
  111.6 0.1 pad_maximum_fusion.1
  111.7 1.3 %copy.17 = bf16[128,2,1024]{2,1,0:T(2,128)(2,1)} copy(bf16[128,2,1024]{2,0,1:T(8,128)(2,1)S(1)} %pad_maximum_fusion.1) | data formatting | bytes 1048576
  (35 shorter events, 0.1 us)
Async XLA Ops:
  0.6 19.1 %collective-permute-start.10 = (bf16[64,1024]{1,0:T(8,128)(2,1)}, bf16[64,1024]{1,0:T(8,128)(2,1)S(1)}, u32[]{:S(2)}, u32[]{:S(2)}) collective-permute-start(bf16[64,1024]{1,0:T(8,128)(2,1)} %v.1), channel_id=1, source_target_pairs={{0,8},{8,0},{1,9},{9,1},{2,10},{10,2},{3,11},{11,3},{4,12},{12,4},... | collective-permute-start | bytes 393224 | tf_op jit(solution)/shard_map/ppermute | solution.py:311
  8.5 11.3 %collective-permute-start.9 = (bf16[64,1024]{1,0:T(8,128)(2,1)}, bf16[64,1024]{1,0:T(8,128)(2,1)S(1)}, u32[]{:S(2)}, u32[]{:S(2)}) collective-permute-start(bf16[64,1024]{1,0:T(8,128)(2,1)} %k.1), channel_id=1, source_target_pairs={{0,8},{8,0},{1,9},{9,1},{2,10},{10,2},{3,11},{11,3},{4,12},{12,4},... | collective-permute-start | bytes 393224 | tf_op jit(solution)/shard_map/ppermute | solution.py:310
  9.4 22.4 %collective-permute-start.1 = (bf16[16,2048]{1,0:T(8,128)(2,1)S(1)}, bf16[16,2048]{1,0:T(8,128)(2,1)S(1)}, u32[]{:S(2)}, u32[]{:S(2)}) collective-permute-start(bf16[16,2048]{1,0:T(8,128)(2,1)S(1)} %pad_maximum_fusion.3), channel_id=1, source_target_pairs={{4,0},{8,4},{12,8},{16,12},{20,16},{24,20},{28,24},{32,28},{36,32}... | collective-permute-start | bytes 196616 | tf_op jit(solution)/shard_map/ppermute | solution.py:26
  12.7 19.1 %collective-permute-start = (bf16[16,2048]{1,0:T(8,128)(2,1)S(1)}, bf16[16,2048]{1,0:T(8,128)(2,1)S(1)}, u32[]{:S(2)}, u32[]{:S(2)}) collective-permute-start(bf16[16,2048]{1,0:T(8,128)(2,1)S(1)} %pad_maximum_fusion.2), channel_id=1, source_target_pairs={{0,4},{4,8},{8,12},{12,16},{16,20},{20,24},{24,28},{28,32},{32,36}... | collective-permute-start | bytes 196616 | tf_op jit(solution)/shard_map/ppermute | solution.py:26
  19.8 0.9 copy-start.5
  20.7 0.9 copy-start.6
  21.6 0.9 copy-start.7
  24.2 7.1 %copy-start.13 = (s32[128,1]{0,1:T(1,128)S(1)}, s32[128,1]{0,1:T(1,128)}, u32[]{:S(2)}) copy-start(s32[128,1]{0,1:T(1,128)} %param.21) | copy-start | bytes 1540
  24.2 7.3 %copy-start.11 = (bf16[2048,7]{0,1:T(8,128)(2,1)S(1)}, bf16[2048,7]{0,1:T(8,128)(2,1)}, u32[]{:S(2)}) copy-start(bf16[2048,7]{0,1:T(8,128)(2,1)} %param.14) | copy-start | bytes 86020
  24.2 7.5 %copy-start = (bf16[64,2048]{1,0:T(8,128)(2,1)S(1)}, bf16[64,2048]{1,0:T(8,128)(2,1)}, u32[]{:S(2)}) copy-start(bf16[64,2048]{1,0:T(8,128)(2,1)} %stream.3) | copy-start | bytes 786436
  24.2 7.5 %copy-start.1 = (bf16[64,2048]{1,0:T(8,128)(2,1)S(1)}, bf16[64,2048]{1,0:T(8,128)(2,1)}, u32[]{:S(2)}) copy-start(bf16[64,2048]{1,0:T(8,128)(2,1)} %pre.3) | copy-start | bytes 786436
  24.2 7.5 %copy-start.2 = (bf16[64,2048]{1,0:T(8,128)(2,1)S(1)}, bf16[64,2048]{1,0:T(8,128)(2,1)}, u32[]{:S(2)}) copy-start(bf16[64,2048]{1,0:T(8,128)(2,1)} %post.4) | copy-start | bytes 786436
  24.3 46.5 %all-to-all-start = ((bf16[16,288,128]{2,1,0:T(8,128)(2,1)}), bf16[16,288,128]{2,1,0:T(8,128)(2,1)S(1)}, u32[]{:S(2)}, u32[]{:S(2)}) async-start(bf16[16,288,128]{2,1,0:T(8,128)(2,1)} %pack.1), calls=%async_computation | async-start | bytes 2359296 | tf_op jit(solution)/shard_map/all_to_all | solution.py:356
  31.2 21.1 %copy-start.3 = (bf16[64,2048]{1,0:T(8,128)(2,1)S(1)}, bf16[64,2048]{1,0:T(8,128)(2,1)}, u32[]{:S(2)}) copy-start(bf16[64,2048]{1,0:T(8,128)(2,1)} %mrpre.1) | copy-start | bytes 786436
  53.9 15.6 %collective-permute-start.4 = (bf16[32,2048]{1,0:T(8,128)(2,1)S(1)}, bf16[32,2048]{1,0:T(8,128)(2,1)S(1)}, u32[]{:S(2)}, u32[]{:S(2)}) collective-permute-start(bf16[32,2048]{1,0:T(8,128)(2,1)S(1)} %get-tuple-element.13.early), channel_id=1, source_target_pairs={{248,252},{252,248},{249,253},{253,249},{250,254},{254,250},{251,2... | collective-permute-start | bytes 393224 | tf_op jit(solution)/shard_map/ppermute | solution.py:26
  54.6 16.2 %collective-permute-start.5 = (bf16[32,2048]{1,0:T(8,128)(2,1)S(1)}, bf16[32,2048]{1,0:T(8,128)(2,1)S(1)}, u32[]{:S(2)}, u32[]{:S(2)}) collective-permute-start(bf16[32,2048]{1,0:T(8,128)(2,1)S(1)} %get-tuple-element.14.late), channel_id=1, source_target_pairs={{8,0},{12,4},{16,8},{20,12},{24,16},{28,20},{32,24},{36,28},{40,32... | collective-permute-start | bytes 393224 | tf_op jit(solution)/shard_map/ppermute | solution.py:26
  55.9 20.0 %collective-permute-start.2 = (bf16[32,2048]{1,0:T(8,128)(2,1)S(1)}, bf16[32,2048]{1,0:T(8,128)(2,1)S(1)}, u32[]{:S(2)}, u32[]{:S(2)}) collective-permute-start(bf16[32,2048]{1,0:T(8,128)(2,1)S(1)} %get-tuple-element.13.early), channel_id=1, source_target_pairs={{0,8},{4,12},{8,16},{12,20},{16,24},{20,28},{24,32},{28,36},{32,40... | collective-permute-start | bytes 393224 | tf_op jit(solution)/shard_map/ppermute | solution.py:26
  65.7 10.2 %collective-permute-start.3 = (bf16[32,2048]{1,0:T(8,128)(2,1)S(1)}, bf16[32,2048]{1,0:T(8,128)(2,1)S(1)}, u32[]{:S(2)}, u32[]{:S(2)}) collective-permute-start(bf16[32,2048]{1,0:T(8,128)(2,1)S(1)} %get-tuple-element.13.early), channel_id=1, source_target_pairs={{0,16},{4,20},{8,24},{12,28},{16,32},{20,36},{24,40},{28,44},{32,4... | collective-permute-start | bytes 393224 | tf_op jit(solution)/shard_map/ppermute | solution.py:26
  68.8 5.7 %collective-permute-start.6 = (bf16[32,2048]{1,0:T(8,128)(2,1)S(1)}, bf16[32,2048]{1,0:T(8,128)(2,1)S(1)}, u32[]{:S(2)}, u32[]{:S(2)}) collective-permute-start(bf16[32,2048]{1,0:T(8,128)(2,1)S(1)} %get-tuple-element.13.early), channel_id=1, source_target_pairs={{240,252},{244,248},{248,244},{252,240},{241,253},{245,249},{249,2... | collective-permute-start | bytes 393224 | tf_op jit(solution)/shard_map/ppermute | solution.py:26
  69.5 5.7 %collective-permute-start.7 = (bf16[32,2048]{1,0:T(8,128)(2,1)S(1)}, bf16[32,2048]{1,0:T(8,128)(2,1)S(1)}, u32[]{:S(2)}, u32[]{:S(2)}) collective-permute-start(bf16[32,2048]{1,0:T(8,128)(2,1)S(1)} %get-tuple-element.14.late), channel_id=1, source_target_pairs={{16,0},{20,4},{24,8},{28,12},{32,16},{36,20},{40,24},{44,28},{48,3... | collective-permute-start | bytes 393224 | tf_op jit(solution)/shard_map/ppermute | solution.py:26
  70.8 6.1 %collective-permute-start.11 = (bf16[16,288,128]{2,1,0:T(8,128)(2,1)S(1)}, bf16[16,288,128]{2,1,0:T(8,128)(2,1)S(1)}, u32[]{:S(2)}, u32[]{:S(2)}) collective-permute-start(bf16[16,288,128]{2,1,0:T(8,128)(2,1)S(1)} %all-to-all-done.mine), channel_id=1, source_target_pairs={{0,4},{4,0},{1,5},{5,1},{2,6},{6,2},{3,7},{7,3},{8,12},{12,8},{9,1... | collective-permute-start | bytes 3538952 | tf_op jit(solution)/shard_map/ppermute | solution.py:357
  82.1 17.2 %copy-start.8 = (bf16[1,32,2048]{2,1,0:T(8,128)(2,1)S(1)}, bf16[1,32,2048]{2,1,0:T(8,128)(2,1)}, u32[]{:S(2)}) copy-start(bf16[1,32,2048]{2,1,0:T(8,128)(2,1)} %get-tuple-element.34) | copy-start | bytes 393220
  82.1 17.3 %copy-start.9 = (bf16[1,32,2048]{2,1,0:T(8,128)(2,1)S(1)}, bf16[1,32,2048]{2,1,0:T(8,128)(2,1)}, u32[]{:S(2)}) copy-start(bf16[1,32,2048]{2,1,0:T(8,128)(2,1)} %get-tuple-element.40) | copy-start | bytes 393220
  82.1 17.3 %copy-start.10 = (bf16[1,32,2048]{2,1,0:T(8,128)(2,1)S(1)}, bf16[1,32,2048]{2,1,0:T(8,128)(2,1)}, u32[]{:S(2)}) copy-start(bf16[1,32,2048]{2,1,0:T(8,128)(2,1)} %get-tuple-element.41) | copy-start | bytes 393220
  82.1 18.1 %copy-start.12 = (bf16[4,128]{1,0:T(4,128)(2,1)S(1)}, bf16[4,128]{1,0:T(4,128)(2,1)}, u32[]{:S(2)}) copy-start(bf16[4,128]{1,0:T(4,128)(2,1)} %param.17) | copy-start | bytes 3076
  82.1 19.6 %copy-start.4 = (bf16[64,2048]{1,0:T(8,128)(2,1)S(1)}, bf16[64,2048]{1,0:T(8,128)(2,1)}, u32[]{:S(2)}) copy-start(bf16[64,2048]{1,0:T(8,128)(2,1)} %post.5) | copy-start | bytes 786436
  82.2 28.7 %all-to-all-start.1 = ((bf16[16,160,128]{2,1,0:T(8,128)(2,1)}), bf16[16,160,128]{2,1,0:T(8,128)(2,1)S(1)}, u32[]{:S(2)}, u32[]{:S(2)}) async-start(bf16[16,160,128]{2,1,0:T(8,128)(2,1)} %attend.1), calls=%async_computation.1 | async-start | bytes 1310720 | tf_op jit(solution)/shard_map/all_to_all | solution.py:378
  99.5 2.3 %collective-permute-start.8 = (bf16[4,32,2048]{2,1,0:T(8,128)(2,1)S(1)}, bf16[4,32,2048]{2,1,0:T(8,128)(2,1)S(1)}, u32[]{:S(2)}, u32[]{:S(2)}) collective-permute-start(bf16[4,32,2048]{2,1,0:T(8,128)(2,1)S(1)} %pad_maximum_fusion), channel_id=1, source_target_pairs={{0,4},{4,0},{1,5},{5,1},{2,6},{6,2},{3,7},{7,3},{8,12},{12,8},{9,1... | collective-permute-start | bytes 1572872 | tf_op jit(solution)/shard_map/ppermute | solution.py:351

commit v2 on v1

v2 whole, which is shorter than its diff:
```python
import functools
import math

import jax
import jax.numpy as jnp
from jax import lax
from jax.experimental import pallas as pl
from jax.experimental.pallas import tpu as pltpu
from jax.sharding import Mesh, PartitionSpec as P

HEAD_DIM = 128
CAP = 4
EPS_NORM = 1e-06
MASKED = -1e30
CTX = ("x", "y", "zh", "c")
F32 = jnp.float32
BF16 = jnp.bfloat16
LANES = 128
TILE = 32
TAPS = 7
HALO = 40
PAIRS = tuple((a, b) for a in range(TAPS + 1) for b in range(a, TAPS + 1))


def ctx_route(array, target):
    pairs = [(i, target(i)) for i in range(64) if 0 <= target(i) < 64]
    return lax.ppermute(array, CTX, pairs)


def next_chip(i):
    return 63 if i == 63 else (i + 1 if i % 2 else i - 1)


def across(i):
    return (i + 1 if i % 2 else i - 1) % 64


def second_chip(i):
    return {63: 61, 61: 63}.get(i, i + 3 if i % 2 else i - 3)


SWAP = [(0, 1), (1, 0)]


def call(kernel, out_shape, scratch=(), in_spaces=None, flops=0, nbytes=0, name=None, out_space=pltpu.VMEM, vmem=24):
    specs = [pl.BlockSpec(memory_space=space) for space in in_spaces]
    if isinstance(out_shape, (list, tuple)):
        outs = [pl.BlockSpec(memory_space=pltpu.VMEM) for _ in out_shape]
    else:
        outs = pl.BlockSpec(memory_space=out_space)
    return pl.pallas_call(
        kernel,
        out_shape=out_shape,
        in_specs=specs,
        out_specs=outs,
        scratch_shapes=list(scratch),
        compiler_params=pltpu.CompilerParams(vmem_limit_bytes=vmem * 1024 * 1024),
        cost_estimate=pl.CostEstimate(flops=flops, bytes_accessed=nbytes, transcendentals=0),
        name=name,
    )


V, S = pltpu.VMEM, pltpu.SMEM


def lanes_at(index, width):
    return pl.ds(pl.multiple_of(index * width, width), width)


def halo_rows(meta, far, near, early, step):
    odd = meta[5] == 1
    rows = pl.ds(pl.multiple_of(128 + step // 8 * 16, 16), 16)
    other = far[rows, lanes_at(step % 8, LANES)].astype(F32)
    other = jnp.where(meta[0] == 0, jnp.zeros_like(other), other)
    twin = near[:, lanes_at(step, LANES)].astype(F32)
    before = jnp.where(odd, twin, other)
    after = jnp.where(meta[0] == 63, early, jnp.where(odd, other, twin))
    return before, after


def sum_pairs(out, row, base, tiles, terms_of, packed=None):
    zero = jnp.zeros((8, LANES), F32)
    lane = lax.broadcasted_iota(jnp.int32, (8, LANES), 1)
    packed = zero if packed is None else packed
    for tile in range(tiles):

        def collect(step, sums, tile=tile):
            terms = terms_of(tile, lanes_at(step, LANES))
            return tuple(t + terms[a] * terms[b] for t, (a, b) in zip(sums, PAIRS))

        sums = lax.fori_loop(0, base, collect, (zero,) * len(PAIRS), unroll=4)
        for q, part in enumerate(sums):
            packed = jnp.where(lane == q + 64 * tile, jnp.sum(part, axis=1, keepdims=True), packed)
    out[row : row + 8, :] = packed


def stats_kernel(stream, pre, post, taps, out, us, sf, pf, tf):
    tf[0:TAPS, :] = taps[...].astype(F32)
    chunks = stream.shape[1] // LANES

    def prepare(step, carry):
        cs = lanes_at(step, LANES)
        s = stream[:, cs].astype(F32)
        sf[:, cs] = s
        pf[:, cs] = post[:, cs].astype(F32)
        us[:, cs] = s * pre[:, cs].astype(F32)
        return carry

    lax.fori_loop(0, chunks, prepare, 0, unroll=2)
    out[0:8, :] = jnp.zeros((8, LANES), F32)
    for group in range(1, TILE // 8):

        def terms_of(tile, cs, group=group):
            row = tile * TILE + group * 8
            gate = pf[row : row + 8, cs]
            behind = [us[pl.ds(row - j, 8), cs] for j in range(TAPS)]
            return [sf[row : row + 8, cs]] + [tf[j : j + 1, cs] * gate * behind[j] for j in range(TAPS)]

        sum_pairs(out, group * 8, chunks, 2, terms_of)


def head_kernel(meta, stream, pre, post, taps, far, near, partial, out, us, sf, pf, tf):
    tf[0:TAPS, :] = taps[...].astype(F32)
    chunks = stream.shape[1] // LANES

    def prepare(step, carry):
        cs = lanes_at(step, LANES)
        own = [ref[16:TILE, cs].astype(F32)[8:16] for ref in (stream, pre)]
        halos = halo_rows(meta, far, near, jnp.concatenate(own, axis=0), step)
        squares = []
        for tile in range(2):
            halo = halos[tile]
            rows = slice(tile * TILE, tile * TILE + 16)
            s = stream[rows, cs].astype(F32)[0:8]
            sf[tile, :, cs] = s
            pf[tile, :, cs] = post[rows, cs].astype(F32)[0:8]
            us[tile, 0:8, cs] = halo[0:8] * halo[8:16]
            us[tile, 8:16, cs] = s * pre[rows, cs].astype(F32)[0:8]
            squares.append(carry[tile] + halo[0:8] * halo[0:8])
        return tuple(squares)

    zero = jnp.zeros((8, LANES), F32)
    squares = lax.fori_loop(0, chunks, prepare, (zero, zero), unroll=2)
    lane = lax.broadcasted_iota(jnp.int32, (8, LANES), 1)
    packed = zero
    for tile in range(2):
        packed = jnp.where(lane == HALO + 64 * tile, jnp.sum(squares[tile], axis=1, keepdims=True), packed)

    def terms_of(tile, cs):
        gate = pf[tile, :, cs]
        behind = [us[tile, pl.ds(8 - j, 8), cs] for j in range(TAPS)]
        return [sf[tile, :, cs]] + [tf[j : j + 1, cs] * gate * behind[j] for j in range(TAPS)]

    sum_pairs(out, 0, chunks, 2, terms_of, packed)
    out[8:TILE, :] = partial[8:TILE, :]


def pack_kernel(k, v, far, q, out):
    for a in range(8):
        cols = slice(a * LANES, (a + 1) * LANES)
        for xb in range(2):
            n = ((a // 4) * 2 + xb) * 4 + a % 4
            out[n, 0:64, :] = k[:, cols]
            out[n, 64:128, :] = v[:, cols]
            out[n, 128:256, :] = far[0:128, cols]
            for t in range(2):
                low = TILE * t + 16 * xb
                out[n, 256 + 16 * t : 272 + 16 * t, :] = q[low : low + 16, cols]


def mix_kernel(
    meta, stream, pre, post, mrpre, taps, he, hl, half, other, mixed, keep, give,
    sc, s2, xs, tf,
):
    odd = meta[5] == 1
    tf[0:TAPS, :] = taps[...].astype(F32)
    width = 1.0 / 8192.0
    total = half[...] + other[...]
    scale = lax.rsqrt(total * width + EPS_NORM)
    for tile in range(2):
        near = 64 * tile
        far = near + HALO
        sc[tile, 0:8, :] = jnp.broadcast_to(scale[0:8, far : far + 1], (8, LANES))
        sc[tile, 8:40, :] = jnp.broadcast_to(scale[:, near : near + 1], (TILE, LANES))
    lane = lax.broadcasted_iota(jnp.int32, (TILE, LANES), 1)
    for tile in range(2):
        factor = [jnp.ones((TILE, LANES), F32)]
        for j in range(TAPS):
            factor.append(sc[tile, pl.ds(8 - j, TILE), :])
        weight = jnp.zeros((TILE, LANES), F32)
        for q, (a, b) in enumerate(PAIRS):
            term = factor[a] * factor[b]
            weight = jnp.where(lane == q + 64 * tile, term if a == b else term * 2.0, weight)
        rows = slice(tile * TILE, (tile + 1) * TILE)
        squares = jnp.sum(weight * total, axis=1, keepdims=True)
        second = lax.rsqrt(jnp.maximum(squares, 0.0) * width + EPS_NORM)
        s2[rows, :] = jnp.broadcast_to(second, (TILE, LANES))

    def one(step, carry):
        cs = lanes_at(step, LANES)
        s = stream[:, cs].astype(F32)
        p = pre[:, cs].astype(F32)
        u = s * p
        own = jnp.concatenate([s[TILE - 8 : TILE], p[TILE - 8 : TILE]], axis=0)
        before, after = halo_rows(meta, he, hl, own, step)
        eu, lu = before[0:8] * before[8:16], after[0:8] * after[8:16]
        gate = post[:, cs].astype(F32)
        front = mrpre[:, cs].astype(F32)
        for tile, halo in enumerate((eu, lu)):
            rows = slice(tile * TILE, (tile + 1) * TILE)
            xs[tile, 0:8, :] = (halo * sc[tile, 0:8, :]).astype(BF16).astype(F32)
            xs[tile, 8:40, :] = (u[rows] * sc[tile, 8:40, :]).astype(BF16).astype(F32)
        values = []
        for tile in range(2):
            rows = slice(tile * TILE, (tile + 1) * TILE)
            acc = jnp.zeros((TILE, LANES), F32)
            for j in range(TAPS):
                acc = acc + tf[j : j + 1, cs] * xs[tile, pl.ds(8 - j, TILE), :]
            value = (s[rows] + gate[rows] * acc).astype(BF16)
            mixed[rows, cs] = value
            values.append((front[rows] * value.astype(F32) * s2[rows, :]).astype(BF16))
        keep[:, cs] = jnp.where(odd, values[0], values[1])
        give[:, cs] = jnp.where(odd, values[1], values[0])
        return carry

    lax.fori_loop(0, stream.shape[1] // LANES, one, 0)


def conv_kernel(meta, taps, mixed, post, keep, give, got, one, two, rest, out, state, ext):
    ext[0, 0:32, :] = two[32:64, :]
    ext[0, 32:64, :] = two[0:32, :]
    ext[0, 64:96, :] = one[32:64, :]
    ext[0, 96:128, :] = one[0:32, :]
    ext[0, 128:160, :] = give[...]
    ext[1, 0:32, :] = rest[64:96, :]
    ext[1, 32:64, :] = rest[32:64, :]
    ext[1, 64:96, :] = rest[0:32, :]
    ext[1, 96:128, :] = got[...]
    ext[1, 128:160, :] = keep[...]
    group_width = out.shape[1] // taps.shape[0]
    for g in range(taps.shape[0]):
        row = jnp.broadcast_to(taps[g : g + 1, :], (TILE, 256))
        toeplitz = pltpu.roll(row, 0, 1, stride=1, stride_axis=0)[:, 0:160].astype(BF16)
        cols = slice(g * group_width, (g + 1) * group_width)
        for part in range(2):
            place = meta[5] if part == 0 else 1 - meta[5]
            rows = pl.ds(pl.multiple_of(place * TILE, TILE), TILE)
            acc = jnp.dot(toeplitz, ext[part, :, cols], preferred_element_type=F32)
            value = mixed[rows, cols].astype(F32) + post[rows, cols].astype(F32) * acc
            out[rows, cols] = value.astype(BF16)

    @pl.when(meta[0] == 0)
    def _():
        state[...] = ext[1, 32:160, :]

    @pl.when(meta[0] != 0)
    def _():
        state[...] = jnp.zeros_like(state)


def attend_kernel(meta, slots, mine, twin, after, out, scores):
    xb, zh, c = meta[2], meta[4], meta[5]

    def pieces(n, carry):
        for slot in range(2):
            tile = slots[n * 2 + slot]
            held = jnp.maximum(tile, 0)
            late = (held >= 64).astype(jnp.int32)
            device = jnp.where(held >= 64, 127 - held, held)
            across_z = (device // 2) % 2 != zh
            holder = jnp.where(device % 2 == 1, device + 1, device + 63) % 64
            holder = jnp.where(across_z, holder, device)
            src, cd = holder // 4, holder % 2
            low = jnp.where(across_z, 128, 0) + late * TILE
            for kv in range(2):
                rows = pl.ds(pl.multiple_of(low + 64 * kv, TILE), TILE)
                value = jnp.where(cd == c, mine[src, rows, :], twin[src, rows, :])
                value = jnp.where(tile >= 0, value, jnp.zeros_like(value))
                first = 32 + (slot * 2 + kv) * TILE
                out[n, first : first + TILE, :] = value
        return carry

    lax.fori_loop(0, 16, pieces, 0, unroll=4)
    log_scale = math.log2(math.e) / math.sqrt(HEAD_DIM)
    def owner(core, far):
        def of(src):
            device = src * 4 + zh * 2 + core
            return (jnp.where(core == 1, device + 1, device + 63) % 64) if far else device

        return of

    groups = [(ref, 128 * far, owner(core, far)) for ref, core in ((mine, c), (twin, 1 - c)) for far in range(2)]

    def place(device, late, u):
        return (127 - device if late else device) * TILE + u

    def columns(late):
        col = lax.broadcasted_iota(jnp.int32, (1, 512), 1)
        return [place(of(col // TILE), late, col % TILE) for _, _, of in groups]

    def tiles(ref, low, count):
        return ref[:, low : low + count, :].reshape(16 * count, LANES)

    block = 128
    places = (columns(False), columns(True))
    for late in range(2):
        for part in range(256 // block):
            src0 = part * (block // 16)
            query = mine[src0 : src0 + block // 16, 256 + 16 * late : 272 + 16 * late, :]
            query = query.reshape(block, LANES)
            row = lax.broadcasted_iota(jnp.int32, (block, 1), 0)
            spot = place((src0 + row // 16) * 4 + zh * 2 + c, bool(late), xb * 16 + row % 16)
            top = jnp.full((block, LANES), MASKED, F32)
            jobs = []
            for key_late in range(late + 1):
                for g, (ref, low, _) in enumerate(groups):
                    jobs.append((len(jobs), key_late, g, ref, low + TILE * key_late))
            for n, key_late, g, ref, low in jobs:
                keys = tiles(ref, low, TILE)
                found = lax.dot_general(
                    query, keys, (((1,), (1,)), ((), ())), preferred_element_type=F32
                )
                if key_late == late:
                    found = jnp.where(places[key_late][g] <= spot, found, MASKED)
                scores[:, n * 512 : (n + 1) * 512] = found
                for k in range(4):
                    top = jnp.maximum(top, found[:, k * LANES : (k + 1) * LANES])
            top = jnp.max(top, axis=1, keepdims=True)
            total = jnp.zeros((block, LANES), F32)
            summed = jnp.zeros((block, LANES), F32)
            for n, key_late, g, ref, low in jobs:
                weights = jnp.exp2((scores[:, n * 512 : (n + 1) * 512] - top) * log_scale)
                for k in range(4):
                    total = total + weights[:, k * LANES : (k + 1) * LANES]
                values = tiles(ref, low + 64, TILE)
                summed = summed + jnp.dot(
                    weights.astype(BF16), values, preferred_element_type=F32
                )
            result = (summed / jnp.sum(total, axis=1, keepdims=True)).astype(BF16)
            out[src0 : src0 + block // 16, 16 * late : 16 * late + 16, :] = result.reshape(
                block // 16, 16, LANES
            )


def unpack_kernel(came, att, keys, values):
    for n in range(16):
        xa, xb, y = n // 8, (n // 4) % 2, n % 4
        a = xa * 4 + y
        cols = slice(a * LANES, (a + 1) * LANES)
        att[16 * xb : 16 * xb + 16, cols] = came[n, 0:16, :]
        att[TILE + 16 * xb : TILE + 16 * xb + 16, cols] = came[n, 16:32, :]
        for slot in range(2):
            rows = slice((xb * 2 + slot) * TILE, (xb * 2 + slot + 1) * TILE)
            low = 32 + slot * 2 * TILE
            keys[rows, cols] = came[n, low : low + TILE, :]
            values[rows, cols] = came[n, low + TILE : low + 2 * TILE, :]


def shape(dims, dtype=BF16):
    return jax.ShapeDtypeStruct(dims, dtype)


def body(stream, se_pre, se_post, se_taps, mr_pre, mr_post, mr_taps, query, key, value, owner):
    x, y, zh, c = (lax.axis_index(name) for name in CTX)
    me = ((x * 4 + y) * 2 + zh) * 2 + c
    meta = jnp.stack([me, x // 2, x % 2, y, zh, c, c, c]).astype(jnp.int32)
    rows, channels = stream.shape

    odd = c == 1
    early_raw = jnp.concatenate([stream[24:32], se_pre[24:32]], axis=0)
    late_raw = jnp.concatenate([stream[56:64], se_pre[56:64]], axis=0)
    outer = jnp.where(odd, early_raw, late_raw)
    halo_near = lax.ppermute(jnp.where(odd, late_raw, early_raw), "c", SWAP)
    crossing = jnp.concatenate([key, value, outer[:, :1024], outer[:, 1024:]], axis=0)
    far = ctx_route(crossing, across)
    taps = se_taps.T
    partial = call(
        stats_kernel,
        shape((TILE, LANES), F32),
        [pltpu.VMEM((rows, channels), F32)] * 3 + [pltpu.VMEM((8, channels), F32)],
        [V] * 4,
        flops=15_000_000,
        nbytes=800_000,
        name="stats",
    )(stream, se_pre, se_post, taps)
    sums = call(
        head_kernel,
        shape((TILE, LANES), F32),
        [pltpu.VMEM((2, 16, channels), F32)] + [pltpu.VMEM((2, 8, channels), F32)] * 2 + [pltpu.VMEM((8, channels), F32)],
        [S] + [V] * 7,
        flops=5_000_000,
        nbytes=300_000,
        name="head",
    )(meta, stream, se_pre, se_post, taps, far, halo_near, partial)
    packed, sums = lax.optimization_barrier((far, sums))
    half = sums + lax.ppermute(sums, "tp", [(i, i ^ 1) for i in range(4)])
    other = lax.ppermute(half, "tp", [(i, i ^ 2) for i in range(4)])
    mixed, keep, give = call(
        mix_kernel,
        [shape((rows, channels)), shape((TILE, channels)), shape((TILE, channels))],
        [pltpu.VMEM((2, 40, LANES), F32), pltpu.VMEM((64, LANES), F32), pltpu.VMEM((2, 40, LANES), F32)]
        + [pltpu.VMEM((8, channels), F32)],
        [S] + [V] * 9,
        flops=8_000_000,
        nbytes=3_500_000,
        name="mix",
    )(meta, stream, se_pre, se_post, mr_pre, taps, far, halo_near, half, other)

    got = lax.ppermute(give, "c", SWAP)
    pair = jnp.concatenate([keep, got], axis=0)
    heads = call(
        pack_kernel, shape((16, 288, LANES)), (), [V] * 4, nbytes=2_000_000, name="pack"
    )(key, value, packed, query)
    mine = lax.all_to_all(heads, ("x", "y"), 0, 0, tiled=True)
    two = ctx_route(pair, second_chip)
    one = ctx_route(pair, next_chip)
    mark = pair[:16, :128]
    mine, pair = lax.optimization_barrier((mine, pair))
    share = jnp.concatenate([one, two[:TILE]], axis=0)

    rest = lax.ppermute(share, "c", SWAP)
    twin = lax.ppermute(mine, "c", [(0, 1), (1, 0)])

    owners = owner[:, 0]
    tile_ids = jnp.arange(128, dtype=jnp.int32)
    earlier = tile_ids[:, None] > tile_ids[None, :]
    ranks = jnp.sum((earlier & (owners[:, None] == owners[None, :])).astype(jnp.int32), axis=1)
    place_of = owners * CAP + ranks
    want = (jnp.arange(16, dtype=jnp.int32)[:, None] * 4 + zh * 2 + c) * CAP
    want = (want + (x % 2) * 2 + jnp.arange(2, dtype=jnp.int32)[None, :]).reshape(32)
    match = want[:, None] == place_of[None, :]
    slots = jnp.sum(jnp.where(match, tile_ids[None, :] + 1, 0), axis=1) - 1

    answered = call(
        attend_kernel,
        shape((16, 160, LANES)),
        [pltpu.VMEM((128, 4096), F32)],
        [S, S, V, V, V],
        flops=1_000_000_000,
        nbytes=3_000_000,
        name="attend",
    )(meta, slots.astype(jnp.int32), mine, twin, mark)
    came = lax.all_to_all(answered, ("x", "y"), 0, 0, tiled=True)
    attention_out, cache_keys, cache_values = call(
        unpack_kernel,
        [shape((rows, 1024)), shape((128, 1024)), shape((128, 1024))],
        (),
        [V],
        nbytes=1_300_000,
        name="unpack",
    )(came)
    decode_cache = jnp.stack([cache_keys, cache_values], axis=1)

    reversed_taps = jnp.pad(mr_taps[:, ::-1].astype(F32), ((0, 0), (1, 127)))
    hyena_stream, filter_state = call(
        conv_kernel,
        [shape((rows, channels)), shape((128, channels))],
        [pltpu.VMEM((2, 160, channels), BF16)],
        [S] + [V] * 9,
        flops=100_000_000,
        nbytes=3_000_000,
        name="conv",
    )(meta, reversed_taps, mixed, mr_post, keep, give, got, one, two, rest)
    return hyena_stream, attention_out, decode_cache, filter_state


def solution(mesh):
    fine = Mesh(mesh.devices.reshape(4, 4, 2, 2, 4), (*CTX, "tp"))
    block = P(CTX, "tp")
    in_specs = (block, block, block, P("tp", None), block, block, P("tp", None), block, block, block, P())
    out_specs = (block, block, P(CTX, None, "tp"), block)
    return jax.shard_map(body, mesh=fine, in_specs=in_specs, out_specs=out_specs, check_vma=False)
```

time: 114 us -> 93.2 us (0.82)
  the two profiles are of different devices: /device:TPU:1 before, /device:TPU:33 now
where the time goes in v2:
time: 93.2 us; the launch traced here: 92.8 us
  starting transfers between devices  43.5 us (47%)
  waiting for transfers between devices  27 us (29%)
  Pallas kernels  15.8 us (17%)
  local copies, waits for them, and re-layouts  3.89 us (4%)
  other arithmetic  1.62 us (2%)
  between operations  0.94 us (1%)
    ppermute x3, starting transfers between devices, ctx_route(): return lax.ppermute(array, CTX, pairs)  15.1 us
    all_to_all x1, starting transfers between devices, body(): came = lax.all_to_all(answered, ('x', 'y'), 0, 0, tiled=True)  10.1 us
    ppermute x3, waiting for transfers between devices, ctx_route(): return lax.ppermute(array, CTX, pairs)  8.34 us
    all_to_all x1, waiting for transfers between devices, body(): came = lax.all_to_all(answered, ('x', 'y'), 0, 0, tiled=True)  6.95 us
    all_to_all x1, starting transfers between devices, body(): mine = lax.all_to_all(heads, ('x', 'y'), 0, 0, tiled=True)  6.74 us
    pallas_call x1, Pallas kernels, body(): call(attend_kernel, shape((16, 160, LANES)), [pltpu.VMEM((128, 4096), F32...  6.04 us
    ppermute x1, starting transfers between devices, body(): halo_near = lax.ppermute(jnp.where(odd, late_raw, early_raw), 'c', SWAP)  4.48 us
    all_to_all x1, waiting for transfers between devices, body(): mine = lax.all_to_all(heads, ('x', 'y'), 0, 0, tiled=True)  4.09 us
  transfers between devices with their start and end apart: 11, of which 7 were waited for; matrix products, arithmetic and copies ran while one was open for 2% of the time, Pallas kernels for 13%

profile of v2, /device:TPU:33, one launch (start us, length us, event | category | flops | bytes accessed | tf_op | source)
XLA Modules:
  0.0 92.8 jit_solution(242764194729746731)
XLA Ops:
  0.7 0.9 fusion.1
  1.6 1.0 %pad_maximum_fusion.2 = bf16[160,1024]{1,0:T(8,128)(2,1)S(1)} fusion(bf16[16,1024]{1,0:T(8,128)(2,1)S(1)} %get-tuple-element.45, bf16[16,1024]{1,0:T(8,128)(2,1)S(1)} %get-tuple-element.44, bf16[64,1024]{1,0:T(8,128)(2,1)} %v.1, bf16[64,1024]{1,0:T(8,128)(2,1)} %k.1), kind=kLoop, calls=%fused_computation.2 | loop fusion | flops 1310720 | bytes 655360 | tf_op jit(solution)/shard_map/concatenate | solution.py:374
  2.6 0.0 copy-start.3
  2.6 0.0 copy-start.4
  2.6 0.0 copy-start.8
  2.6 6.7 %collective-permute-start = (bf16[160,1024]{1,0:T(8,128)(2,1)S(1)}, bf16[160,1024]{1,0:T(8,128)(2,1)S(1)}, u32[]{:S(2)}, u32[]{:S(2)}) collective-permute-start(bf16[160,1024]{1,0:T(8,128)(2,1)S(1)} %pad_maximum_fusion.2), channel_id=1, source_target_pairs={{0,252},{4,8},{8,4},{12,16},{16,12},{20,24},{24,20},{28,32},{32,28... | collective-permute-start | bytes 983048 | tf_op jit(solution)/shard_map/ppermute | solution.py:27
  9.3 4.5 %collective-permute-start.1 = (bf16[16,2048]{1,0:T(8,128)(2,1)S(1)}, bf16[16,2048]{1,0:T(8,128)(2,1)S(1)}, u32[]{:S(2)}, u32[]{:S(2)}) collective-permute-start(bf16[16,2048]{1,0:T(8,128)(2,1)S(1)} %get-tuple-element.42), channel_id=1, source_target_pairs={{0,4},{4,0},{1,5},{5,1},{2,6},{6,2},{3,7},{7,3},{8,12},{12,8},{9,1... | collective-permute-start | bytes 196616 | tf_op jit(solution)/shard_map/ppermute | solution.py:373
  13.8 0.1 stack.38.meta
  13.9 0.0 copy-done
  13.9 2.6 %stats.1.partial = f32[32,128]{1,0:T(8,128)S(1)} custom-call(bf16[64,2048]{1,0:T(8,128)(2,1)S(1)} %copy-done, bf16[64,2048]{1,0:T(8,128)(2,1)S(1)} %copy-done.1, bf16[64,2048]{1,0:T(8,128)(2,1)S(1)} %copy-done.2, bf16[7,2048]{1,0:T(8,128)(2,1)S(1)} %bitcast.11), custom_call_target="tpu_custom_call" | custom-call | flops 15000000 | bytes 800000 | tf_op jit(solution)/shard_map/stats/pallas_call | solution.py:377
  16.5 0.0 collective-permute-done.1.near.hl
  16.5 8.3 %collective-permute-done.far.he = bf16[160,1024]{1,0:T(8,128)(2,1)S(1)} collective-permute-done((bf16[160,1024]{1,0:T(8,128)(2,1)S(1)}, bf16[160,1024]{1,0:T(8,128)(2,1)S(1)}, u32[]{:S(2)}, u32[]{:S(2)}) %collective-permute-start) | collective-permute-done | bytes 327712 | tf_op jit(solution)/shard_map/ppermute | solution.py:27
  24.8 1.6 %head.1 = f32[32,128]{1,0:T(8,128)S(1)} custom-call(s32[8]{0:T(128)S(1)} %stack.38.meta, bf16[64,2048]{1,0:T(8,128)(2,1)S(1)} %copy-done, bf16[64,2048]{1,0:T(8,128)(2,1)S(1)} %copy-done.1, bf16[64,2048]{1,0:T(8,128)(2,1)S(1)} %copy-done.2, bf16[7,2048]{1,0:T(8,128)(2,1)S(1)} %bitcast.12, bf16[160,1024]{1,0:T(8,128)(2,1)S(1)} %collective-permute-done.far.he, ...), custom_call_target="tpu_custom_call" | custom-call | flops 5000000 | bytes 300000 | tf_op jit(solution)/shard_map/head/pallas_call | solution.py:386
  26.5 0.0 copy-done.3
  26.5 1.2 %pack.1 = bf16[16,288,128]{2,1,0:T(8,128)(2,1)} custom-call(bf16[64,1024]{1,0:T(8,128)(2,1)S(1)} %copy-done.4, bf16[64,1024]{1,0:T(8,128)(2,1)S(1)} %copy-done.3, bf16[160,1024]{1,0:T(8,128)(2,1)S(1)} %collective-permute-done.far.he, bf16[64,1024]{1,0:T(8,128)(2,1)S(1)} %copy-done.8), custom_call_target="tpu_custom_call" | custom-call | bytes 2000000 | tf_op jit(solution)/shard_map/pack/pallas_call | solution.py:411
  27.7 6.7 %all-to-all-start = ((bf16[16,288,128]{2,1,0:T(8,128)(2,1)}), bf16[16,288,128]{2,1,0:T(8,128)(2,1)S(1)}, u32[]{:S(2)}, u32[]{:S(2)}) async-start(bf16[16,288,128]{2,1,0:T(8,128)(2,1)} %pack.1), calls=%async_computation | async-start | bytes 2359296 | tf_op jit(solution)/shard_map/all_to_all | solution.py:414
  34.4 0.0 copy-start.10
  34.4 0.1 collective-permute-start.2
  34.5 2.6 %collective-permute-done.2 = f32[32,128]{1,0:T(8,128)S(1)} collective-permute-done((f32[32,128]{1,0:T(8,128)S(1)}, f32[32,128]{1,0:T(8,128)S(1)}, u32[]{:S(2)}, u32[]{:S(2)}) %collective-permute-start.2) | collective-permute-done | bytes 16416 | tf_op jit(solution)/shard_map/ppermute | solution.py:396
  37.1 0.5 collective-permute-start.3
  37.7 3.2 %collective-permute-done.3.other = f32[32,128]{1,0:T(8,128)S(1)} collective-permute-done((f32[32,128]{1,0:T(8,128)S(1)}, f32[32,128]{1,0:T(8,128)S(1)}, u32[]{:S(2)}, u32[]{:S(2)}) %collective-permute-start.3) | collective-permute-done | bytes 16416 | tf_op jit(solution)/shard_map/ppermute | solution.py:397
  40.9 1.7 %mix.1 = (bf16[64,2048]{1,0:T(8,128)(2,1)S(1)}, bf16[32,2048]{1,0:T(8,128)(2,1)S(1)}, bf16[32,2048]{1,0:T(8,128)(2,1)S(1)}) custom-call(s32[8]{0:T(128)S(1)} %stack.38.meta, bf16[64,2048]{1,0:T(8,128)(2,1)S(1)} %copy-done, bf16[64,2048]{1,0:T(8,128)(2,1)S(1)} %copy-done.1, bf16[64,2048]{1,0:T(8,128)(2,1)S(1)} %copy-done.2, bf16[64,2048]{1,0:T(8,128)(2,1)S(1)} %copy-done.6, ...), custom_call_target="tpu_custom_call" | custom-call | flops 8000000 | bytes 3500000 | tf_op jit(solution)/shard_map/mix/pallas_call | solution.py:398
  42.6 3.0 %collective-permute-start.4 = (bf16[32,2048]{1,0:T(8,128)(2,1)S(1)}, bf16[32,2048]{1,0:T(8,128)(2,1)S(1)}, u32[]{:S(2)}, u32[]{:S(2)}) collective-permute-start(bf16[32,2048]{1,0:T(8,128)(2,1)S(1)} %get-tuple-element.18.give), channel_id=1, source_target_pairs={{0,4},{4,0},{1,5},{5,1},{2,6},{6,2},{3,7},{7,3},{8,12},{12,8},{9,1... | collective-permute-start | bytes 393224 | tf_op jit(solution)/shard_map/ppermute | solution.py:409
  45.6 0.7 constant_dynamic-update-slice_fusion.1
  46.2 0.3 collective-permute-done.4.got
  46.5 0.7 constant_dynamic-update-slice_fusion
  47.2 4.1 %all-to-all-done.mine = bf16[16,288,128]{2,1,0:T(8,128)(2,1)S(1)} async-done(((bf16[16,288,128]{2,1,0:T(8,128)(2,1)}), bf16[16,288,128]{2,1,0:T(8,128)(2,1)S(1)}, u32[]{:S(2)}, u32[]{:S(2)}) %all-to-all-start) | async-done | bytes 1179680 | tf_op jit(solution)/shard_map/all_to_all | solution.py:414
  51.3 3.4 %collective-permute-start.8 = (bf16[16,288,128]{2,1,0:T(8,128)(2,1)S(1)}, bf16[16,288,128]{2,1,0:T(8,128)(2,1)}, u32[]{:S(2)}, u32[]{:S(2)}) collective-permute-start(bf16[16,288,128]{2,1,0:T(8,128)(2,1)S(1)} %all-to-all-done.mine), channel_id=1, source_target_pairs={{0,4},{4,0},{1,5},{5,1},{2,6},{6,2},{3,7},{7,3},{8,12},{12,8},{9,1... | collective-permute-start | bytes 3538952 | tf_op jit(solution)/shard_map/ppermute | solution.py:422
  54.7 0.1 iota_add_fusion
  54.8 0.1 add.106
  54.9 0.2 convert_reduce_fusion
  55.1 2.1 %collective-permute-start.6 = (bf16[64,2048]{1,0:T(8,128)(2,1)}, bf16[64,2048]{1,0:T(8,128)(2,1)S(1)}, u32[]{:S(2)}, u32[]{:S(2)}) collective-permute-start(bf16[64,2048]{1,0:T(8,128)(2,1)} %constant_dynamic-update-slice_fusion), channel_id=1, source_target_pairs={{4,16},{12,24},{16,4},{20,32},{24,12},{28,40},{32,20},{36,48},{40,... | collective-permute-start | bytes 786440 | tf_op jit(solution)/shard_map/ppermute | solution.py:27
  57.2 0.2 select_reduce_fusion
  57.3 6.3 %collective-permute-start.5 = (bf16[64,2048]{1,0:T(8,128)(2,1)}, bf16[64,2048]{1,0:T(8,128)(2,1)S(1)}, u32[]{:S(2)}, u32[]{:S(2)}) collective-permute-start(bf16[64,2048]{1,0:T(8,128)(2,1)} %constant_dynamic-update-slice_fusion), channel_id=1, source_target_pairs={{4,8},{8,4},{12,16},{16,12},{20,24},{24,20},{28,32},{32,28},{36,40... | collective-permute-start | bytes 786440 | tf_op jit(solution)/shard_map/ppermute | solution.py:27
  63.7 0.0 collective-permute-done.6.two
  63.7 0.0 collective-permute-done.8.twin
  63.7 6.0 %attend.1 = bf16[16,160,128]{2,1,0:T(8,128)(2,1)} custom-call(s32[8]{0:T(128)S(1)} %stack.38.meta, s32[32]{0:T(128)S(1)} %broadcast_add_fusion.slots, bf16[16,288,128]{2,1,0:T(8,128)(2,1)S(1)} %all-to-all-done.mine, bf16[16,288,128]{2,1,0:T(8,128)(2,1)} %collective-permute-done.8.twin, bf16[16,128]{1,0:T(8,128)(2,1)S(1)} %slice.31.after), custom_call_target="tpu_custom_call" | custom-call | flops 1000000000 | bytes 3000000 | tf_op jit(solution)/shard_map/attend/pallas_call | solution.py:434
  69.8 10.1 %all-to-all-start.1 = ((bf16[16,160,128]{2,1,0:T(8,128)(2,1)}), bf16[16,160,128]{2,1,0:T(8,128)(2,1)S(1)}, u32[]{:S(2)}, u32[]{:S(2)}) async-start(bf16[16,160,128]{2,1,0:T(8,128)(2,1)} %attend.1), calls=%async_computation.1 | async-start | bytes 1310720 | tf_op jit(solution)/shard_map/all_to_all | solution.py:443
  79.9 0.0 collective-permute-done.5.one
  80.0 0.1 collective-permute-start.7
  80.1 0.1 rev.3
  80.2 0.1 pad_convert_fusion.taps
  80.3 1.5 %collective-permute-done.7.rest = bf16[96,2048]{1,0:T(8,128)(2,1)S(1)} collective-permute-done((bf16[96,2048]{1,0:T(8,128)(2,1)S(1)}, bf16[96,2048]{1,0:T(8,128)(2,1)S(1)}, u32[]{:S(2)}, u32[]{:S(2)}) %collective-permute-start.7) | collective-permute-done | bytes 393248 | tf_op jit(solution)/shard_map/ppermute | solution.py:421
  81.8 1.9 %conv.1 = (bf16[64,2048]{1,0:T(8,128)(2,1)}, bf16[128,2048]{1,0:T(8,128)(2,1)}) custom-call(s32[8]{0:T(128)S(1)} %stack.38.meta, f32[4,256]{1,0:T(4,128)S(1)} %pad_convert_fusion.taps, bf16[64,2048]{1,0:T(8,128)(2,1)S(1)} %get-tuple-element.16.mixed, bf16[64,2048]{1,0:T(8,128)(2,1)S(1)} %copy-done.7, bf16[32,2048]{1,0:T(8,128)(2,1)S(1)} %get-tuple-element.17.keep, ...), custom_call_target="tpu_custom_call" | custom-call | flops 100000000 | bytes 3000000 | tf_op jit(solution)/shard_map/conv/pallas_call | solution.py:455
  83.7 6.9 %all-to-all-done.1.came = bf16[16,160,128]{2,1,0:T(8,128)(2,1)S(1)} async-done(((bf16[16,160,128]{2,1,0:T(8,128)(2,1)}), bf16[16,160,128]{2,1,0:T(8,128)(2,1)S(1)}, u32[]{:S(2)}, u32[]{:S(2)}) %all-to-all-start.1) | async-done | bytes 655392 | tf_op jit(solution)/shard_map/all_to_all | solution.py:443
  90.6 0.8 unpack.1
  91.4 0.1 pad_maximum_fusion
  91.5 1.3 %copy.17 = bf16[128,2,1024]{2,1,0:T(2,128)(2,1)} copy(bf16[128,2,1024]{2,0,1:T(8,128)(2,1)S(1)} %pad_maximum_fusion) | data formatting | bytes 1048576
  (25 shorter events, 0.1 us)
Async XLA Ops:
  0.6 13.2 %copy-start.1 = (bf16[64,2048]{1,0:T(8,128)(2,1)S(1)}, bf16[64,2048]{1,0:T(8,128)(2,1)}, u32[]{:S(2)}) copy-start(bf16[64,2048]{1,0:T(8,128)(2,1)} %pre.5) | copy-start | bytes 786436
  0.6 13.2 %copy-start = (bf16[64,2048]{1,0:T(8,128)(2,1)S(1)}, bf16[64,2048]{1,0:T(8,128)(2,1)}, u32[]{:S(2)}) copy-start(bf16[64,2048]{1,0:T(8,128)(2,1)} %stream.5) | copy-start | bytes 786436
  0.7 13.2 %copy-start.2 = (bf16[64,2048]{1,0:T(8,128)(2,1)S(1)}, bf16[64,2048]{1,0:T(8,128)(2,1)}, u32[]{:S(2)}) copy-start(bf16[64,2048]{1,0:T(8,128)(2,1)} %post.6) | copy-start | bytes 786436
  0.7 13.2 %copy-start.5 = (bf16[2048,7]{0,1:T(8,128)(2,1)S(1)}, bf16[2048,7]{0,1:T(8,128)(2,1)}, u32[]{:S(2)}) copy-start(bf16[2048,7]{0,1:T(8,128)(2,1)} %param.14) | copy-start | bytes 86020
  2.6 23.8 %copy-start.3 = (bf16[64,1024]{1,0:T(8,128)(2,1)S(1)}, bf16[64,1024]{1,0:T(8,128)(2,1)}, u32[]{:S(2)}) copy-start(bf16[64,1024]{1,0:T(8,128)(2,1)} %v.1) | copy-start | bytes 393220
  2.6 23.8 %copy-start.4 = (bf16[64,1024]{1,0:T(8,128)(2,1)S(1)}, bf16[64,1024]{1,0:T(8,128)(2,1)}, u32[]{:S(2)}) copy-start(bf16[64,1024]{1,0:T(8,128)(2,1)} %k.1) | copy-start | bytes 393220
  2.6 23.8 %copy-start.8 = (bf16[64,1024]{1,0:T(8,128)(2,1)S(1)}, bf16[64,1024]{1,0:T(8,128)(2,1)}, u32[]{:S(2)}) copy-start(bf16[64,1024]{1,0:T(8,128)(2,1)} %q.1) | copy-start | bytes 393220
  2.6 22.2 %collective-permute-start = (bf16[160,1024]{1,0:T(8,128)(2,1)S(1)}, bf16[160,1024]{1,0:T(8,128)(2,1)S(1)}, u32[]{:S(2)}, u32[]{:S(2)}) collective-permute-start(bf16[160,1024]{1,0:T(8,128)(2,1)S(1)} %pad_maximum_fusion.2), channel_id=1, source_target_pairs={{0,252},{4,8},{8,4},{12,16},{16,12},{20,24},{24,20},{28,32},{32,28... | collective-permute-start | bytes 983048 | tf_op jit(solution)/shard_map/ppermute | solution.py:27
  9.3 7.2 %collective-permute-start.1 = (bf16[16,2048]{1,0:T(8,128)(2,1)S(1)}, bf16[16,2048]{1,0:T(8,128)(2,1)S(1)}, u32[]{:S(2)}, u32[]{:S(2)}) collective-permute-start(bf16[16,2048]{1,0:T(8,128)(2,1)S(1)} %get-tuple-element.42), channel_id=1, source_target_pairs={{0,4},{4,0},{1,5},{5,1},{2,6},{6,2},{3,7},{7,3},{8,12},{12,8},{9,1... | collective-permute-start | bytes 196616 | tf_op jit(solution)/shard_map/ppermute | solution.py:373
  27.7 13.2 %copy-start.6 = (bf16[64,2048]{1,0:T(8,128)(2,1)S(1)}, bf16[64,2048]{1,0:T(8,128)(2,1)}, u32[]{:S(2)}) copy-start(bf16[64,2048]{1,0:T(8,128)(2,1)} %mrpre.1) | copy-start | bytes 786436
  27.7 23.6 %all-to-all-start = ((bf16[16,288,128]{2,1,0:T(8,128)(2,1)}), bf16[16,288,128]{2,1,0:T(8,128)(2,1)S(1)}, u32[]{:S(2)}, u32[]{:S(2)}) async-start(bf16[16,288,128]{2,1,0:T(8,128)(2,1)} %pack.1), calls=%async_computation | async-start | bytes 2359296 | tf_op jit(solution)/shard_map/all_to_all | solution.py:414
  34.4 20.4 %copy-start.10 = (s32[128,1]{0,1:T(1,128)S(1)}, s32[128,1]{0,1:T(1,128)}, u32[]{:S(2)}) copy-start(s32[128,1]{0,1:T(1,128)} %param.21) | copy-start | bytes 1540
  34.4 2.7 %collective-permute-start.2 = (f32[32,128]{1,0:T(8,128)S(1)}, f32[32,128]{1,0:T(8,128)S(1)}, u32[]{:S(2)}, u32[]{:S(2)}) collective-permute-start(f32[32,128]{1,0:T(8,128)S(1)} %head.1), channel_id=1, source_target_pairs={{0,1},{1,0},{2,3},{3,2},{4,5},{5,4},{6,7},{7,6},{8,9},{9,8},{10,11... | collective-permute-start | bytes 49160 | tf_op jit(solution)/shard_map/ppermute | solution.py:396
  37.1 3.8 %collective-permute-start.3 = (f32[32,128]{1,0:T(8,128)S(1)}, f32[32,128]{1,0:T(8,128)S(1)}, u32[]{:S(2)}, u32[]{:S(2)}) collective-permute-start(f32[32,128]{1,0:T(8,128)S(1)} %add.96.half), channel_id=1, source_target_pairs={{0,2},{1,3},{2,0},{3,1},{4,6},{5,7},{6,4},{7,5},{8,10},{9,11},{10,... | collective-permute-start | bytes 49160 | tf_op jit(solution)/shard_map/ppermute | solution.py:397
  42.6 3.9 %collective-permute-start.4 = (bf16[32,2048]{1,0:T(8,128)(2,1)S(1)}, bf16[32,2048]{1,0:T(8,128)(2,1)S(1)}, u32[]{:S(2)}, u32[]{:S(2)}) collective-permute-start(bf16[32,2048]{1,0:T(8,128)(2,1)S(1)} %get-tuple-element.18.give), channel_id=1, source_target_pairs={{0,4},{4,0},{1,5},{5,1},{2,6},{6,2},{3,7},{7,3},{8,12},{12,8},{9,1... | collective-permute-start | bytes 393224 | tf_op jit(solution)/shard_map/ppermute | solution.py:409
  51.3 12.4 %collective-permute-start.8 = (bf16[16,288,128]{2,1,0:T(8,128)(2,1)S(1)}, bf16[16,288,128]{2,1,0:T(8,128)(2,1)}, u32[]{:S(2)}, u32[]{:S(2)}) collective-permute-start(bf16[16,288,128]{2,1,0:T(8,128)(2,1)S(1)} %all-to-all-done.mine), channel_id=1, source_target_pairs={{0,4},{4,0},{1,5},{5,1},{2,6},{6,2},{3,7},{7,3},{8,12},{12,8},{9,1... | collective-permute-start | bytes 3538952 | tf_op jit(solution)/shard_map/ppermute | solution.py:422
  55.1 8.6 %collective-permute-start.6 = (bf16[64,2048]{1,0:T(8,128)(2,1)}, bf16[64,2048]{1,0:T(8,128)(2,1)S(1)}, u32[]{:S(2)}, u32[]{:S(2)}) collective-permute-start(bf16[64,2048]{1,0:T(8,128)(2,1)} %constant_dynamic-update-slice_fusion), channel_id=1, source_target_pairs={{4,16},{12,24},{16,4},{20,32},{24,12},{28,40},{32,20},{36,48},{40,... | collective-permute-start | bytes 786440 | tf_op jit(solution)/shard_map/ppermute | solution.py:27
  57.3 22.6 %collective-permute-start.5 = (bf16[64,2048]{1,0:T(8,128)(2,1)}, bf16[64,2048]{1,0:T(8,128)(2,1)S(1)}, u32[]{:S(2)}, u32[]{:S(2)}) collective-permute-start(bf16[64,2048]{1,0:T(8,128)(2,1)} %constant_dynamic-update-slice_fusion), channel_id=1, source_target_pairs={{4,8},{8,4},{12,16},{16,12},{20,24},{24,20},{28,32},{32,28},{36,40... | collective-permute-start | bytes 786440 | tf_op jit(solution)/shard_map/ppermute | solution.py:27
  69.8 10.3 %copy-start.9 = (bf16[4,128]{1,0:T(4,128)(2,1)S(1)}, bf16[4,128]{1,0:T(4,128)(2,1)}, u32[]{:S(2)}) copy-start(bf16[4,128]{1,0:T(4,128)(2,1)} %param.17) | copy-start | bytes 3076
  69.8 12.0 %copy-start.7 = (bf16[64,2048]{1,0:T(8,128)(2,1)S(1)}, bf16[64,2048]{1,0:T(8,128)(2,1)}, u32[]{:S(2)}) copy-start(bf16[64,2048]{1,0:T(8,128)(2,1)} %post.7) | copy-start | bytes 786436
  69.8 20.8 %all-to-all-start.1 = ((bf16[16,160,128]{2,1,0:T(8,128)(2,1)}), bf16[16,160,128]{2,1,0:T(8,128)(2,1)S(1)}, u32[]{:S(2)}, u32[]{:S(2)}) async-start(bf16[16,160,128]{2,1,0:T(8,128)(2,1)} %attend.1), calls=%async_computation.1 | async-start | bytes 1310720 | tf_op jit(solution)/shard_map/all_to_all | solution.py:443
  80.0 1.8 %collective-permute-start.7 = (bf16[96,2048]{1,0:T(8,128)(2,1)S(1)}, bf16[96,2048]{1,0:T(8,128)(2,1)S(1)}, u32[]{:S(2)}, u32[]{:S(2)}) collective-permute-start(bf16[96,2048]{1,0:T(8,128)(2,1)S(1)} %pad_maximum_fusion.1), channel_id=1, source_target_pairs={{0,4},{4,0},{1,5},{5,1},{2,6},{6,2},{3,7},{7,3},{8,12},{12,8},{9,1... | collective-permute-start | bytes 1179656 | tf_op jit(solution)/shard_map/ppermute | solution.py:421

commit v3 on v2

--- a/solution.py
+++ b/solution.py
@@ -69,7 +69,7 @@
 
 def halo_rows(meta, far, near, early, step):
     odd = meta[5] == 1
-    rows = pl.ds(pl.multiple_of(128 + step // 8 * 16, 16), 16)
+    rows = pl.ds(pl.multiple_of(64 + step // 8 * 16, 16), 16)
     other = far[rows, lanes_at(step % 8, LANES)].astype(F32)
     other = jnp.where(meta[0] == 0, jnp.zeros_like(other), other)
     twin = near[:, lanes_at(step, LANES)].astype(F32)
@@ -155,14 +155,15 @@
     out[8:TILE, :] = partial[8:TILE, :]
 
 
-def pack_kernel(k, v, far, q, out):
+def pack_kernel(k, v, far, far_values, q, out):
     for a in range(8):
         cols = slice(a * LANES, (a + 1) * LANES)
         for xb in range(2):
             n = ((a // 4) * 2 + xb) * 4 + a % 4
             out[n, 0:64, :] = k[:, cols]
             out[n, 64:128, :] = v[:, cols]
-            out[n, 128:256, :] = far[0:128, cols]
+            out[n, 128:192, :] = far[0:64, cols]
+            out[n, 192:256, :] = far_values[:, cols]
             for t in range(2):
                 low = TILE * t + 16 * xb
                 out[n, 256 + 16 * t : 272 + 16 * t, :] = q[low : low + 16, cols]
@@ -258,12 +259,24 @@
         state[...] = jnp.zeros_like(state)
 
 
+def slots_kernel(meta, owner_row, owner_col, out):
+    xb, zh, c = meta[2], meta[4], meta[5]
+    row = lax.broadcasted_iota(jnp.int32, (128, 128), 0)
+    col = lax.broadcasted_iota(jnp.int32, (128, 128), 1)
+    mine = owner_col[...]
+    before = (owner_row[...] == mine) & (col < row)
+    rank = jnp.sum(jnp.where(before, 1, 0), axis=1, keepdims=True)
+    want = (col // 2 * 4 + zh * 2 + c) * CAP + xb * 2 + col % 2
+    found = (mine * CAP + rank == want) & (col < 32)
+    out[...] = jnp.sum(jnp.where(found, row + 1, 0), axis=0, keepdims=True) - 1
+
+
 def attend_kernel(meta, slots, mine, twin, after, out, scores):
     xb, zh, c = meta[2], meta[4], meta[5]
 
     def pieces(n, carry):
         for slot in range(2):
-            tile = slots[n * 2 + slot]
+            tile = slots[0, n * 2 + slot]
             held = jnp.maximum(tile, 0)
             late = (held >= 64).astype(jnp.int32)
             device = jnp.where(held >= 64, 127 - held, held)
@@ -371,8 +384,9 @@
     late_raw = jnp.concatenate([stream[56:64], se_pre[56:64]], axis=0)
     outer = jnp.where(odd, early_raw, late_raw)
     halo_near = lax.ppermute(jnp.where(odd, late_raw, early_raw), "c", SWAP)
-    crossing = jnp.concatenate([key, value, outer[:, :1024], outer[:, 1024:]], axis=0)
-    far = ctx_route(crossing, across)
+    far = ctx_route(jnp.concatenate([key, outer[:, :1024], outer[:, 1024:]], axis=0), across)
+    held, halo_near = lax.optimization_barrier((value, halo_near))
+    far_values = ctx_route(held, across)
     taps = se_taps.T
     partial = call(
         stats_kernel,
@@ -392,8 +406,8 @@
         nbytes=300_000,
         name="head",
     )(meta, stream, se_pre, se_post, taps, far, halo_near, partial)
-    packed, sums = lax.optimization_barrier((far, sums))
     half = sums + lax.ppermute(sums, "tp", [(i, i ^ 1) for i in range(4)])
+    packed, half = lax.optimization_barrier((far_values, half))
     other = lax.ppermute(half, "tp", [(i, i ^ 2) for i in range(4)])
     mixed, keep, give = call(
         mix_kernel,
@@ -409,8 +423,8 @@
     got = lax.ppermute(give, "c", SWAP)
     pair = jnp.concatenate([keep, got], axis=0)
     heads = call(
-        pack_kernel, shape((16, 288, LANES)), (), [V] * 4, nbytes=2_000_000, name="pack"
-    )(key, value, packed, query)
+        pack_kernel, shape((16, 288, LANES)), (), [V] * 5, nbytes=2_000_000, name="pack"
+    )(key, value, far, packed, query)
     mine = lax.all_to_all(heads, ("x", "y"), 0, 0, tiled=True)
     two = ctx_route(pair, second_chip)
     one = ctx_route(pair, next_chip)
@@ -421,16 +435,9 @@
     rest = lax.ppermute(share, "c", SWAP)
     twin = lax.ppermute(mine, "c", [(0, 1), (1, 0)])
 
-    owners = owner[:, 0]
-    tile_ids = jnp.arange(128, dtype=jnp.int32)
-    earlier = tile_ids[:, None] > tile_ids[None, :]
-    ranks = jnp.sum((earlier & (owners[:, None] == owners[None, :])).astype(jnp.int32), axis=1)
-    place_of = owners * CAP + ranks
-    want = (jnp.arange(16, dtype=jnp.int32)[:, None] * 4 + zh * 2 + c) * CAP
-    want = (want + (x % 2) * 2 + jnp.arange(2, dtype=jnp.int32)[None, :]).reshape(32)
-    match = want[:, None] == place_of[None, :]
-    slots = jnp.sum(jnp.where(match, tile_ids[None, :] + 1, 0), axis=1) - 1
-
+    slots = call(
+        slots_kernel, shape((1, 128), jnp.int32), (), [S, V, V], flops=20_000_000_000, nbytes=70_000, name="slots"
+    )(meta, owner.reshape(1, 128), owner)
     answered = call(
         attend_kernel,
         shape((16, 160, LANES)),
@@ -439,7 +446,7 @@
         flops=1_000_000_000,
         nbytes=3_000_000,
         name="attend",
-    )(meta, slots.astype(jnp.int32), mine, twin, mark)
+    )(meta, slots, mine, twin, mark)
     came = lax.all_to_all(answered, ("x", "y"), 0, 0, tiled=True)
     attention_out, cache_keys, cache_values = call(
         unpack_kernel,

time: 93.2 us -> 85.3 us (0.915)
  waiting for transfers between devices: 27 us -> 18.7 us
  starting transfers between devices: 43.5 us -> 45.8 us
  local copies, waits for them, and re-layouts: 3.89 us -> 2.6 us
    ppermute x3 -> x4, waiting for transfers between devices: 8.34 us -> 2.02 us  [ctx_route(): return lax.ppermute(array, CTX, pairs)]
    all_to_all x1, waiting for transfers between devices: 4.09 us -> 0.01 us  [body(): mine = lax.all_to_all(heads, ('x', 'y'), 0, 0, tiled=True)]
    ppermute x1, waiting for transfers between devices: 3.24 us -> 1.14 us  [body(): other = lax.ppermute(half, 'tp', [(i, i ^ 2) for i in range(4)])]
    ppermute x1, starting transfers between devices: 0.54 us -> 2.32 us  [body(): other = lax.ppermute(half, 'tp', [(i, i ^ 2) for i in range(4)])]
    ppermute x1, waiting for transfers between devices: 0.01 us -> 1.63 us  [body(): twin = lax.ppermute(mine, 'c', [(0, 1), (1, 0)])]
    all_to_all x1, starting transfers between devices: 10.1 us -> 11.6 us  [body(): came = lax.all_to_all(answered, ('x', 'y'), 0, 0, tiled=True)]
    ppermute x1, waiting for transfers between devices: 2.58 us -> 3.94 us  [body(): half = sums + lax.ppermute(sums, 'tp', [(i, i ^ 1) for i in range(4)])]
    ppermute x1, starting transfers between devices: 3.39 us -> 2.31 us  [body(): twin = lax.ppermute(mine, 'c', [(0, 1), (1, 0)])]
  transfers between devices with their start and end apart: 11 -> 12, of which waited for: 7 -> 9; matrix products, arithmetic and copies ran while one was open for 2% -> 1% of each run, Pallas kernels for 13% -> 16%
where the time goes in v3:
time: 85.3 us; the launch traced here: 85 us
  starting transfers between devices  45.8 us (54%)
  waiting for transfers between devices  18.7 us (22%)
  Pallas kernels  15.9 us (19%)
  local copies, waits for them, and re-layouts  2.6 us (3%)
  other arithmetic  1.15 us (1%)
  between operations  0.89 us (1%)
    ppermute x4, starting transfers between devices, ctx_route(): return lax.ppermute(array, CTX, pairs)  14.5 us
    all_to_all x1, starting transfers between devices, body(): came = lax.all_to_all(answered, ('x', 'y'), 0, 0, tiled=True)  11.6 us
    all_to_all x1, starting transfers between devices, body(): mine = lax.all_to_all(heads, ('x', 'y'), 0, 0, tiled=True)  7.1 us
    all_to_all x1, waiting for transfers between devices, body(): came = lax.all_to_all(answered, ('x', 'y'), 0, 0, tiled=True)  6.52 us
    pallas_call x1, Pallas kernels, body(): call(attend_kernel, shape((16, 160, LANES)), [pltpu.VMEM((128, 4096), F32...  5.35 us
    ppermute x1, starting transfers between devices, body(): halo_near = lax.ppermute(jnp.where(odd, late_raw, early_raw), 'c', SWAP)  4.48 us
    ppermute x1, waiting for transfers between devices, body(): half = sums + lax.ppermute(sums, 'tp', [(i, i ^ 1) for i in range(4)])  3.94 us
    ppermute x1, starting transfers between devices, body(): got = lax.ppermute(give, 'c', SWAP)  3.3 us
  transfers between devices with their start and end apart: 12, of which 9 were waited for; matrix products, arithmetic and copies ran while one was open for 1% of the time, Pallas kernels for 16%

profile of v3, /device:TPU:33, one launch (start us, length us, event | category | flops | bytes accessed | tf_op | source)
XLA Modules:
  0.0 85.0 jit_solution(3335755763038010896)
XLA Ops:
  0.6 0.0 copy-start.1
  0.7 0.9 %fusion = (bf16[8,2048]{1,0:T(8,128)(2,1)S(1)}, bf16[8,2048]{1,0:T(8,128)(2,1)S(1)}, bf16[8,2048]{1,0:T(8,128)(2,1)S(1)}, bf16[8,2048]{1,0:T(8,128)(2,1)S(1)}) fusion(bf16[64,2048]{1,0:T(8,128)(2,1)} %stream.5, bf16[64,2048]{1,0:T(8,128)(2,1)} %pre.5), kind=kLoop, calls=%fused_computation.10 | loop fusion | bytes 262144 | tf_op jit(solution)/shard_map/slice | solution.py:383
  1.6 0.0 copy-start.3
  1.6 0.0 copy-start.7
  1.6 0.0 copy-start.8
  1.6 1.0 %pad_maximum_fusion.2 = bf16[96,1024]{1,0:T(8,128)(2,1)S(1)} fusion(bf16[16,1024]{1,0:T(8,128)(2,1)S(1)} %get-tuple-element.41, bf16[16,1024]{1,0:T(8,128)(2,1)S(1)} %get-tuple-element.40, bf16[64,1024]{1,0:T(8,128)(2,1)} %k.1), kind=kLoop, calls=%fused_computation.2 | loop fusion | flops 589824 | bytes 393216 | tf_op jit(solution)/shard_map/concatenate | solution.py:387
  2.6 6.7 %collective-permute-start = (bf16[96,1024]{1,0:T(8,128)(2,1)S(1)}, bf16[96,1024]{1,0:T(8,128)(2,1)S(1)}, u32[]{:S(2)}, u32[]{:S(2)}) collective-permute-start(bf16[96,1024]{1,0:T(8,128)(2,1)S(1)} %pad_maximum_fusion.2), channel_id=1, source_target_pairs={{0,252},{4,8},{8,4},{12,16},{16,12},{20,24},{24,20},{28,32},{32,28... | collective-permute-start | bytes 589832 | tf_op jit(solution)/shard_map/ppermute | solution.py:27
  9.3 4.5 %collective-permute-start.1 = (bf16[16,2048]{1,0:T(8,128)(2,1)S(1)}, bf16[16,2048]{1,0:T(8,128)(2,1)S(1)}, u32[]{:S(2)}, u32[]{:S(2)}) collective-permute-start(bf16[16,2048]{1,0:T(8,128)(2,1)S(1)} %get-tuple-element.38), channel_id=1, source_target_pairs={{0,4},{4,0},{1,5},{5,1},{2,6},{6,2},{3,7},{7,3},{8,12},{12,8},{9,1... | collective-permute-start | bytes 196616 | tf_op jit(solution)/shard_map/ppermute | solution.py:386
  13.8 0.9 %collective-permute-done.1.near.hl = bf16[16,2048]{1,0:T(8,128)(2,1)S(1)} collective-permute-done((bf16[16,2048]{1,0:T(8,128)(2,1)S(1)}, bf16[16,2048]{1,0:T(8,128)(2,1)S(1)}, u32[]{:S(2)}, u32[]{:S(2)}) %collective-permute-start.1) | collective-permute-done | bytes 65568 | tf_op jit(solution)/shard_map/ppermute | solution.py:386
  14.7 0.0 collective-permute-start.2
  14.7 0.1 stack.38.meta
  14.7 0.0 copy-done
  14.8 2.6 %stats.1.partial = f32[32,128]{1,0:T(8,128)S(1)} custom-call(bf16[64,2048]{1,0:T(8,128)(2,1)S(1)} %copy-done, bf16[64,2048]{1,0:T(8,128)(2,1)S(1)} %copy-done.1, bf16[64,2048]{1,0:T(8,128)(2,1)S(1)} %copy-done.2, bf16[7,2048]{1,0:T(8,128)(2,1)S(1)} %bitcast.10), custom_call_target="tpu_custom_call" | custom-call | flops 15000000 | bytes 800000 | tf_op jit(solution)/shard_map/stats/pallas_call | solution.py:391
  17.3 1.8 %collective-permute-done.far.he = bf16[96,1024]{1,0:T(8,128)(2,1)S(1)} collective-permute-done((bf16[96,1024]{1,0:T(8,128)(2,1)S(1)}, bf16[96,1024]{1,0:T(8,128)(2,1)S(1)}, u32[]{:S(2)}, u32[]{:S(2)}) %collective-permute-start) | collective-permute-done | bytes 196640 | tf_op jit(solution)/shard_map/ppermute | solution.py:27
  19.2 1.6 %head.1 = f32[32,128]{1,0:T(8,128)S(1)} custom-call(s32[8]{0:T(128)S(1)} %stack.38.meta, bf16[64,2048]{1,0:T(8,128)(2,1)S(1)} %copy-done, bf16[64,2048]{1,0:T(8,128)(2,1)S(1)} %copy-done.1, bf16[64,2048]{1,0:T(8,128)(2,1)S(1)} %copy-done.2, bf16[7,2048]{1,0:T(8,128)(2,1)S(1)} %bitcast.11, bf16[96,1024]{1,0:T(8,128)(2,1)S(1)} %collective-permute-done.far.he, ...), custom_call_target="tpu_custom_call" | custom-call | flops 5000000 | bytes 300000 | tf_op jit(solution)/shard_map/head/pallas_call | solution.py:400
  20.8 0.1 collective-permute-start.3
  20.9 3.9 %collective-permute-done.3 = f32[32,128]{1,0:T(8,128)S(1)} collective-permute-done((f32[32,128]{1,0:T(8,128)S(1)}, f32[32,128]{1,0:T(8,128)S(1)}, u32[]{:S(2)}, u32[]{:S(2)}) %collective-permute-start.3) | collective-permute-done | bytes 16416 | tf_op jit(solution)/shard_map/ppermute | solution.py:409
  24.9 0.2 collective-permute-done.2.far_values
  25.1 1.2 %pack.1 = bf16[16,288,128]{2,1,0:T(8,128)(2,1)} custom-call(bf16[64,1024]{1,0:T(8,128)(2,1)S(1)} %copy-done.3, bf16[64,1024]{1,0:T(8,128)(2,1)S(1)} %copy-done.7, bf16[96,1024]{1,0:T(8,128)(2,1)S(1)} %collective-permute-done.far.he, bf16[64,1024]{1,0:T(8,128)(2,1)S(1)} %collective-permute-done.2.far_values, bf16[64,1024]{1,0:T(8,128)(2,1)S(1)} %copy-done.8), custom_call_target="tpu_custom_call" | custom-call | bytes 2000000 | tf_op jit(solution)/shard_map/pack/pallas_call | solution.py:425
  26.2 7.1 %all-to-all-start = ((bf16[16,288,128]{2,1,0:T(8,128)(2,1)}), bf16[16,288,128]{2,1,0:T(8,128)(2,1)S(1)}, u32[]{:S(2)}, u32[]{:S(2)}) async-start(bf16[16,288,128]{2,1,0:T(8,128)(2,1)} %pack.1), calls=%async_computation | async-start | bytes 2359296 | tf_op jit(solution)/shard_map/all_to_all | solution.py:428
  33.4 2.3 %collective-permute-start.4 = (f32[32,128]{1,0:T(8,128)S(1)}, f32[32,128]{1,0:T(8,128)S(1)}, u32[]{:S(2)}, u32[]{:S(2)}) collective-permute-start(f32[32,128]{1,0:T(8,128)S(1)} %add.23.half), channel_id=1, source_target_pairs={{0,2},{1,3},{2,0},{3,1},{4,6},{5,7},{6,4},{7,5},{8,10},{9,11},{10,... | collective-permute-start | bytes 49160 | tf_op jit(solution)/shard_map/ppermute | solution.py:411
  35.7 0.1 copy.15.owner_col
  35.8 1.1 %collective-permute-done.4.other = f32[32,128]{1,0:T(8,128)S(1)} collective-permute-done((f32[32,128]{1,0:T(8,128)S(1)}, f32[32,128]{1,0:T(8,128)S(1)}, u32[]{:S(2)}, u32[]{:S(2)}) %collective-permute-start.4) | collective-permute-done | bytes 16416 | tf_op jit(solution)/shard_map/ppermute | solution.py:411
  36.9 0.0 copy-done.5
  36.9 1.7 %mix.1 = (bf16[64,2048]{1,0:T(8,128)(2,1)S(1)}, bf16[32,2048]{1,0:T(8,128)(2,1)S(1)}, bf16[32,2048]{1,0:T(8,128)(2,1)S(1)}) custom-call(s32[8]{0:T(128)S(1)} %stack.38.meta, bf16[64,2048]{1,0:T(8,128)(2,1)S(1)} %copy-done, bf16[64,2048]{1,0:T(8,128)(2,1)S(1)} %copy-done.1, bf16[64,2048]{1,0:T(8,128)(2,1)S(1)} %copy-done.2, bf16[64,2048]{1,0:T(8,128)(2,1)S(1)} %copy-done.5, ...), custom_call_target="tpu_custom_call" | custom-call | flops 8000000 | bytes 3500000 | tf_op jit(solution)/shard_map/mix/pallas_call | solution.py:412
  38.6 3.3 %collective-permute-start.5 = (bf16[32,2048]{1,0:T(8,128)(2,1)S(1)}, bf16[32,2048]{1,0:T(8,128)(2,1)S(1)}, u32[]{:S(2)}, u32[]{:S(2)}) collective-permute-start(bf16[32,2048]{1,0:T(8,128)(2,1)S(1)} %get-tuple-element.22.give), channel_id=1, source_target_pairs={{0,4},{4,0},{1,5},{5,1},{2,6},{6,2},{3,7},{7,3},{8,12},{12,8},{9,1... | collective-permute-start | bytes 393224 | tf_op jit(solution)/shard_map/ppermute | solution.py:423
  41.9 1.0 %collective-permute-done.5.got = bf16[32,2048]{1,0:T(8,128)(2,1)S(1)} collective-permute-done((bf16[32,2048]{1,0:T(8,128)(2,1)S(1)}, bf16[32,2048]{1,0:T(8,128)(2,1)S(1)}, u32[]{:S(2)}, u32[]{:S(2)}) %collective-permute-start.5) | collective-permute-done | bytes 131104 | tf_op jit(solution)/shard_map/ppermute | solution.py:423
  42.9 3.7 %collective-permute-start.7 = (bf16[64,2048]{1,0:T(8,128)(2,1)S(1)}, bf16[64,2048]{1,0:T(8,128)(2,1)S(1)}, u32[]{:S(2)}, u32[]{:S(2)}) collective-permute-start(bf16[64,2048]{1,0:T(8,128)(2,1)S(1)} %constant_dynamic-update-slice_fusion), channel_id=1, source_target_pairs={{4,16},{12,24},{16,4},{20,32},{24,12},{28,40},{32,20},{36,48},{40,... | collective-permute-start | bytes 786440 | tf_op jit(solution)/shard_map/ppermute | solution.py:27
  46.6 4.2 %collective-permute-start.6 = (bf16[64,2048]{1,0:T(8,128)(2,1)S(1)}, bf16[64,2048]{1,0:T(8,128)(2,1)S(1)}, u32[]{:S(2)}, u32[]{:S(2)}) collective-permute-start(bf16[64,2048]{1,0:T(8,128)(2,1)S(1)} %constant_dynamic-update-slice_fusion), channel_id=1, source_target_pairs={{4,8},{8,4},{12,16},{16,12},{20,24},{24,20},{28,32},{32,28},{36,40... | collective-permute-start | bytes 786440 | tf_op jit(solution)/shard_map/ppermute | solution.py:27
  50.8 0.0 all-to-all-done.mine
  50.8 2.3 %collective-permute-start.9 = (bf16[16,288,128]{2,1,0:T(8,128)(2,1)S(1)}, bf16[16,288,128]{2,1,0:T(8,128)(2,1)S(1)}, u32[]{:S(2)}, u32[]{:S(2)}) collective-permute-start(bf16[16,288,128]{2,1,0:T(8,128)(2,1)S(1)} %all-to-all-done.mine), channel_id=1, source_target_pairs={{0,4},{4,0},{1,5},{5,1},{2,6},{6,2},{3,7},{7,3},{8,12},{12,8},{9,1... | collective-permute-start | bytes 3538952 | tf_op jit(solution)/shard_map/ppermute | solution.py:436
  53.1 0.8 slots.1
  54.0 0.0 collective-permute-done.7.two
  54.0 1.6 %collective-permute-done.9.twin = bf16[16,288,128]{2,1,0:T(8,128)(2,1)S(1)} collective-permute-done((bf16[16,288,128]{2,1,0:T(8,128)(2,1)S(1)}, bf16[16,288,128]{2,1,0:T(8,128)(2,1)S(1)}, u32[]{:S(2)}, u32[]{:S(2)}) %collective-permute-start.9) | collective-permute-done | bytes 1179680 | tf_op jit(solution)/shard_map/ppermute | solution.py:436
  55.6 5.3 %attend.1 = bf16[16,160,128]{2,1,0:T(8,128)(2,1)} custom-call(s32[8]{0:T(128)S(1)} %stack.38.meta, s32[1,128]{1,0:T(1,128)S(1)} %slots.1, bf16[16,288,128]{2,1,0:T(8,128)(2,1)S(1)} %all-to-all-done.mine, bf16[16,288,128]{2,1,0:T(8,128)(2,1)S(1)} %collective-permute-done.9.twin, bf16[16,128]{1,0:T(8,128)(2,1)S(1)} %slice.31.after), custom_call_target="tpu_custom_call" | custom-call | flops 1000000000 | bytes 3000000 | tf_op jit(solution)/shard_map/attend/pallas_call | solution.py:441
  61.0 11.6 %all-to-all-start.1 = ((bf16[16,160,128]{2,1,0:T(8,128)(2,1)}), bf16[16,160,128]{2,1,0:T(8,128)(2,1)S(1)}, u32[]{:S(2)}, u32[]{:S(2)}) async-start(bf16[16,160,128]{2,1,0:T(8,128)(2,1)} %attend.1), calls=%async_computation.1 | async-start | bytes 1310720 | tf_op jit(solution)/shard_map/all_to_all | solution.py:450
  72.5 0.0 collective-permute-done.6.one
  72.6 0.1 collective-permute-start.8
  72.7 0.0 copy-done.10
  72.7 0.1 rev.3
  72.8 0.1 pad_convert_fusion.taps
  72.9 1.5 %collective-permute-done.8.rest = bf16[96,2048]{1,0:T(8,128)(2,1)S(1)} collective-permute-done((bf16[96,2048]{1,0:T(8,128)(2,1)S(1)}, bf16[96,2048]{1,0:T(8,128)(2,1)S(1)}, u32[]{:S(2)}, u32[]{:S(2)}) %collective-permute-start.8) | collective-permute-done | bytes 393248 | tf_op jit(solution)/shard_map/ppermute | solution.py:435
  74.4 0.0 copy-done.6
  74.4 1.9 %conv.1 = (bf16[64,2048]{1,0:T(8,128)(2,1)}, bf16[128,2048]{1,0:T(8,128)(2,1)}) custom-call(s32[8]{0:T(128)S(1)} %stack.38.meta, f32[4,256]{1,0:T(4,128)S(1)} %pad_convert_fusion.taps, bf16[64,2048]{1,0:T(8,128)(2,1)S(1)} %get-tuple-element.20.mixed, bf16[64,2048]{1,0:T(8,128)(2,1)S(1)} %copy-done.6, bf16[32,2048]{1,0:T(8,128)(2,1)S(1)} %get-tuple-element.21.keep, ...), custom_call_target="tpu_custom_call" | custom-call | flops 100000000 | bytes 3000000 | tf_op jit(solution)/shard_map/conv/pallas_call | solution.py:462
  76.3 6.5 %all-to-all-done.1.came = bf16[16,160,128]{2,1,0:T(8,128)(2,1)S(1)} async-done(((bf16[16,160,128]{2,1,0:T(8,128)(2,1)}), bf16[16,160,128]{2,1,0:T(8,128)(2,1)S(1)}, u32[]{:S(2)}, u32[]{:S(2)}) %all-to-all-start.1) | async-done | bytes 655392 | tf_op jit(solution)/shard_map/all_to_all | solution.py:450
  82.8 0.8 unpack.1
  83.6 0.1 pad_maximum_fusion
  83.7 1.3 %copy.16 = bf16[128,2,1024]{2,1,0:T(2,128)(2,1)} copy(bf16[128,2,1024]{2,0,1:T(8,128)(2,1)S(1)} %pad_maximum_fusion) | data formatting | bytes 1048576
  (22 shorter events, 0.1 us)
Async XLA Ops:
  0.6 14.1 %copy-start.1 = (bf16[64,2048]{1,0:T(8,128)(2,1)S(1)}, bf16[64,2048]{1,0:T(8,128)(2,1)}, u32[]{:S(2)}) copy-start(bf16[64,2048]{1,0:T(8,128)(2,1)} %pre.5) | copy-start | bytes 786436
  0.6 14.1 %copy-start = (bf16[64,2048]{1,0:T(8,128)(2,1)S(1)}, bf16[64,2048]{1,0:T(8,128)(2,1)}, u32[]{:S(2)}) copy-start(bf16[64,2048]{1,0:T(8,128)(2,1)} %stream.5) | copy-start | bytes 786436
  0.7 14.1 %copy-start.2 = (bf16[64,2048]{1,0:T(8,128)(2,1)S(1)}, bf16[64,2048]{1,0:T(8,128)(2,1)}, u32[]{:S(2)}) copy-start(bf16[64,2048]{1,0:T(8,128)(2,1)} %post.6) | copy-start | bytes 786436
  0.7 14.1 %copy-start.4 = (bf16[2048,7]{0,1:T(8,128)(2,1)S(1)}, bf16[2048,7]{0,1:T(8,128)(2,1)}, u32[]{:S(2)}) copy-start(bf16[2048,7]{0,1:T(8,128)(2,1)} %param.14) | copy-start | bytes 86020
  1.6 23.4 %copy-start.3 = (bf16[64,1024]{1,0:T(8,128)(2,1)S(1)}, bf16[64,1024]{1,0:T(8,128)(2,1)}, u32[]{:S(2)}) copy-start(bf16[64,1024]{1,0:T(8,128)(2,1)} %k.1) | copy-start | bytes 393220
  1.6 23.4 %copy-start.7 = (bf16[64,1024]{1,0:T(8,128)(2,1)S(1)}, bf16[64,1024]{1,0:T(8,128)(2,1)}, u32[]{:S(2)}) copy-start(bf16[64,1024]{1,0:T(8,128)(2,1)} %v.1) | copy-start | bytes 393220
  1.6 23.4 %copy-start.8 = (bf16[64,1024]{1,0:T(8,128)(2,1)S(1)}, bf16[64,1024]{1,0:T(8,128)(2,1)}, u32[]{:S(2)}) copy-start(bf16[64,1024]{1,0:T(8,128)(2,1)} %q.1) | copy-start | bytes 393220
  2.6 16.6 %collective-permute-start = (bf16[96,1024]{1,0:T(8,128)(2,1)S(1)}, bf16[96,1024]{1,0:T(8,128)(2,1)S(1)}, u32[]{:S(2)}, u32[]{:S(2)}) collective-permute-start(bf16[96,1024]{1,0:T(8,128)(2,1)S(1)} %pad_maximum_fusion.2), channel_id=1, source_target_pairs={{0,252},{4,8},{8,4},{12,16},{16,12},{20,24},{24,20},{28,32},{32,28... | collective-permute-start | bytes 589832 | tf_op jit(solution)/shard_map/ppermute | solution.py:27
  9.3 5.4 %collective-permute-start.1 = (bf16[16,2048]{1,0:T(8,128)(2,1)S(1)}, bf16[16,2048]{1,0:T(8,128)(2,1)S(1)}, u32[]{:S(2)}, u32[]{:S(2)}) collective-permute-start(bf16[16,2048]{1,0:T(8,128)(2,1)S(1)} %get-tuple-element.38), channel_id=1, source_target_pairs={{0,4},{4,0},{1,5},{5,1},{2,6},{6,2},{3,7},{7,3},{8,12},{12,8},{9,1... | collective-permute-start | bytes 196616 | tf_op jit(solution)/shard_map/ppermute | solution.py:386
  14.7 10.4 %collective-permute-start.2 = (bf16[64,1024]{1,0:T(8,128)(2,1)}, bf16[64,1024]{1,0:T(8,128)(2,1)S(1)}, u32[]{:S(2)}, u32[]{:S(2)}) collective-permute-start(bf16[64,1024]{1,0:T(8,128)(2,1)} %v.1), channel_id=1, source_target_pairs={{0,252},{4,8},{8,4},{12,16},{16,12},{20,24},{24,20},{28,32},{32,28... | collective-permute-start | bytes 393224 | tf_op jit(solution)/shard_map/ppermute | solution.py:27
  20.8 4.0 %collective-permute-start.3 = (f32[32,128]{1,0:T(8,128)S(1)}, f32[32,128]{1,0:T(8,128)S(1)}, u32[]{:S(2)}, u32[]{:S(2)}) collective-permute-start(f32[32,128]{1,0:T(8,128)S(1)} %head.1), channel_id=1, source_target_pairs={{0,1},{1,0},{2,3},{3,2},{4,5},{5,4},{6,7},{7,6},{8,9},{9,8},{10,11... | collective-permute-start | bytes 49160 | tf_op jit(solution)/shard_map/ppermute | solution.py:409
  26.2 9.4 %copy-start.9 = (s32[128,1]{0,1:T(1,128)S(1)}, s32[128,1]{0,1:T(1,128)}, u32[]{:S(2)}) copy-start(s32[128,1]{0,1:T(1,128)} %param.21) | copy-start | bytes 1540
  26.2 10.7 %copy-start.5 = (bf16[64,2048]{1,0:T(8,128)(2,1)S(1)}, bf16[64,2048]{1,0:T(8,128)(2,1)}, u32[]{:S(2)}) copy-start(bf16[64,2048]{1,0:T(8,128)(2,1)} %mrpre.1) | copy-start | bytes 786436
  26.2 24.6 %all-to-all-start = ((bf16[16,288,128]{2,1,0:T(8,128)(2,1)}), bf16[16,288,128]{2,1,0:T(8,128)(2,1)S(1)}, u32[]{:S(2)}, u32[]{:S(2)}) async-start(bf16[16,288,128]{2,1,0:T(8,128)(2,1)} %pack.1), calls=%async_computation | async-start | bytes 2359296 | tf_op jit(solution)/shard_map/all_to_all | solution.py:428
  33.4 3.6 %collective-permute-start.4 = (f32[32,128]{1,0:T(8,128)S(1)}, f32[32,128]{1,0:T(8,128)S(1)}, u32[]{:S(2)}, u32[]{:S(2)}) collective-permute-start(f32[32,128]{1,0:T(8,128)S(1)} %add.23.half), channel_id=1, source_target_pairs={{0,2},{1,3},{2,0},{3,1},{4,6},{5,7},{6,4},{7,5},{8,10},{9,11},{10,... | collective-permute-start | bytes 49160 | tf_op jit(solution)/shard_map/ppermute | solution.py:411
  38.6 4.3 %collective-permute-start.5 = (bf16[32,2048]{1,0:T(8,128)(2,1)S(1)}, bf16[32,2048]{1,0:T(8,128)(2,1)S(1)}, u32[]{:S(2)}, u32[]{:S(2)}) collective-permute-start(bf16[32,2048]{1,0:T(8,128)(2,1)S(1)} %get-tuple-element.22.give), channel_id=1, source_target_pairs={{0,4},{4,0},{1,5},{5,1},{2,6},{6,2},{3,7},{7,3},{8,12},{12,8},{9,1... | collective-permute-start | bytes 393224 | tf_op jit(solution)/shard_map/ppermute | solution.py:423
  42.9 11.0 %collective-permute-start.7 = (bf16[64,2048]{1,0:T(8,128)(2,1)S(1)}, bf16[64,2048]{1,0:T(8,128)(2,1)S(1)}, u32[]{:S(2)}, u32[]{:S(2)}) collective-permute-start(bf16[64,2048]{1,0:T(8,128)(2,1)S(1)} %constant_dynamic-update-slice_fusion), channel_id=1, source_target_pairs={{4,16},{12,24},{16,4},{20,32},{24,12},{28,40},{32,20},{36,48},{40,... | collective-permute-start | bytes 786440 | tf_op jit(solution)/shard_map/ppermute | solution.py:27
  46.6 25.9 %collective-permute-start.6 = (bf16[64,2048]{1,0:T(8,128)(2,1)S(1)}, bf16[64,2048]{1,0:T(8,128)(2,1)S(1)}, u32[]{:S(2)}, u32[]{:S(2)}) collective-permute-start(bf16[64,2048]{1,0:T(8,128)(2,1)S(1)} %constant_dynamic-update-slice_fusion), channel_id=1, source_target_pairs={{4,8},{8,4},{12,16},{16,12},{20,24},{24,20},{28,32},{32,28},{36,40... | collective-permute-start | bytes 786440 | tf_op jit(solution)/shard_map/ppermute | solution.py:27
  50.8 4.8 %collective-permute-start.9 = (bf16[16,288,128]{2,1,0:T(8,128)(2,1)S(1)}, bf16[16,288,128]{2,1,0:T(8,128)(2,1)S(1)}, u32[]{:S(2)}, u32[]{:S(2)}) collective-permute-start(bf16[16,288,128]{2,1,0:T(8,128)(2,1)S(1)} %all-to-all-done.mine), channel_id=1, source_target_pairs={{0,4},{4,0},{1,5},{5,1},{2,6},{6,2},{3,7},{7,3},{8,12},{12,8},{9,1... | collective-permute-start | bytes 3538952 | tf_op jit(solution)/shard_map/ppermute | solution.py:436
  61.0 11.7 %copy-start.10 = (bf16[4,128]{1,0:T(4,128)(2,1)S(1)}, bf16[4,128]{1,0:T(4,128)(2,1)}, u32[]{:S(2)}) copy-start(bf16[4,128]{1,0:T(4,128)(2,1)} %param.17) | copy-start | bytes 3076
  61.0 13.4 %copy-start.6 = (bf16[64,2048]{1,0:T(8,128)(2,1)S(1)}, bf16[64,2048]{1,0:T(8,128)(2,1)}, u32[]{:S(2)}) copy-start(bf16[64,2048]{1,0:T(8,128)(2,1)} %post.7) | copy-start | bytes 786436
  61.0 21.8 %all-to-all-start.1 = ((bf16[16,160,128]{2,1,0:T(8,128)(2,1)}), bf16[16,160,128]{2,1,0:T(8,128)(2,1)S(1)}, u32[]{:S(2)}, u32[]{:S(2)}) async-start(bf16[16,160,128]{2,1,0:T(8,128)(2,1)} %attend.1), calls=%async_computation.1 | async-start | bytes 1310720 | tf_op jit(solution)/shard_map/all_to_all | solution.py:450
  72.6 1.8 %collective-permute-start.8 = (bf16[96,2048]{1,0:T(8,128)(2,1)S(1)}, bf16[96,2048]{1,0:T(8,128)(2,1)S(1)}, u32[]{:S(2)}, u32[]{:S(2)}) collective-permute-start(bf16[96,2048]{1,0:T(8,128)(2,1)S(1)} %pad_maximum_fusion.1), channel_id=1, source_target_pairs={{0,4},{4,0},{1,5},{5,1},{2,6},{6,2},{3,7},{7,3},{8,12},{12,8},{9,1... | collective-permute-start | bytes 1179656 | tf_op jit(solution)/shard_map/ppermute | solution.py:435

commit v4 on v3

--- a/solution.py
+++ b/solution.py
@@ -268,7 +268,16 @@
     rank = jnp.sum(jnp.where(before, 1, 0), axis=1, keepdims=True)
     want = (col // 2 * 4 + zh * 2 + c) * CAP + xb * 2 + col % 2
     found = (mine * CAP + rank == want) & (col < 32)
-    out[...] = jnp.sum(jnp.where(found, row + 1, 0), axis=0, keepdims=True) - 1
+    tile = jnp.sum(jnp.where(found, row + 1, 0), axis=0, keepdims=True) - 1
+    held = jnp.maximum(tile, 0)
+    late = held >= 64
+    device = jnp.where(late, 127 - held, held)
+    across_z = (device >> 1 & 1) != zh
+    holder = jnp.where(across_z, (device + jnp.where(device & 1 == 1, 1, 63)) & 63, device)
+    out[0:1, :] = holder >> 2
+    out[1:2, :] = jnp.where(across_z, 128, 0) + jnp.where(late, TILE, 0)
+    out[2:3, :] = jnp.where((holder & 1) == c, 1, 0)
+    out[3:4, :] = jnp.where(tile >= 0, 1, 0)
 
 
 def attend_kernel(meta, slots, mine, twin, after, out, scores):
@@ -276,24 +285,18 @@
 
     def pieces(n, carry):
         for slot in range(2):
-            tile = slots[0, n * 2 + slot]
-            held = jnp.maximum(tile, 0)
-            late = (held >= 64).astype(jnp.int32)
-            device = jnp.where(held >= 64, 127 - held, held)
-            across_z = (device // 2) % 2 != zh
-            holder = jnp.where(device % 2 == 1, device + 1, device + 63) % 64
-            holder = jnp.where(across_z, holder, device)
-            src, cd = holder // 4, holder % 2
-            low = jnp.where(across_z, 128, 0) + late * TILE
+            at = n * 2 + slot
+            src, low = slots[0, at], slots[1, at]
+            near, there = slots[2, at] == 1, slots[3, at] == 1
             for kv in range(2):
                 rows = pl.ds(pl.multiple_of(low + 64 * kv, TILE), TILE)
-                value = jnp.where(cd == c, mine[src, rows, :], twin[src, rows, :])
-                value = jnp.where(tile >= 0, value, jnp.zeros_like(value))
+                value = jnp.where(near, mine[src, rows, :], twin[src, rows, :])
+                value = jnp.where(there, value, jnp.zeros_like(value))
                 first = 32 + (slot * 2 + kv) * TILE
                 out[n, first : first + TILE, :] = value
         return carry
 
-    lax.fori_loop(0, 16, pieces, 0, unroll=4)
+    lax.fori_loop(0, 16, pieces, 0, unroll=16)
     log_scale = math.log2(math.e) / math.sqrt(HEAD_DIM)
     def owner(core, far):
         def of(src):
@@ -415,7 +418,7 @@
         [pltpu.VMEM((2, 40, LANES), F32), pltpu.VMEM((64, LANES), F32), pltpu.VMEM((2, 40, LANES), F32)]
         + [pltpu.VMEM((8, channels), F32)],
         [S] + [V] * 9,
-        flops=8_000_000,
+        flops=20_000_000_000,
         nbytes=3_500_000,
         name="mix",
     )(meta, stream, se_pre, se_post, mr_pre, taps, far, halo_near, half, other)
@@ -436,7 +439,7 @@
     twin = lax.ppermute(mine, "c", [(0, 1), (1, 0)])
 
     slots = call(
-        slots_kernel, shape((1, 128), jnp.int32), (), [S, V, V], flops=20_000_000_000, nbytes=70_000, name="slots"
+        slots_kernel, shape((4, 128), jnp.int32), (), [S, V, V], flops=20_000_000_000, nbytes=70_000, name="slots"
     )(meta, owner.reshape(1, 128), owner)
     answered = call(
         attend_kernel,

time: 85.3 us -> 83.6 us (0.980)
  the two profiles are of different devices: /device:TPU:33 before, /device:TPU:224 now
where the time goes in v4:
time: 83.6 us; the launch traced here: 83.3 us
  starting transfers between devices  34.1 us (41%)
  waiting for transfers between devices  29.2 us (35%)
  Pallas kernels  15.2 us (18%)
  local copies, waits for them, and re-layouts  2.6 us (3%)
  other arithmetic  1.15 us (1%)
  between operations  0.91 us (1%)
    ppermute x4, starting transfers between devices, ctx_route(): return lax.ppermute(array, CTX, pairs)  14.6 us
    all_to_all x1, waiting for transfers between devices, body(): mine = lax.all_to_all(heads, ('x', 'y'), 0, 0, tiled=True)  10.9 us
    all_to_all x1, starting transfers between devices, body(): mine = lax.all_to_all(heads, ('x', 'y'), 0, 0, tiled=True)  10.6 us
    all_to_all x1, waiting for transfers between devices, body(): came = lax.all_to_all(answered, ('x', 'y'), 0, 0, tiled=True)  10.2 us
    pallas_call x1, Pallas kernels, body(): call(attend_kernel, shape((16, 160, LANES)), [pltpu.VMEM((128, 4096), F32...  4.65 us
    all_to_all x1, starting transfers between devices, body(): came = lax.all_to_all(answered, ('x', 'y'), 0, 0, tiled=True)  3.74 us
    ppermute x1, waiting for transfers between devices, body(): half = sums + lax.ppermute(sums, 'tp', [(i, i ^ 1) for i in range(4)])  2.98 us
    pallas_call x1, Pallas kernels, body(): call(stats_kernel, shape((TILE, LANES), F32), [pltpu.VMEM((rows, channels...  2.57 us
  transfers between devices with their start and end apart: 12, of which 7 were waited for; matrix products, arithmetic and copies ran while one was open for 1% of the time, Pallas kernels for 17%

profile of v4, /device:TPU:224, one launch (start us, length us, event | category | flops | bytes accessed | tf_op | source)
XLA Modules:
  0.0 83.3 jit_solution(7770500158460019393)
XLA Ops:
  0.6 0.0 copy-start.1
  0.6 0.0 copy-start
  0.7 0.9 %fusion = (bf16[8,2048]{1,0:T(8,128)(2,1)S(1)}, bf16[8,2048]{1,0:T(8,128)(2,1)S(1)}, bf16[8,2048]{1,0:T(8,128)(2,1)S(1)}, bf16[8,2048]{1,0:T(8,128)(2,1)S(1)}) fusion(bf16[64,2048]{1,0:T(8,128)(2,1)} %stream.5, bf16[64,2048]{1,0:T(8,128)(2,1)} %pre.5), kind=kLoop, calls=%fused_computation.10 | loop fusion | bytes 262144 | tf_op jit(solution)/shard_map/slice | solution.py:386
  1.6 0.0 copy-start.8
  1.6 0.0 copy-start.3
  1.6 0.0 copy-start.6
  1.6 0.0 copy-start.7
  1.7 1.0 %pad_maximum_fusion.2 = bf16[96,1024]{1,0:T(8,128)(2,1)S(1)} fusion(bf16[16,1024]{1,0:T(8,128)(2,1)S(1)} %get-tuple-element.41, bf16[16,1024]{1,0:T(8,128)(2,1)S(1)} %get-tuple-element.40, bf16[64,1024]{1,0:T(8,128)(2,1)} %k.1), kind=kLoop, calls=%fused_computation.2 | loop fusion | flops 589824 | bytes 393216 | tf_op jit(solution)/shard_map/concatenate | solution.py:390
  2.6 1.0 %collective-permute-start = (bf16[96,1024]{1,0:T(8,128)(2,1)S(1)}, bf16[96,1024]{1,0:T(8,128)(2,1)S(1)}, u32[]{:S(2)}, u32[]{:S(2)}) collective-permute-start(bf16[96,1024]{1,0:T(8,128)(2,1)S(1)} %pad_maximum_fusion.2), channel_id=1, source_target_pairs={{0,252},{4,8},{8,4},{12,16},{16,12},{20,24},{24,20},{28,32},{32,28... | collective-permute-start | bytes 589832 | tf_op jit(solution)/shard_map/ppermute | solution.py:27
  3.6 1.7 %collective-permute-start.1 = (bf16[16,2048]{1,0:T(8,128)(2,1)S(1)}, bf16[16,2048]{1,0:T(8,128)(2,1)S(1)}, u32[]{:S(2)}, u32[]{:S(2)}) collective-permute-start(bf16[16,2048]{1,0:T(8,128)(2,1)S(1)} %get-tuple-element.38), channel_id=1, source_target_pairs={{0,4},{4,0},{1,5},{5,1},{2,6},{6,2},{3,7},{7,3},{8,12},{12,8},{9,1... | collective-permute-start | bytes 196616 | tf_op jit(solution)/shard_map/ppermute | solution.py:389
  5.3 0.9 %collective-permute-done.1.near.hl = bf16[16,2048]{1,0:T(8,128)(2,1)S(1)} collective-permute-done((bf16[16,2048]{1,0:T(8,128)(2,1)S(1)}, bf16[16,2048]{1,0:T(8,128)(2,1)S(1)}, u32[]{:S(2)}, u32[]{:S(2)}) %collective-permute-start.1) | collective-permute-done | bytes 65568 | tf_op jit(solution)/shard_map/ppermute | solution.py:389
  6.2 7.6 %collective-permute-start.2 = (bf16[64,1024]{1,0:T(8,128)(2,1)}, bf16[64,1024]{1,0:T(8,128)(2,1)S(1)}, u32[]{:S(2)}, u32[]{:S(2)}) collective-permute-start(bf16[64,1024]{1,0:T(8,128)(2,1)} %v.1), channel_id=1, source_target_pairs={{0,252},{4,8},{8,4},{12,16},{16,12},{20,24},{24,20},{28,32},{32,28... | collective-permute-start | bytes 393224 | tf_op jit(solution)/shard_map/ppermute | solution.py:27
  13.8 0.1 stack.38.meta
  13.8 0.0 copy-done.1
  13.9 2.6 %stats.1.partial = f32[32,128]{1,0:T(8,128)S(1)} custom-call(bf16[64,2048]{1,0:T(8,128)(2,1)S(1)} %copy-done, bf16[64,2048]{1,0:T(8,128)(2,1)S(1)} %copy-done.1, bf16[64,2048]{1,0:T(8,128)(2,1)S(1)} %copy-done.2, bf16[7,2048]{1,0:T(8,128)(2,1)S(1)} %bitcast.12), custom_call_target="tpu_custom_call" | custom-call | flops 15000000 | bytes 800000 | tf_op jit(solution)/shard_map/stats/pallas_call | solution.py:394
  16.4 0.0 collective-permute-done.far.he
  16.4 1.6 %head.1 = f32[32,128]{1,0:T(8,128)S(1)} custom-call(s32[8]{0:T(128)S(1)} %stack.38.meta, bf16[64,2048]{1,0:T(8,128)(2,1)S(1)} %copy-done, bf16[64,2048]{1,0:T(8,128)(2,1)S(1)} %copy-done.1, bf16[64,2048]{1,0:T(8,128)(2,1)S(1)} %copy-done.2, bf16[7,2048]{1,0:T(8,128)(2,1)S(1)} %bitcast.13, bf16[96,1024]{1,0:T(8,128)(2,1)S(1)} %collective-permute-done.far.he, ...), custom_call_target="tpu_custom_call" | custom-call | flops 5000000 | bytes 300000 | tf_op jit(solution)/shard_map/head/pallas_call | solution.py:403
  18.1 1.1 %collective-permute-start.3 = (f32[32,128]{1,0:T(8,128)S(1)}, f32[32,128]{1,0:T(8,128)S(1)}, u32[]{:S(2)}, u32[]{:S(2)}) collective-permute-start(f32[32,128]{1,0:T(8,128)S(1)} %head.1), channel_id=1, source_target_pairs={{0,1},{1,0},{2,3},{3,2},{4,5},{5,4},{6,7},{7,6},{8,9},{9,8},{10,11... | collective-permute-start | bytes 49160 | tf_op jit(solution)/shard_map/ppermute | solution.py:412
  19.2 3.0 %collective-permute-done.3 = f32[32,128]{1,0:T(8,128)S(1)} collective-permute-done((f32[32,128]{1,0:T(8,128)S(1)}, f32[32,128]{1,0:T(8,128)S(1)}, u32[]{:S(2)}, u32[]{:S(2)}) %collective-permute-start.3) | collective-permute-done | bytes 16416 | tf_op jit(solution)/shard_map/ppermute | solution.py:412
  22.2 0.0 collective-permute-done.2.far_values
  22.2 1.3 %collective-permute-start.4 = (f32[32,128]{1,0:T(8,128)S(1)}, f32[32,128]{1,0:T(8,128)S(1)}, u32[]{:S(2)}, u32[]{:S(2)}) collective-permute-start(f32[32,128]{1,0:T(8,128)S(1)} %add.23.half), channel_id=1, source_target_pairs={{0,2},{1,3},{2,0},{3,1},{4,6},{5,7},{6,4},{7,5},{8,10},{9,11},{10,... | collective-permute-start | bytes 49160 | tf_op jit(solution)/shard_map/ppermute | solution.py:414
  23.5 0.0 copy-done.8
  23.5 0.1 copy.15.owner_col
  23.6 1.2 %pack.1 = bf16[16,288,128]{2,1,0:T(8,128)(2,1)} custom-call(bf16[64,1024]{1,0:T(8,128)(2,1)S(1)} %copy-done.3, bf16[64,1024]{1,0:T(8,128)(2,1)S(1)} %copy-done.6, bf16[96,1024]{1,0:T(8,128)(2,1)S(1)} %collective-permute-done.far.he, bf16[64,1024]{1,0:T(8,128)(2,1)S(1)} %collective-permute-done.2.far_values, bf16[64,1024]{1,0:T(8,128)(2,1)S(1)} %copy-done.7), custom_call_target="tpu_custom_call" | custom-call | bytes 2000000 | tf_op jit(solution)/shard_map/pack/pallas_call | solution.py:428
  24.8 10.6 %all-to-all-start = ((bf16[16,288,128]{2,1,0:T(8,128)(2,1)}), bf16[16,288,128]{2,1,0:T(8,128)(2,1)S(1)}, u32[]{:S(2)}, u32[]{:S(2)}) async-start(bf16[16,288,128]{2,1,0:T(8,128)(2,1)} %pack.1), calls=%async_computation | async-start | bytes 2359296 | tf_op jit(solution)/shard_map/all_to_all | solution.py:431
  35.4 0.0 collective-permute-done.4.other
  35.4 1.7 %mix.1 = (bf16[64,2048]{1,0:T(8,128)(2,1)S(1)}, bf16[32,2048]{1,0:T(8,128)(2,1)S(1)}, bf16[32,2048]{1,0:T(8,128)(2,1)S(1)}) custom-call(s32[8]{0:T(128)S(1)} %stack.38.meta, bf16[64,2048]{1,0:T(8,128)(2,1)S(1)} %copy-done, bf16[64,2048]{1,0:T(8,128)(2,1)S(1)} %copy-done.1, bf16[64,2048]{1,0:T(8,128)(2,1)S(1)} %copy-done.2, bf16[64,2048]{1,0:T(8,128)(2,1)S(1)} %copy-done.9, ...), custom_call_target="tpu_custom_call" | custom-call | flops 20000000000 | bytes 3500000 | tf_op jit(solution)/shard_map/mix/pallas_call | solution.py:415
  37.1 0.4 collective-permute-start.5
  37.5 1.1 %collective-permute-done.5.got = bf16[32,2048]{1,0:T(8,128)(2,1)S(1)} collective-permute-done((bf16[32,2048]{1,0:T(8,128)(2,1)S(1)}, bf16[32,2048]{1,0:T(8,128)(2,1)S(1)}, u32[]{:S(2)}, u32[]{:S(2)}) %collective-permute-start.5) | collective-permute-done | bytes 131104 | tf_op jit(solution)/shard_map/ppermute | solution.py:426
  38.6 0.7 collective-permute-start.7
  39.3 5.4 %collective-permute-start.6 = (bf16[64,2048]{1,0:T(8,128)(2,1)S(1)}, bf16[64,2048]{1,0:T(8,128)(2,1)S(1)}, u32[]{:S(2)}, u32[]{:S(2)}) collective-permute-start(bf16[64,2048]{1,0:T(8,128)(2,1)S(1)} %constant_dynamic-update-slice_fusion), channel_id=1, source_target_pairs={{4,8},{8,4},{12,16},{16,12},{20,24},{24,20},{28,32},{32,28},{36,40... | collective-permute-start | bytes 786440 | tf_op jit(solution)/shard_map/ppermute | solution.py:27
  44.7 10.9 %all-to-all-done.mine = bf16[16,288,128]{2,1,0:T(8,128)(2,1)S(1)} async-done(((bf16[16,288,128]{2,1,0:T(8,128)(2,1)}), bf16[16,288,128]{2,1,0:T(8,128)(2,1)S(1)}, u32[]{:S(2)}, u32[]{:S(2)}) %all-to-all-start) | async-done | bytes 1179680 | tf_op jit(solution)/shard_map/all_to_all | solution.py:431
  55.6 0.0 collective-permute-start.9
  55.6 0.8 slots.1
  56.5 0.0 collective-permute-done.7.two
  56.5 2.0 %collective-permute-done.9.twin = bf16[16,288,128]{2,1,0:T(8,128)(2,1)S(1)} collective-permute-done((bf16[16,288,128]{2,1,0:T(8,128)(2,1)S(1)}, bf16[16,288,128]{2,1,0:T(8,128)(2,1)S(1)}, u32[]{:S(2)}, u32[]{:S(2)}) %collective-permute-start.9) | collective-permute-done | bytes 1179680 | tf_op jit(solution)/shard_map/ppermute | solution.py:439
  58.5 4.7 %attend.1 = bf16[16,160,128]{2,1,0:T(8,128)(2,1)} custom-call(s32[8]{0:T(128)S(1)} %stack.38.meta, s32[4,128]{1,0:T(4,128)S(1)} %slots.1, bf16[16,288,128]{2,1,0:T(8,128)(2,1)S(1)} %all-to-all-done.mine, bf16[16,288,128]{2,1,0:T(8,128)(2,1)S(1)} %collective-permute-done.9.twin, bf16[16,128]{1,0:T(8,128)(2,1)S(1)} %slice.31.after), custom_call_target="tpu_custom_call" | custom-call | flops 1000000000 | bytes 3000000 | tf_op jit(solution)/shard_map/attend/pallas_call | solution.py:444
  63.1 3.7 %all-to-all-start.1 = ((bf16[16,160,128]{2,1,0:T(8,128)(2,1)}), bf16[16,160,128]{2,1,0:T(8,128)(2,1)S(1)}, u32[]{:S(2)}, u32[]{:S(2)}) async-start(bf16[16,160,128]{2,1,0:T(8,128)(2,1)} %attend.1), calls=%async_computation.1 | async-start | bytes 1310720 | tf_op jit(solution)/shard_map/all_to_all | solution.py:453
  66.9 0.0 collective-permute-done.6.one
  66.9 0.7 collective-permute-start.8
  67.7 0.1 rev.3
  67.8 0.1 pad_convert_fusion.taps
  67.8 1.2 %collective-permute-done.8.rest = bf16[96,2048]{1,0:T(8,128)(2,1)S(1)} collective-permute-done((bf16[96,2048]{1,0:T(8,128)(2,1)S(1)}, bf16[96,2048]{1,0:T(8,128)(2,1)S(1)}, u32[]{:S(2)}, u32[]{:S(2)}) %collective-permute-start.8) | collective-permute-done | bytes 393248 | tf_op jit(solution)/shard_map/ppermute | solution.py:438
  69.0 1.9 %conv.1 = (bf16[64,2048]{1,0:T(8,128)(2,1)}, bf16[128,2048]{1,0:T(8,128)(2,1)}) custom-call(s32[8]{0:T(128)S(1)} %stack.38.meta, f32[4,256]{1,0:T(4,128)S(1)} %pad_convert_fusion.taps, bf16[64,2048]{1,0:T(8,128)(2,1)S(1)} %get-tuple-element.20.mixed, bf16[64,2048]{1,0:T(8,128)(2,1)S(1)} %copy-done.4, bf16[32,2048]{1,0:T(8,128)(2,1)S(1)} %get-tuple-element.21.keep, ...), custom_call_target="tpu_custom_call" | custom-call | flops 100000000 | bytes 3000000 | tf_op jit(solution)/shard_map/conv/pallas_call | solution.py:465
  70.9 10.2 %all-to-all-done.1.came = bf16[16,160,128]{2,1,0:T(8,128)(2,1)S(1)} async-done(((bf16[16,160,128]{2,1,0:T(8,128)(2,1)}), bf16[16,160,128]{2,1,0:T(8,128)(2,1)S(1)}, u32[]{:S(2)}, u32[]{:S(2)}) %all-to-all-start.1) | async-done | bytes 655392 | tf_op jit(solution)/shard_map/all_to_all | solution.py:453
  81.1 0.8 unpack.1
  81.9 0.1 pad_maximum_fusion
  81.9 1.3 %copy.16 = bf16[128,2,1024]{2,1,0:T(2,128)(2,1)} copy(bf16[128,2,1024]{2,0,1:T(8,128)(2,1)S(1)} %pad_maximum_fusion) | data formatting | bytes 1048576
  (22 shorter events, 0.1 us)
Async XLA Ops:
  0.6 13.2 %copy-start.1 = (bf16[64,2048]{1,0:T(8,128)(2,1)S(1)}, bf16[64,2048]{1,0:T(8,128)(2,1)}, u32[]{:S(2)}) copy-start(bf16[64,2048]{1,0:T(8,128)(2,1)} %pre.5) | copy-start | bytes 786436
  0.6 13.2 %copy-start = (bf16[64,2048]{1,0:T(8,128)(2,1)S(1)}, bf16[64,2048]{1,0:T(8,128)(2,1)}, u32[]{:S(2)}) copy-start(bf16[64,2048]{1,0:T(8,128)(2,1)} %stream.5) | copy-start | bytes 786436
  0.7 13.2 %copy-start.2 = (bf16[64,2048]{1,0:T(8,128)(2,1)S(1)}, bf16[64,2048]{1,0:T(8,128)(2,1)}, u32[]{:S(2)}) copy-start(bf16[64,2048]{1,0:T(8,128)(2,1)} %post.6) | copy-start | bytes 786436
  0.7 13.2 %copy-start.5 = (bf16[2048,7]{0,1:T(8,128)(2,1)S(1)}, bf16[2048,7]{0,1:T(8,128)(2,1)}, u32[]{:S(2)}) copy-start(bf16[2048,7]{0,1:T(8,128)(2,1)} %param.14) | copy-start | bytes 86020
  1.6 21.9 %copy-start.8 = (s32[128,1]{0,1:T(1,128)S(1)}, s32[128,1]{0,1:T(1,128)}, u32[]{:S(2)}) copy-start(s32[128,1]{0,1:T(1,128)} %param.21) | copy-start | bytes 1540
  1.6 22.0 %copy-start.3 = (bf16[64,1024]{1,0:T(8,128)(2,1)S(1)}, bf16[64,1024]{1,0:T(8,128)(2,1)}, u32[]{:S(2)}) copy-start(bf16[64,1024]{1,0:T(8,128)(2,1)} %k.1) | copy-start | bytes 393220
  1.6 22.0 %copy-start.6 = (bf16[64,1024]{1,0:T(8,128)(2,1)S(1)}, bf16[64,1024]{1,0:T(8,128)(2,1)}, u32[]{:S(2)}) copy-start(bf16[64,1024]{1,0:T(8,128)(2,1)} %v.1) | copy-start | bytes 393220
  1.6 21.9 %copy-start.7 = (bf16[64,1024]{1,0:T(8,128)(2,1)S(1)}, bf16[64,1024]{1,0:T(8,128)(2,1)}, u32[]{:S(2)}) copy-start(bf16[64,1024]{1,0:T(8,128)(2,1)} %q.1) | copy-start | bytes 393220
  2.6 13.8 %collective-permute-start = (bf16[96,1024]{1,0:T(8,128)(2,1)S(1)}, bf16[96,1024]{1,0:T(8,128)(2,1)S(1)}, u32[]{:S(2)}, u32[]{:S(2)}) collective-permute-start(bf16[96,1024]{1,0:T(8,128)(2,1)S(1)} %pad_maximum_fusion.2), channel_id=1, source_target_pairs={{0,252},{4,8},{8,4},{12,16},{16,12},{20,24},{24,20},{28,32},{32,28... | collective-permute-start | bytes 589832 | tf_op jit(solution)/shard_map/ppermute | solution.py:27
  3.6 2.6 %collective-permute-start.1 = (bf16[16,2048]{1,0:T(8,128)(2,1)S(1)}, bf16[16,2048]{1,0:T(8,128)(2,1)S(1)}, u32[]{:S(2)}, u32[]{:S(2)}) collective-permute-start(bf16[16,2048]{1,0:T(8,128)(2,1)S(1)} %get-tuple-element.38), channel_id=1, source_target_pairs={{0,4},{4,0},{1,5},{5,1},{2,6},{6,2},{3,7},{7,3},{8,12},{12,8},{9,1... | collective-permute-start | bytes 196616 | tf_op jit(solution)/shard_map/ppermute | solution.py:389
  6.2 16.0 %collective-permute-start.2 = (bf16[64,1024]{1,0:T(8,128)(2,1)}, bf16[64,1024]{1,0:T(8,128)(2,1)S(1)}, u32[]{:S(2)}, u32[]{:S(2)}) collective-permute-start(bf16[64,1024]{1,0:T(8,128)(2,1)} %v.1), channel_id=1, source_target_pairs={{0,252},{4,8},{8,4},{12,16},{16,12},{20,24},{24,20},{28,32},{32,28... | collective-permute-start | bytes 393224 | tf_op jit(solution)/shard_map/ppermute | solution.py:27
  18.1 4.1 %collective-permute-start.3 = (f32[32,128]{1,0:T(8,128)S(1)}, f32[32,128]{1,0:T(8,128)S(1)}, u32[]{:S(2)}, u32[]{:S(2)}) collective-permute-start(f32[32,128]{1,0:T(8,128)S(1)} %head.1), channel_id=1, source_target_pairs={{0,1},{1,0},{2,3},{3,2},{4,5},{5,4},{6,7},{7,6},{8,9},{9,8},{10,11... | collective-permute-start | bytes 49160 | tf_op jit(solution)/shard_map/ppermute | solution.py:412
  22.2 13.2 %collective-permute-start.4 = (f32[32,128]{1,0:T(8,128)S(1)}, f32[32,128]{1,0:T(8,128)S(1)}, u32[]{:S(2)}, u32[]{:S(2)}) collective-permute-start(f32[32,128]{1,0:T(8,128)S(1)} %add.23.half), channel_id=1, source_target_pairs={{0,2},{1,3},{2,0},{3,1},{4,6},{5,7},{6,4},{7,5},{8,10},{9,11},{10,... | collective-permute-start | bytes 49160 | tf_op jit(solution)/shard_map/ppermute | solution.py:414
  24.8 10.6 %copy-start.9 = (bf16[64,2048]{1,0:T(8,128)(2,1)S(1)}, bf16[64,2048]{1,0:T(8,128)(2,1)}, u32[]{:S(2)}) copy-start(bf16[64,2048]{1,0:T(8,128)(2,1)} %mrpre.1) | copy-start | bytes 786436
  24.8 30.8 %all-to-all-start = ((bf16[16,288,128]{2,1,0:T(8,128)(2,1)}), bf16[16,288,128]{2,1,0:T(8,128)(2,1)S(1)}, u32[]{:S(2)}, u32[]{:S(2)}) async-start(bf16[16,288,128]{2,1,0:T(8,128)(2,1)} %pack.1), calls=%async_computation | async-start | bytes 2359296 | tf_op jit(solution)/shard_map/all_to_all | solution.py:431
  37.1 1.4 %collective-permute-start.5 = (bf16[32,2048]{1,0:T(8,128)(2,1)S(1)}, bf16[32,2048]{1,0:T(8,128)(2,1)S(1)}, u32[]{:S(2)}, u32[]{:S(2)}) collective-permute-start(bf16[32,2048]{1,0:T(8,128)(2,1)S(1)} %get-tuple-element.22.give), channel_id=1, source_target_pairs={{0,4},{4,0},{1,5},{5,1},{2,6},{6,2},{3,7},{7,3},{8,12},{12,8},{9,1... | collective-permute-start | bytes 393224 | tf_op jit(solution)/shard_map/ppermute | solution.py:426
  38.6 17.9 %collective-permute-start.7 = (bf16[64,2048]{1,0:T(8,128)(2,1)S(1)}, bf16[64,2048]{1,0:T(8,128)(2,1)S(1)}, u32[]{:S(2)}, u32[]{:S(2)}) collective-permute-start(bf16[64,2048]{1,0:T(8,128)(2,1)S(1)} %constant_dynamic-update-slice_fusion), channel_id=1, source_target_pairs={{4,16},{12,24},{16,4},{20,32},{24,12},{28,40},{32,20},{36,48},{40,... | collective-permute-start | bytes 786440 | tf_op jit(solution)/shard_map/ppermute | solution.py:27
  39.3 27.6 %collective-permute-start.6 = (bf16[64,2048]{1,0:T(8,128)(2,1)S(1)}, bf16[64,2048]{1,0:T(8,128)(2,1)S(1)}, u32[]{:S(2)}, u32[]{:S(2)}) collective-permute-start(bf16[64,2048]{1,0:T(8,128)(2,1)S(1)} %constant_dynamic-update-slice_fusion), channel_id=1, source_target_pairs={{4,8},{8,4},{12,16},{16,12},{20,24},{24,20},{28,32},{32,28},{36,40... | collective-permute-start | bytes 786440 | tf_op jit(solution)/shard_map/ppermute | solution.py:27
  55.6 2.8 %collective-permute-start.9 = (bf16[16,288,128]{2,1,0:T(8,128)(2,1)S(1)}, bf16[16,288,128]{2,1,0:T(8,128)(2,1)S(1)}, u32[]{:S(2)}, u32[]{:S(2)}) collective-permute-start(bf16[16,288,128]{2,1,0:T(8,128)(2,1)S(1)} %all-to-all-done.mine), channel_id=1, source_target_pairs={{0,4},{4,0},{1,5},{5,1},{2,6},{6,2},{3,7},{7,3},{8,12},{12,8},{9,1... | collective-permute-start | bytes 3538952 | tf_op jit(solution)/shard_map/ppermute | solution.py:439
  63.1 4.5 %copy-start.10 = (bf16[4,128]{1,0:T(4,128)(2,1)S(1)}, bf16[4,128]{1,0:T(4,128)(2,1)}, u32[]{:S(2)}) copy-start(bf16[4,128]{1,0:T(4,128)(2,1)} %param.17) | copy-start | bytes 3076
  63.1 5.9 %copy-start.4 = (bf16[64,2048]{1,0:T(8,128)(2,1)S(1)}, bf16[64,2048]{1,0:T(8,128)(2,1)}, u32[]{:S(2)}) copy-start(bf16[64,2048]{1,0:T(8,128)(2,1)} %post.7) | copy-start | bytes 786436
  63.1 17.9 %all-to-all-start.1 = ((bf16[16,160,128]{2,1,0:T(8,128)(2,1)}), bf16[16,160,128]{2,1,0:T(8,128)(2,1)S(1)}, u32[]{:S(2)}, u32[]{:S(2)}) async-start(bf16[16,160,128]{2,1,0:T(8,128)(2,1)} %attend.1), calls=%async_computation.1 | async-start | bytes 1310720 | tf_op jit(solution)/shard_map/all_to_all | solution.py:453
  66.9 2.1 %collective-permute-start.8 = (bf16[96,2048]{1,0:T(8,128)(2,1)S(1)}, bf16[96,2048]{1,0:T(8,128)(2,1)S(1)}, u32[]{:S(2)}, u32[]{:S(2)}) collective-permute-start(bf16[96,2048]{1,0:T(8,128)(2,1)S(1)} %pad_maximum_fusion.1), channel_id=1, source_target_pairs={{0,4},{4,0},{1,5},{5,1},{2,6},{6,2},{3,7},{7,3},{8,12},{12,8},{9,1... | collective-permute-start | bytes 1179656 | tf_op jit(solution)/shard_map/ppermute | solution.py:438

commit v5 on v4

--- a/solution.py
+++ b/solution.py
@@ -317,7 +317,7 @@
     def tiles(ref, low, count):
         return ref[:, low : low + count, :].reshape(16 * count, LANES)
 
-    block = 128
+    block = 256
     places = (columns(False), columns(True))
     for late in range(2):
         for part in range(256 // block):
@@ -358,7 +358,7 @@
             )
 
 
-def unpack_kernel(came, att, keys, values):
+def unpack_kernel(came, att, cache):
     for n in range(16):
         xa, xb, y = n // 8, (n // 4) % 2, n % 4
         a = xa * 4 + y
@@ -368,8 +368,8 @@
         for slot in range(2):
             rows = slice((xb * 2 + slot) * TILE, (xb * 2 + slot + 1) * TILE)
             low = 32 + slot * 2 * TILE
-            keys[rows, cols] = came[n, low : low + TILE, :]
-            values[rows, cols] = came[n, low + TILE : low + 2 * TILE, :]
+            cache[rows, 0, cols] = came[n, low : low + TILE, :]
+            cache[rows, 1, cols] = came[n, low + TILE : low + 2 * TILE, :]
 
 
 def shape(dims, dtype=BF16):
@@ -444,22 +444,21 @@
     answered = call(
         attend_kernel,
         shape((16, 160, LANES)),
-        [pltpu.VMEM((128, 4096), F32)],
+        [pltpu.VMEM((256, 4096), F32)],
         [S, S, V, V, V],
         flops=1_000_000_000,
         nbytes=3_000_000,
         name="attend",
     )(meta, slots, mine, twin, mark)
     came = lax.all_to_all(answered, ("x", "y"), 0, 0, tiled=True)
-    attention_out, cache_keys, cache_values = call(
+    attention_out, decode_cache = call(
         unpack_kernel,
-        [shape((rows, 1024)), shape((128, 1024)), shape((128, 1024))],
+        [shape((rows, 1024)), shape((128, 2, 1024))],
         (),
         [V],
         nbytes=1_300_000,
         name="unpack",
     )(came)
-    decode_cache = jnp.stack([cache_keys, cache_values], axis=1)
 
     reversed_taps = jnp.pad(mr_taps[:, ::-1].astype(F32), ((0, 0), (1, 127)))
     hyena_stream, filter_state = call(

time: 83.6 us -> 82.9 us (level)
  local copies, waits for them, and re-layouts: 2.6 us -> 1.27 us
    unnamed x25 -> x24, local copies, waits for them, and re-layouts: 1.51 us -> 0.17 us
where the time goes in v5:
time: 82.9 us; the launch traced here: 82.5 us
  starting transfers between devices  34.1 us (41%)
  waiting for transfers between devices  29.2 us (35%)
  Pallas kernels  15.9 us (19%)
  local copies, waits for them, and re-layouts  1.27 us (2%)
  other arithmetic  1.1 us (1%)
  between operations  0.9 us (1%)
    ppermute x4, starting transfers between devices, ctx_route(): return lax.ppermute(array, CTX, pairs)  14.6 us
    all_to_all x1, waiting for transfers between devices, body(): mine = lax.all_to_all(heads, ('x', 'y'), 0, 0, tiled=True)  10.9 us
    all_to_all x1, starting transfers between devices, body(): mine = lax.all_to_all(heads, ('x', 'y'), 0, 0, tiled=True)  10.6 us
    all_to_all x1, waiting for transfers between devices, body(): came = lax.all_to_all(answered, ('x', 'y'), 0, 0, tiled=True)  10.2 us
    pallas_call x1, Pallas kernels, body(): call(attend_kernel, shape((16, 160, LANES)), [pltpu.VMEM((256, 4096), F32...  4.39 us
    all_to_all x1, starting transfers between devices, body(): came = lax.all_to_all(answered, ('x', 'y'), 0, 0, tiled=True)  3.74 us
    ppermute x1, waiting for transfers between devices, body(): half = sums + lax.ppermute(sums, 'tp', [(i, i ^ 1) for i in range(4)])  2.98 us
    pallas_call x1, Pallas kernels, body(): call(stats_kernel, shape((TILE, LANES), F32), [pltpu.VMEM((rows, channels...  2.57 us
  transfers between devices with their start and end apart: 12, of which 7 were waited for; matrix products, arithmetic and copies ran while one was open for 1% of the time, Pallas kernels for 17%

profile of v5, /device:TPU:224, one launch (start us, length us, event | category | flops | bytes accessed | tf_op | source)
XLA Modules:
  0.0 82.5 jit_solution(17664030640527157927)
XLA Ops:
  0.6 0.0 copy-start.1
  0.6 0.0 copy-start
  0.7 0.9 %fusion = (bf16[8,2048]{1,0:T(8,128)(2,1)S(1)}, bf16[8,2048]{1,0:T(8,128)(2,1)S(1)}, bf16[8,2048]{1,0:T(8,128)(2,1)S(1)}, bf16[8,2048]{1,0:T(8,128)(2,1)S(1)}) fusion(bf16[64,2048]{1,0:T(8,128)(2,1)} %stream.5, bf16[64,2048]{1,0:T(8,128)(2,1)} %pre.5), kind=kLoop, calls=%fused_computation.9 | loop fusion | bytes 262144 | tf_op jit(solution)/shard_map/slice | solution.py:386
  1.6 0.0 copy-start.8
  1.6 0.0 copy-start.3
  1.6 0.0 copy-start.6
  1.6 0.0 copy-start.7
  1.7 1.0 %pad_maximum_fusion.1 = bf16[96,1024]{1,0:T(8,128)(2,1)S(1)} fusion(bf16[16,1024]{1,0:T(8,128)(2,1)S(1)} %get-tuple-element.35, bf16[16,1024]{1,0:T(8,128)(2,1)S(1)} %get-tuple-element.34, bf16[64,1024]{1,0:T(8,128)(2,1)} %k.1), kind=kLoop, calls=%fused_computation.1 | loop fusion | flops 589824 | bytes 393216 | tf_op jit(solution)/shard_map/concatenate | solution.py:390
  2.6 1.0 %collective-permute-start = (bf16[96,1024]{1,0:T(8,128)(2,1)S(1)}, bf16[96,1024]{1,0:T(8,128)(2,1)S(1)}, u32[]{:S(2)}, u32[]{:S(2)}) collective-permute-start(bf16[96,1024]{1,0:T(8,128)(2,1)S(1)} %pad_maximum_fusion.1), channel_id=1, source_target_pairs={{0,252},{4,8},{8,4},{12,16},{16,12},{20,24},{24,20},{28,32},{32,28... | collective-permute-start | bytes 589832 | tf_op jit(solution)/shard_map/ppermute | solution.py:27
  3.6 1.7 %collective-permute-start.1 = (bf16[16,2048]{1,0:T(8,128)(2,1)S(1)}, bf16[16,2048]{1,0:T(8,128)(2,1)S(1)}, u32[]{:S(2)}, u32[]{:S(2)}) collective-permute-start(bf16[16,2048]{1,0:T(8,128)(2,1)S(1)} %get-tuple-element.32), channel_id=1, source_target_pairs={{0,4},{4,0},{1,5},{5,1},{2,6},{6,2},{3,7},{7,3},{8,12},{12,8},{9,1... | collective-permute-start | bytes 196616 | tf_op jit(solution)/shard_map/ppermute | solution.py:389
  5.3 0.9 %collective-permute-done.1.near.hl = bf16[16,2048]{1,0:T(8,128)(2,1)S(1)} collective-permute-done((bf16[16,2048]{1,0:T(8,128)(2,1)S(1)}, bf16[16,2048]{1,0:T(8,128)(2,1)S(1)}, u32[]{:S(2)}, u32[]{:S(2)}) %collective-permute-start.1) | collective-permute-done | bytes 65568 | tf_op jit(solution)/shard_map/ppermute | solution.py:389
  6.2 7.6 %collective-permute-start.2 = (bf16[64,1024]{1,0:T(8,128)(2,1)}, bf16[64,1024]{1,0:T(8,128)(2,1)S(1)}, u32[]{:S(2)}, u32[]{:S(2)}) collective-permute-start(bf16[64,1024]{1,0:T(8,128)(2,1)} %v.1), channel_id=1, source_target_pairs={{0,252},{4,8},{8,4},{12,16},{16,12},{20,24},{24,20},{28,32},{32,28... | collective-permute-start | bytes 393224 | tf_op jit(solution)/shard_map/ppermute | solution.py:27
  13.8 0.1 stack.29.meta
  13.8 0.0 copy-done.1
  13.9 2.6 %stats.1.partial = f32[32,128]{1,0:T(8,128)S(1)} custom-call(bf16[64,2048]{1,0:T(8,128)(2,1)S(1)} %copy-done, bf16[64,2048]{1,0:T(8,128)(2,1)S(1)} %copy-done.1, bf16[64,2048]{1,0:T(8,128)(2,1)S(1)} %copy-done.2, bf16[7,2048]{1,0:T(8,128)(2,1)S(1)} %bitcast.8), custom_call_target="tpu_custom_call" | custom-call | flops 15000000 | bytes 800000 | tf_op jit(solution)/shard_map/stats/pallas_call | solution.py:394
  16.4 0.0 collective-permute-done.far.he
  16.4 1.6 %head.1 = f32[32,128]{1,0:T(8,128)S(1)} custom-call(s32[8]{0:T(128)S(1)} %stack.29.meta, bf16[64,2048]{1,0:T(8,128)(2,1)S(1)} %copy-done, bf16[64,2048]{1,0:T(8,128)(2,1)S(1)} %copy-done.1, bf16[64,2048]{1,0:T(8,128)(2,1)S(1)} %copy-done.2, bf16[7,2048]{1,0:T(8,128)(2,1)S(1)} %bitcast.9, bf16[96,1024]{1,0:T(8,128)(2,1)S(1)} %collective-permute-done.far.he, ...), custom_call_target="tpu_custom_call" | custom-call | flops 5000000 | bytes 300000 | tf_op jit(solution)/shard_map/head/pallas_call | solution.py:403
  18.1 1.1 %collective-permute-start.3 = (f32[32,128]{1,0:T(8,128)S(1)}, f32[32,128]{1,0:T(8,128)S(1)}, u32[]{:S(2)}, u32[]{:S(2)}) collective-permute-start(f32[32,128]{1,0:T(8,128)S(1)} %head.1), channel_id=1, source_target_pairs={{0,1},{1,0},{2,3},{3,2},{4,5},{5,4},{6,7},{7,6},{8,9},{9,8},{10,11... | collective-permute-start | bytes 49160 | tf_op jit(solution)/shard_map/ppermute | solution.py:412
  19.2 3.0 %collective-permute-done.3 = f32[32,128]{1,0:T(8,128)S(1)} collective-permute-done((f32[32,128]{1,0:T(8,128)S(1)}, f32[32,128]{1,0:T(8,128)S(1)}, u32[]{:S(2)}, u32[]{:S(2)}) %collective-permute-start.3) | collective-permute-done | bytes 16416 | tf_op jit(solution)/shard_map/ppermute | solution.py:412
  22.2 0.0 collective-permute-done.2.far_values
  22.2 1.3 %collective-permute-start.4 = (f32[32,128]{1,0:T(8,128)S(1)}, f32[32,128]{1,0:T(8,128)S(1)}, u32[]{:S(2)}, u32[]{:S(2)}) collective-permute-start(f32[32,128]{1,0:T(8,128)S(1)} %add.23.half), channel_id=1, source_target_pairs={{0,2},{1,3},{2,0},{3,1},{4,6},{5,7},{6,4},{7,5},{8,10},{9,11},{10,... | collective-permute-start | bytes 49160 | tf_op jit(solution)/shard_map/ppermute | solution.py:414
  23.5 0.0 copy-done.8
  23.5 0.1 copy.15.owner_col
  23.6 1.2 %pack.1 = bf16[16,288,128]{2,1,0:T(8,128)(2,1)} custom-call(bf16[64,1024]{1,0:T(8,128)(2,1)S(1)} %copy-done.3, bf16[64,1024]{1,0:T(8,128)(2,1)S(1)} %copy-done.6, bf16[96,1024]{1,0:T(8,128)(2,1)S(1)} %collective-permute-done.far.he, bf16[64,1024]{1,0:T(8,128)(2,1)S(1)} %collective-permute-done.2.far_values, bf16[64,1024]{1,0:T(8,128)(2,1)S(1)} %copy-done.7), custom_call_target="tpu_custom_call" | custom-call | bytes 2000000 | tf_op jit(solution)/shard_map/pack/pallas_call | solution.py:428
  24.8 10.6 %all-to-all-start = ((bf16[16,288,128]{2,1,0:T(8,128)(2,1)}), bf16[16,288,128]{2,1,0:T(8,128)(2,1)S(1)}, u32[]{:S(2)}, u32[]{:S(2)}) async-start(bf16[16,288,128]{2,1,0:T(8,128)(2,1)} %pack.1), calls=%async_computation | async-start | bytes 2359296 | tf_op jit(solution)/shard_map/all_to_all | solution.py:431
  35.4 0.0 collective-permute-done.4.other
  35.4 1.7 %mix.1 = (bf16[64,2048]{1,0:T(8,128)(2,1)S(1)}, bf16[32,2048]{1,0:T(8,128)(2,1)S(1)}, bf16[32,2048]{1,0:T(8,128)(2,1)S(1)}) custom-call(s32[8]{0:T(128)S(1)} %stack.29.meta, bf16[64,2048]{1,0:T(8,128)(2,1)S(1)} %copy-done, bf16[64,2048]{1,0:T(8,128)(2,1)S(1)} %copy-done.1, bf16[64,2048]{1,0:T(8,128)(2,1)S(1)} %copy-done.2, bf16[64,2048]{1,0:T(8,128)(2,1)S(1)} %copy-done.9, ...), custom_call_target="tpu_custom_call" | custom-call | flops 20000000000 | bytes 3500000 | tf_op jit(solution)/shard_map/mix/pallas_call | solution.py:415
  37.1 0.4 collective-permute-start.5
  37.5 1.1 %collective-permute-done.5.got = bf16[32,2048]{1,0:T(8,128)(2,1)S(1)} collective-permute-done((bf16[32,2048]{1,0:T(8,128)(2,1)S(1)}, bf16[32,2048]{1,0:T(8,128)(2,1)S(1)}, u32[]{:S(2)}, u32[]{:S(2)}) %collective-permute-start.5) | collective-permute-done | bytes 131104 | tf_op jit(solution)/shard_map/ppermute | solution.py:426
  38.6 0.7 collective-permute-start.7
  39.3 5.4 %collective-permute-start.6 = (bf16[64,2048]{1,0:T(8,128)(2,1)S(1)}, bf16[64,2048]{1,0:T(8,128)(2,1)S(1)}, u32[]{:S(2)}, u32[]{:S(2)}) collective-permute-start(bf16[64,2048]{1,0:T(8,128)(2,1)S(1)} %constant_dynamic-update-slice_fusion), channel_id=1, source_target_pairs={{4,8},{8,4},{12,16},{16,12},{20,24},{24,20},{28,32},{32,28},{36,40... | collective-permute-start | bytes 786440 | tf_op jit(solution)/shard_map/ppermute | solution.py:27
  44.7 10.9 %all-to-all-done.mine = bf16[16,288,128]{2,1,0:T(8,128)(2,1)S(1)} async-done(((bf16[16,288,128]{2,1,0:T(8,128)(2,1)}), bf16[16,288,128]{2,1,0:T(8,128)(2,1)S(1)}, u32[]{:S(2)}, u32[]{:S(2)}) %all-to-all-start) | async-done | bytes 1179680 | tf_op jit(solution)/shard_map/all_to_all | solution.py:431
  55.6 0.0 collective-permute-start.9
  55.6 0.8 slots.1
  56.5 0.0 collective-permute-done.7.two
  56.5 2.0 %collective-permute-done.9.twin = bf16[16,288,128]{2,1,0:T(8,128)(2,1)S(1)} collective-permute-done((bf16[16,288,128]{2,1,0:T(8,128)(2,1)S(1)}, bf16[16,288,128]{2,1,0:T(8,128)(2,1)S(1)}, u32[]{:S(2)}, u32[]{:S(2)}) %collective-permute-start.9) | collective-permute-done | bytes 1179680 | tf_op jit(solution)/shard_map/ppermute | solution.py:439
  58.5 4.4 %attend.1 = bf16[16,160,128]{2,1,0:T(8,128)(2,1)} custom-call(s32[8]{0:T(128)S(1)} %stack.29.meta, s32[4,128]{1,0:T(4,128)S(1)} %slots.1, bf16[16,288,128]{2,1,0:T(8,128)(2,1)S(1)} %all-to-all-done.mine, bf16[16,288,128]{2,1,0:T(8,128)(2,1)S(1)} %collective-permute-done.9.twin, bf16[16,128]{1,0:T(8,128)(2,1)S(1)} %slice.31.after), custom_call_target="tpu_custom_call" | custom-call | flops 1000000000 | bytes 3000000 | tf_op jit(solution)/shard_map/attend/pallas_call | solution.py:444
  62.9 3.7 %all-to-all-start.1 = ((bf16[16,160,128]{2,1,0:T(8,128)(2,1)}), bf16[16,160,128]{2,1,0:T(8,128)(2,1)S(1)}, u32[]{:S(2)}, u32[]{:S(2)}) async-start(bf16[16,160,128]{2,1,0:T(8,128)(2,1)} %attend.1), calls=%async_computation.1 | async-start | bytes 1310720 | tf_op jit(solution)/shard_map/all_to_all | solution.py:453
  66.6 0.0 collective-permute-done.6.one
  66.7 0.7 collective-permute-start.8
  67.4 0.0 copy-done.10
  67.4 0.1 rev.3
  67.5 0.1 pad_convert_fusion.taps
  67.6 1.2 %collective-permute-done.8.rest = bf16[96,2048]{1,0:T(8,128)(2,1)S(1)} collective-permute-done((bf16[96,2048]{1,0:T(8,128)(2,1)S(1)}, bf16[96,2048]{1,0:T(8,128)(2,1)S(1)}, u32[]{:S(2)}, u32[]{:S(2)}) %collective-permute-start.8) | collective-permute-done | bytes 393248 | tf_op jit(solution)/shard_map/ppermute | solution.py:438
  68.8 0.0 copy-done.4
  68.8 1.9 %conv.1 = (bf16[64,2048]{1,0:T(8,128)(2,1)}, bf16[128,2048]{1,0:T(8,128)(2,1)}) custom-call(s32[8]{0:T(128)S(1)} %stack.29.meta, f32[4,256]{1,0:T(4,128)S(1)} %pad_convert_fusion.taps, bf16[64,2048]{1,0:T(8,128)(2,1)S(1)} %get-tuple-element.19.mixed, bf16[64,2048]{1,0:T(8,128)(2,1)S(1)} %copy-done.4, bf16[32,2048]{1,0:T(8,128)(2,1)S(1)} %get-tuple-element.20.keep, ...), custom_call_target="tpu_custom_call" | custom-call | flops 100000000 | bytes 3000000 | tf_op jit(solution)/shard_map/conv/pallas_call | solution.py:464
  70.6 10.2 %all-to-all-done.1.came = bf16[16,160,128]{2,1,0:T(8,128)(2,1)S(1)} async-done(((bf16[16,160,128]{2,1,0:T(8,128)(2,1)}), bf16[16,160,128]{2,1,0:T(8,128)(2,1)S(1)}, u32[]{:S(2)}, u32[]{:S(2)}) %all-to-all-start.1) | async-done | bytes 655392 | tf_op jit(solution)/shard_map/all_to_all | solution.py:453
  80.8 1.7 %unpack.1 = (bf16[64,1024]{1,0:T(8,128)(2,1)}, bf16[128,2,1024]{2,1,0:T(2,128)(2,1)}) custom-call(bf16[16,160,128]{2,1,0:T(8,128)(2,1)S(1)} %all-to-all-done.1.came), custom_call_target="tpu_custom_call" | custom-call | bytes 1300000 | tf_op jit(solution)/shard_map/unpack/pallas_call | solution.py:454
  (20 shorter events, 0.1 us)
Async XLA Ops:
  0.6 13.2 %copy-start.1 = (bf16[64,2048]{1,0:T(8,128)(2,1)S(1)}, bf16[64,2048]{1,0:T(8,128)(2,1)}, u32[]{:S(2)}) copy-start(bf16[64,2048]{1,0:T(8,128)(2,1)} %pre.5) | copy-start | bytes 786436
  0.6 13.2 %copy-start = (bf16[64,2048]{1,0:T(8,128)(2,1)S(1)}, bf16[64,2048]{1,0:T(8,128)(2,1)}, u32[]{:S(2)}) copy-start(bf16[64,2048]{1,0:T(8,128)(2,1)} %stream.5) | copy-start | bytes 786436
  0.7 13.2 %copy-start.2 = (bf16[64,2048]{1,0:T(8,128)(2,1)S(1)}, bf16[64,2048]{1,0:T(8,128)(2,1)}, u32[]{:S(2)}) copy-start(bf16[64,2048]{1,0:T(8,128)(2,1)} %post.6) | copy-start | bytes 786436
  0.7 13.2 %copy-start.5 = (bf16[2048,7]{0,1:T(8,128)(2,1)S(1)}, bf16[2048,7]{0,1:T(8,128)(2,1)}, u32[]{:S(2)}) copy-start(bf16[2048,7]{0,1:T(8,128)(2,1)} %param.14) | copy-start | bytes 86020
  1.6 21.9 %copy-start.8 = (s32[128,1]{0,1:T(1,128)S(1)}, s32[128,1]{0,1:T(1,128)}, u32[]{:S(2)}) copy-start(s32[128,1]{0,1:T(1,128)} %param.21) | copy-start | bytes 1540
  1.6 22.0 %copy-start.3 = (bf16[64,1024]{1,0:T(8,128)(2,1)S(1)}, bf16[64,1024]{1,0:T(8,128)(2,1)}, u32[]{:S(2)}) copy-start(bf16[64,1024]{1,0:T(8,128)(2,1)} %k.1) | copy-start | bytes 393220
  1.6 22.0 %copy-start.6 = (bf16[64,1024]{1,0:T(8,128)(2,1)S(1)}, bf16[64,1024]{1,0:T(8,128)(2,1)}, u32[]{:S(2)}) copy-start(bf16[64,1024]{1,0:T(8,128)(2,1)} %v.1) | copy-start | bytes 393220
  1.6 21.9 %copy-start.7 = (bf16[64,1024]{1,0:T(8,128)(2,1)S(1)}, bf16[64,1024]{1,0:T(8,128)(2,1)}, u32[]{:S(2)}) copy-start(bf16[64,1024]{1,0:T(8,128)(2,1)} %q.1) | copy-start | bytes 393220
  2.6 13.8 %collective-permute-start = (bf16[96,1024]{1,0:T(8,128)(2,1)S(1)}, bf16[96,1024]{1,0:T(8,128)(2,1)S(1)}, u32[]{:S(2)}, u32[]{:S(2)}) collective-permute-start(bf16[96,1024]{1,0:T(8,128)(2,1)S(1)} %pad_maximum_fusion.1), channel_id=1, source_target_pairs={{0,252},{4,8},{8,4},{12,16},{16,12},{20,24},{24,20},{28,32},{32,28... | collective-permute-start | bytes 589832 | tf_op jit(solution)/shard_map/ppermute | solution.py:27
  3.6 2.6 %collective-permute-start.1 = (bf16[16,2048]{1,0:T(8,128)(2,1)S(1)}, bf16[16,2048]{1,0:T(8,128)(2,1)S(1)}, u32[]{:S(2)}, u32[]{:S(2)}) collective-permute-start(bf16[16,2048]{1,0:T(8,128)(2,1)S(1)} %get-tuple-element.32), channel_id=1, source_target_pairs={{0,4},{4,0},{1,5},{5,1},{2,6},{6,2},{3,7},{7,3},{8,12},{12,8},{9,1... | collective-permute-start | bytes 196616 | tf_op jit(solution)/shard_map/ppermute | solution.py:389
  6.2 16.0 %collective-permute-start.2 = (bf16[64,1024]{1,0:T(8,128)(2,1)}, bf16[64,1024]{1,0:T(8,128)(2,1)S(1)}, u32[]{:S(2)}, u32[]{:S(2)}) collective-permute-start(bf16[64,1024]{1,0:T(8,128)(2,1)} %v.1), channel_id=1, source_target_pairs={{0,252},{4,8},{8,4},{12,16},{16,12},{20,24},{24,20},{28,32},{32,28... | collective-permute-start | bytes 393224 | tf_op jit(solution)/shard_map/ppermute | solution.py:27
  18.1 4.1 %collective-permute-start.3 = (f32[32,128]{1,0:T(8,128)S(1)}, f32[32,128]{1,0:T(8,128)S(1)}, u32[]{:S(2)}, u32[]{:S(2)}) collective-permute-start(f32[32,128]{1,0:T(8,128)S(1)} %head.1), channel_id=1, source_target_pairs={{0,1},{1,0},{2,3},{3,2},{4,5},{5,4},{6,7},{7,6},{8,9},{9,8},{10,11... | collective-permute-start | bytes 49160 | tf_op jit(solution)/shard_map/ppermute | solution.py:412
  22.2 13.2 %collective-permute-start.4 = (f32[32,128]{1,0:T(8,128)S(1)}, f32[32,128]{1,0:T(8,128)S(1)}, u32[]{:S(2)}, u32[]{:S(2)}) collective-permute-start(f32[32,128]{1,0:T(8,128)S(1)} %add.23.half), channel_id=1, source_target_pairs={{0,2},{1,3},{2,0},{3,1},{4,6},{5,7},{6,4},{7,5},{8,10},{9,11},{10,... | collective-permute-start | bytes 49160 | tf_op jit(solution)/shard_map/ppermute | solution.py:414
  24.8 10.6 %copy-start.9 = (bf16[64,2048]{1,0:T(8,128)(2,1)S(1)}, bf16[64,2048]{1,0:T(8,128)(2,1)}, u32[]{:S(2)}) copy-start(bf16[64,2048]{1,0:T(8,128)(2,1)} %mrpre.1) | copy-start | bytes 786436
  24.8 30.8 %all-to-all-start = ((bf16[16,288,128]{2,1,0:T(8,128)(2,1)}), bf16[16,288,128]{2,1,0:T(8,128)(2,1)S(1)}, u32[]{:S(2)}, u32[]{:S(2)}) async-start(bf16[16,288,128]{2,1,0:T(8,128)(2,1)} %pack.1), calls=%async_computation | async-start | bytes 2359296 | tf_op jit(solution)/shard_map/all_to_all | solution.py:431
  37.1 1.4 %collective-permute-start.5 = (bf16[32,2048]{1,0:T(8,128)(2,1)S(1)}, bf16[32,2048]{1,0:T(8,128)(2,1)S(1)}, u32[]{:S(2)}, u32[]{:S(2)}) collective-permute-start(bf16[32,2048]{1,0:T(8,128)(2,1)S(1)} %get-tuple-element.21.give), channel_id=1, source_target_pairs={{0,4},{4,0},{1,5},{5,1},{2,6},{6,2},{3,7},{7,3},{8,12},{12,8},{9,1... | collective-permute-start | bytes 393224 | tf_op jit(solution)/shard_map/ppermute | solution.py:426
  38.6 17.9 %collective-permute-start.7 = (bf16[64,2048]{1,0:T(8,128)(2,1)S(1)}, bf16[64,2048]{1,0:T(8,128)(2,1)S(1)}, u32[]{:S(2)}, u32[]{:S(2)}) collective-permute-start(bf16[64,2048]{1,0:T(8,128)(2,1)S(1)} %constant_dynamic-update-slice_fusion), channel_id=1, source_target_pairs={{4,16},{12,24},{16,4},{20,32},{24,12},{28,40},{32,20},{36,48},{40,... | collective-permute-start | bytes 786440 | tf_op jit(solution)/shard_map/ppermute | solution.py:27
  39.3 27.4 %collective-permute-start.6 = (bf16[64,2048]{1,0:T(8,128)(2,1)S(1)}, bf16[64,2048]{1,0:T(8,128)(2,1)S(1)}, u32[]{:S(2)}, u32[]{:S(2)}) collective-permute-start(bf16[64,2048]{1,0:T(8,128)(2,1)S(1)} %constant_dynamic-update-slice_fusion), channel_id=1, source_target_pairs={{4,8},{8,4},{12,16},{16,12},{20,24},{24,20},{28,32},{32,28},{36,40... | collective-permute-start | bytes 786440 | tf_op jit(solution)/shard_map/ppermute | solution.py:27
  55.6 2.8 %collective-permute-start.9 = (bf16[16,288,128]{2,1,0:T(8,128)(2,1)S(1)}, bf16[16,288,128]{2,1,0:T(8,128)(2,1)S(1)}, u32[]{:S(2)}, u32[]{:S(2)}) collective-permute-start(bf16[16,288,128]{2,1,0:T(8,128)(2,1)S(1)} %all-to-all-done.mine), channel_id=1, source_target_pairs={{0,4},{4,0},{1,5},{5,1},{2,6},{6,2},{3,7},{7,3},{8,12},{12,8},{9,1... | collective-permute-start | bytes 3538952 | tf_op jit(solution)/shard_map/ppermute | solution.py:439
  62.9 4.5 %copy-start.10 = (bf16[4,128]{1,0:T(4,128)(2,1)S(1)}, bf16[4,128]{1,0:T(4,128)(2,1)}, u32[]{:S(2)}) copy-start(bf16[4,128]{1,0:T(4,128)(2,1)} %param.17) | copy-start | bytes 3076
  62.9 5.9 %copy-start.4 = (bf16[64,2048]{1,0:T(8,128)(2,1)S(1)}, bf16[64,2048]{1,0:T(8,128)(2,1)}, u32[]{:S(2)}) copy-start(bf16[64,2048]{1,0:T(8,128)(2,1)} %post.7) | copy-start | bytes 786436
  62.9 17.9 %all-to-all-start.1 = ((bf16[16,160,128]{2,1,0:T(8,128)(2,1)}), bf16[16,160,128]{2,1,0:T(8,128)(2,1)S(1)}, u32[]{:S(2)}, u32[]{:S(2)}) async-start(bf16[16,160,128]{2,1,0:T(8,128)(2,1)} %attend.1), calls=%async_computation.1 | async-start | bytes 1310720 | tf_op jit(solution)/shard_map/all_to_all | solution.py:453
  66.7 2.1 %collective-permute-start.8 = (bf16[96,2048]{1,0:T(8,128)(2,1)S(1)}, bf16[96,2048]{1,0:T(8,128)(2,1)S(1)}, u32[]{:S(2)}, u32[]{:S(2)}) collective-permute-start(bf16[96,2048]{1,0:T(8,128)(2,1)S(1)} %pad_maximum_fusion), channel_id=1, source_target_pairs={{0,4},{4,0},{1,5},{5,1},{2,6},{6,2},{3,7},{7,3},{8,12},{12,8},{9,1... | collective-permute-start | bytes 1179656 | tf_op jit(solution)/shard_map/ppermute | solution.py:438

commit v6 on v5

--- a/solution.py
+++ b/solution.py
@@ -140,7 +140,7 @@
         return tuple(squares)
 
     zero = jnp.zeros((8, LANES), F32)
-    squares = lax.fori_loop(0, chunks, prepare, (zero, zero), unroll=2)
+    squares = lax.fori_loop(0, chunks, prepare, (zero, zero), unroll=4)
     lane = lax.broadcasted_iota(jnp.int32, (8, LANES), 1)
     packed = zero
     for tile in range(2):
@@ -224,7 +224,7 @@
         give[:, cs] = jnp.where(odd, values[1], values[0])
         return carry
 
-    lax.fori_loop(0, stream.shape[1] // LANES, one, 0)
+    lax.fori_loop(0, stream.shape[1] // LANES, one, 0, unroll=2)
 
 
 def conv_kernel(meta, taps, mixed, post, keep, give, got, one, two, rest, out, state, ext):

time: 82.9 us -> 82.9 us (level)
  no operation moved by 1% of the time
where the time goes in v6:
time: 82.9 us; the launch traced here: 82.5 us
  starting transfers between devices  34.1 us (41%)
  waiting for transfers between devices  29.3 us (35%)
  Pallas kernels  15.8 us (19%)
  local copies, waits for them, and re-layouts  1.27 us (2%)
  other arithmetic  1.1 us (1%)
  between operations  0.9 us (1%)
    ppermute x4, starting transfers between devices, ctx_route(): return lax.ppermute(array, CTX, pairs)  14.6 us
    all_to_all x1, waiting for transfers between devices, body(): mine = lax.all_to_all(heads, ('x', 'y'), 0, 0, tiled=True)  11 us
    all_to_all x1, starting transfers between devices, body(): mine = lax.all_to_all(heads, ('x', 'y'), 0, 0, tiled=True)  10.6 us
    all_to_all x1, waiting for transfers between devices, body(): came = lax.all_to_all(answered, ('x', 'y'), 0, 0, tiled=True)  10.2 us
    pallas_call x1, Pallas kernels, body(): call(attend_kernel, shape((16, 160, LANES)), [pltpu.VMEM((256, 4096), F32...  4.39 us
    all_to_all x1, starting transfers between devices, body(): came = lax.all_to_all(answered, ('x', 'y'), 0, 0, tiled=True)  3.74 us
    ppermute x1, waiting for transfers between devices, body(): half = sums + lax.ppermute(sums, 'tp', [(i, i ^ 1) for i in range(4)])  3 us
    pallas_call x1, Pallas kernels, body(): call(stats_kernel, shape((TILE, LANES), F32), [pltpu.VMEM((rows, channels...  2.57 us
  transfers between devices with their start and end apart: 12, of which 7 were waited for; matrix products, arithmetic and copies ran while one was open for 1% of the time, Pallas kernels for 17%

profile of v6, /device:TPU:224, one launch (start us, length us, event | category | flops | bytes accessed | tf_op | source)
XLA Modules:
  0.0 82.5 jit_solution(13401648056857041416)
XLA Ops:
  0.6 0.0 copy-start.1
  0.6 0.0 copy-start
  0.7 0.0 copy-start.2
  0.7 0.9 %fusion = (bf16[8,2048]{1,0:T(8,128)(2,1)S(1)}, bf16[8,2048]{1,0:T(8,128)(2,1)S(1)}, bf16[8,2048]{1,0:T(8,128)(2,1)S(1)}, bf16[8,2048]{1,0:T(8,128)(2,1)S(1)}) fusion(bf16[64,2048]{1,0:T(8,128)(2,1)} %stream.5, bf16[64,2048]{1,0:T(8,128)(2,1)} %pre.5), kind=kLoop, calls=%fused_computation.9 | loop fusion | bytes 262144 | tf_op jit(solution)/shard_map/slice | solution.py:386
  1.6 0.0 copy-start.8
  1.6 0.0 copy-start.3
  1.6 0.0 copy-start.6
  1.6 0.0 copy-start.7
  1.7 1.0 %pad_maximum_fusion.1 = bf16[96,1024]{1,0:T(8,128)(2,1)S(1)} fusion(bf16[16,1024]{1,0:T(8,128)(2,1)S(1)} %get-tuple-element.35, bf16[16,1024]{1,0:T(8,128)(2,1)S(1)} %get-tuple-element.34, bf16[64,1024]{1,0:T(8,128)(2,1)} %k.1), kind=kLoop, calls=%fused_computation.1 | loop fusion | flops 589824 | bytes 393216 | tf_op jit(solution)/shard_map/concatenate | solution.py:390
  2.6 1.0 %collective-permute-start = (bf16[96,1024]{1,0:T(8,128)(2,1)S(1)}, bf16[96,1024]{1,0:T(8,128)(2,1)S(1)}, u32[]{:S(2)}, u32[]{:S(2)}) collective-permute-start(bf16[96,1024]{1,0:T(8,128)(2,1)S(1)} %pad_maximum_fusion.1), channel_id=1, source_target_pairs={{0,252},{4,8},{8,4},{12,16},{16,12},{20,24},{24,20},{28,32},{32,28... | collective-permute-start | bytes 589832 | tf_op jit(solution)/shard_map/ppermute | solution.py:27
  3.6 1.7 %collective-permute-start.1 = (bf16[16,2048]{1,0:T(8,128)(2,1)S(1)}, bf16[16,2048]{1,0:T(8,128)(2,1)S(1)}, u32[]{:S(2)}, u32[]{:S(2)}) collective-permute-start(bf16[16,2048]{1,0:T(8,128)(2,1)S(1)} %get-tuple-element.32), channel_id=1, source_target_pairs={{0,4},{4,0},{1,5},{5,1},{2,6},{6,2},{3,7},{7,3},{8,12},{12,8},{9,1... | collective-permute-start | bytes 196616 | tf_op jit(solution)/shard_map/ppermute | solution.py:389
  5.3 0.9 %collective-permute-done.1.near.hl = bf16[16,2048]{1,0:T(8,128)(2,1)S(1)} collective-permute-done((bf16[16,2048]{1,0:T(8,128)(2,1)S(1)}, bf16[16,2048]{1,0:T(8,128)(2,1)S(1)}, u32[]{:S(2)}, u32[]{:S(2)}) %collective-permute-start.1) | collective-permute-done | bytes 65568 | tf_op jit(solution)/shard_map/ppermute | solution.py:389
  6.2 7.6 %collective-permute-start.2 = (bf16[64,1024]{1,0:T(8,128)(2,1)}, bf16[64,1024]{1,0:T(8,128)(2,1)S(1)}, u32[]{:S(2)}, u32[]{:S(2)}) collective-permute-start(bf16[64,1024]{1,0:T(8,128)(2,1)} %v.1), channel_id=1, source_target_pairs={{0,252},{4,8},{8,4},{12,16},{16,12},{20,24},{24,20},{28,32},{32,28... | collective-permute-start | bytes 393224 | tf_op jit(solution)/shard_map/ppermute | solution.py:27
  13.8 0.1 stack.29.meta
  13.8 0.0 copy-done.1
  13.9 2.6 %stats.1.partial = f32[32,128]{1,0:T(8,128)S(1)} custom-call(bf16[64,2048]{1,0:T(8,128)(2,1)S(1)} %copy-done, bf16[64,2048]{1,0:T(8,128)(2,1)S(1)} %copy-done.1, bf16[64,2048]{1,0:T(8,128)(2,1)S(1)} %copy-done.2, bf16[7,2048]{1,0:T(8,128)(2,1)S(1)} %bitcast.8), custom_call_target="tpu_custom_call" | custom-call | flops 15000000 | bytes 800000 | tf_op jit(solution)/shard_map/stats/pallas_call | solution.py:394
  16.4 0.0 collective-permute-done.far.he
  16.4 1.6 %head.1 = f32[32,128]{1,0:T(8,128)S(1)} custom-call(s32[8]{0:T(128)S(1)} %stack.29.meta, bf16[64,2048]{1,0:T(8,128)(2,1)S(1)} %copy-done, bf16[64,2048]{1,0:T(8,128)(2,1)S(1)} %copy-done.1, bf16[64,2048]{1,0:T(8,128)(2,1)S(1)} %copy-done.2, bf16[7,2048]{1,0:T(8,128)(2,1)S(1)} %bitcast.9, bf16[96,1024]{1,0:T(8,128)(2,1)S(1)} %collective-permute-done.far.he, ...), custom_call_target="tpu_custom_call" | custom-call | flops 5000000 | bytes 300000 | tf_op jit(solution)/shard_map/head/pallas_call | solution.py:403
  18.1 1.1 %collective-permute-start.3 = (f32[32,128]{1,0:T(8,128)S(1)}, f32[32,128]{1,0:T(8,128)S(1)}, u32[]{:S(2)}, u32[]{:S(2)}) collective-permute-start(f32[32,128]{1,0:T(8,128)S(1)} %head.1), channel_id=1, source_target_pairs={{0,1},{1,0},{2,3},{3,2},{4,5},{5,4},{6,7},{7,6},{8,9},{9,8},{10,11... | collective-permute-start | bytes 49160 | tf_op jit(solution)/shard_map/ppermute | solution.py:412
  19.2 3.0 %collective-permute-done.3 = f32[32,128]{1,0:T(8,128)S(1)} collective-permute-done((f32[32,128]{1,0:T(8,128)S(1)}, f32[32,128]{1,0:T(8,128)S(1)}, u32[]{:S(2)}, u32[]{:S(2)}) %collective-permute-start.3) | collective-permute-done | bytes 16416 | tf_op jit(solution)/shard_map/ppermute | solution.py:412
  22.2 0.0 collective-permute-done.2.far_values
  22.2 1.3 %collective-permute-start.4 = (f32[32,128]{1,0:T(8,128)S(1)}, f32[32,128]{1,0:T(8,128)S(1)}, u32[]{:S(2)}, u32[]{:S(2)}) collective-permute-start(f32[32,128]{1,0:T(8,128)S(1)} %add.23.half), channel_id=1, source_target_pairs={{0,2},{1,3},{2,0},{3,1},{4,6},{5,7},{6,4},{7,5},{8,10},{9,11},{10,... | collective-permute-start | bytes 49160 | tf_op jit(solution)/shard_map/ppermute | solution.py:414
  23.5 0.1 copy.15.owner_col
  23.6 1.2 %pack.1 = bf16[16,288,128]{2,1,0:T(8,128)(2,1)} custom-call(bf16[64,1024]{1,0:T(8,128)(2,1)S(1)} %copy-done.3, bf16[64,1024]{1,0:T(8,128)(2,1)S(1)} %copy-done.6, bf16[96,1024]{1,0:T(8,128)(2,1)S(1)} %collective-permute-done.far.he, bf16[64,1024]{1,0:T(8,128)(2,1)S(1)} %collective-permute-done.2.far_values, bf16[64,1024]{1,0:T(8,128)(2,1)S(1)} %copy-done.7), custom_call_target="tpu_custom_call" | custom-call | bytes 2000000 | tf_op jit(solution)/shard_map/pack/pallas_call | solution.py:428
  24.8 10.6 %all-to-all-start = ((bf16[16,288,128]{2,1,0:T(8,128)(2,1)}), bf16[16,288,128]{2,1,0:T(8,128)(2,1)S(1)}, u32[]{:S(2)}, u32[]{:S(2)}) async-start(bf16[16,288,128]{2,1,0:T(8,128)(2,1)} %pack.1), calls=%async_computation | async-start | bytes 2359296 | tf_op jit(solution)/shard_map/all_to_all | solution.py:431
  35.4 0.0 collective-permute-done.4.other
  35.4 1.6 %mix.1 = (bf16[64,2048]{1,0:T(8,128)(2,1)S(1)}, bf16[32,2048]{1,0:T(8,128)(2,1)S(1)}, bf16[32,2048]{1,0:T(8,128)(2,1)S(1)}) custom-call(s32[8]{0:T(128)S(1)} %stack.29.meta, bf16[64,2048]{1,0:T(8,128)(2,1)S(1)} %copy-done, bf16[64,2048]{1,0:T(8,128)(2,1)S(1)} %copy-done.1, bf16[64,2048]{1,0:T(8,128)(2,1)S(1)} %copy-done.2, bf16[64,2048]{1,0:T(8,128)(2,1)S(1)} %copy-done.9, ...), custom_call_target="tpu_custom_call" | custom-call | flops 20000000000 | bytes 3500000 | tf_op jit(solution)/shard_map/mix/pallas_call | solution.py:415
  37.1 0.4 collective-permute-start.5
  37.4 1.1 %collective-permute-done.5.got = bf16[32,2048]{1,0:T(8,128)(2,1)S(1)} collective-permute-done((bf16[32,2048]{1,0:T(8,128)(2,1)S(1)}, bf16[32,2048]{1,0:T(8,128)(2,1)S(1)}, u32[]{:S(2)}, u32[]{:S(2)}) %collective-permute-start.5) | collective-permute-done | bytes 131104 | tf_op jit(solution)/shard_map/ppermute | solution.py:426
  38.5 0.7 collective-permute-start.7
  39.2 5.4 %collective-permute-start.6 = (bf16[64,2048]{1,0:T(8,128)(2,1)S(1)}, bf16[64,2048]{1,0:T(8,128)(2,1)S(1)}, u32[]{:S(2)}, u32[]{:S(2)}) collective-permute-start(bf16[64,2048]{1,0:T(8,128)(2,1)S(1)} %constant_dynamic-update-slice_fusion), channel_id=1, source_target_pairs={{4,8},{8,4},{12,16},{16,12},{20,24},{24,20},{28,32},{32,28},{36,40... | collective-permute-start | bytes 786440 | tf_op jit(solution)/shard_map/ppermute | solution.py:27
  44.6 11.0 %all-to-all-done.mine = bf16[16,288,128]{2,1,0:T(8,128)(2,1)S(1)} async-done(((bf16[16,288,128]{2,1,0:T(8,128)(2,1)}), bf16[16,288,128]{2,1,0:T(8,128)(2,1)S(1)}, u32[]{:S(2)}, u32[]{:S(2)}) %all-to-all-start) | async-done | bytes 1179680 | tf_op jit(solution)/shard_map/all_to_all | solution.py:431
  55.6 0.0 collective-permute-start.9
  55.6 0.8 slots.1
  56.4 0.0 collective-permute-done.7.two
  56.5 2.0 %collective-permute-done.9.twin = bf16[16,288,128]{2,1,0:T(8,128)(2,1)S(1)} collective-permute-done((bf16[16,288,128]{2,1,0:T(8,128)(2,1)S(1)}, bf16[16,288,128]{2,1,0:T(8,128)(2,1)S(1)}, u32[]{:S(2)}, u32[]{:S(2)}) %collective-permute-start.9) | collective-permute-done | bytes 1179680 | tf_op jit(solution)/shard_map/ppermute | solution.py:439
  58.5 4.4 %attend.1 = bf16[16,160,128]{2,1,0:T(8,128)(2,1)} custom-call(s32[8]{0:T(128)S(1)} %stack.29.meta, s32[4,128]{1,0:T(4,128)S(1)} %slots.1, bf16[16,288,128]{2,1,0:T(8,128)(2,1)S(1)} %all-to-all-done.mine, bf16[16,288,128]{2,1,0:T(8,128)(2,1)S(1)} %collective-permute-done.9.twin, bf16[16,128]{1,0:T(8,128)(2,1)S(1)} %slice.31.after), custom_call_target="tpu_custom_call" | custom-call | flops 1000000000 | bytes 3000000 | tf_op jit(solution)/shard_map/attend/pallas_call | solution.py:444
  62.9 3.7 %all-to-all-start.1 = ((bf16[16,160,128]{2,1,0:T(8,128)(2,1)}), bf16[16,160,128]{2,1,0:T(8,128)(2,1)S(1)}, u32[]{:S(2)}, u32[]{:S(2)}) async-start(bf16[16,160,128]{2,1,0:T(8,128)(2,1)} %attend.1), calls=%async_computation.1 | async-start | bytes 1310720 | tf_op jit(solution)/shard_map/all_to_all | solution.py:453
  66.6 0.0 collective-permute-done.6.one
  66.7 0.7 collective-permute-start.8
  67.4 0.0 copy-done.10
  67.4 0.1 rev.3
  67.5 0.1 pad_convert_fusion.taps
  67.6 1.2 %collective-permute-done.8.rest = bf16[96,2048]{1,0:T(8,128)(2,1)S(1)} collective-permute-done((bf16[96,2048]{1,0:T(8,128)(2,1)S(1)}, bf16[96,2048]{1,0:T(8,128)(2,1)S(1)}, u32[]{:S(2)}, u32[]{:S(2)}) %collective-permute-start.8) | collective-permute-done | bytes 393248 | tf_op jit(solution)/shard_map/ppermute | solution.py:438
  68.7 0.0 copy-done.4
  68.7 1.9 %conv.1 = (bf16[64,2048]{1,0:T(8,128)(2,1)}, bf16[128,2048]{1,0:T(8,128)(2,1)}) custom-call(s32[8]{0:T(128)S(1)} %stack.29.meta, f32[4,256]{1,0:T(4,128)S(1)} %pad_convert_fusion.taps, bf16[64,2048]{1,0:T(8,128)(2,1)S(1)} %get-tuple-element.19.mixed, bf16[64,2048]{1,0:T(8,128)(2,1)S(1)} %copy-done.4, bf16[32,2048]{1,0:T(8,128)(2,1)S(1)} %get-tuple-element.20.keep, ...), custom_call_target="tpu_custom_call" | custom-call | flops 100000000 | bytes 3000000 | tf_op jit(solution)/shard_map/conv/pallas_call | solution.py:464
  70.6 10.2 %all-to-all-done.1.came = bf16[16,160,128]{2,1,0:T(8,128)(2,1)S(1)} async-done(((bf16[16,160,128]{2,1,0:T(8,128)(2,1)}), bf16[16,160,128]{2,1,0:T(8,128)(2,1)S(1)}, u32[]{:S(2)}, u32[]{:S(2)}) %all-to-all-start.1) | async-done | bytes 655392 | tf_op jit(solution)/shard_map/all_to_all | solution.py:453
  80.8 1.7 %unpack.1 = (bf16[64,1024]{1,0:T(8,128)(2,1)}, bf16[128,2,1024]{2,1,0:T(2,128)(2,1)}) custom-call(bf16[16,160,128]{2,1,0:T(8,128)(2,1)S(1)} %all-to-all-done.1.came), custom_call_target="tpu_custom_call" | custom-call | bytes 1300000 | tf_op jit(solution)/shard_map/unpack/pallas_call | solution.py:454
  (20 shorter events, 0.1 us)
Async XLA Ops:
  0.6 13.2 %copy-start.1 = (bf16[64,2048]{1,0:T(8,128)(2,1)S(1)}, bf16[64,2048]{1,0:T(8,128)(2,1)}, u32[]{:S(2)}) copy-start(bf16[64,2048]{1,0:T(8,128)(2,1)} %pre.5) | copy-start | bytes 786436
  0.6 13.2 %copy-start = (bf16[64,2048]{1,0:T(8,128)(2,1)S(1)}, bf16[64,2048]{1,0:T(8,128)(2,1)}, u32[]{:S(2)}) copy-start(bf16[64,2048]{1,0:T(8,128)(2,1)} %stream.5) | copy-start | bytes 786436
  0.7 13.2 %copy-start.2 = (bf16[64,2048]{1,0:T(8,128)(2,1)S(1)}, bf16[64,2048]{1,0:T(8,128)(2,1)}, u32[]{:S(2)}) copy-start(bf16[64,2048]{1,0:T(8,128)(2,1)} %post.6) | copy-start | bytes 786436
  0.7 13.2 %copy-start.5 = (bf16[2048,7]{0,1:T(8,128)(2,1)S(1)}, bf16[2048,7]{0,1:T(8,128)(2,1)}, u32[]{:S(2)}) copy-start(bf16[2048,7]{0,1:T(8,128)(2,1)} %param.14) | copy-start | bytes 86020
  1.6 21.8 %copy-start.8 = (s32[128,1]{0,1:T(1,128)S(1)}, s32[128,1]{0,1:T(1,128)}, u32[]{:S(2)}) copy-start(s32[128,1]{0,1:T(1,128)} %param.21) | copy-start | bytes 1540
  1.6 22.0 %copy-start.3 = (bf16[64,1024]{1,0:T(8,128)(2,1)S(1)}, bf16[64,1024]{1,0:T(8,128)(2,1)}, u32[]{:S(2)}) copy-start(bf16[64,1024]{1,0:T(8,128)(2,1)} %k.1) | copy-start | bytes 393220
  1.6 21.9 %copy-start.6 = (bf16[64,1024]{1,0:T(8,128)(2,1)S(1)}, bf16[64,1024]{1,0:T(8,128)(2,1)}, u32[]{:S(2)}) copy-start(bf16[64,1024]{1,0:T(8,128)(2,1)} %v.1) | copy-start | bytes 393220
  1.6 21.9 %copy-start.7 = (bf16[64,1024]{1,0:T(8,128)(2,1)S(1)}, bf16[64,1024]{1,0:T(8,128)(2,1)}, u32[]{:S(2)}) copy-start(bf16[64,1024]{1,0:T(8,128)(2,1)} %q.1) | copy-start | bytes 393220
  2.6 13.8 %collective-permute-start = (bf16[96,1024]{1,0:T(8,128)(2,1)S(1)}, bf16[96,1024]{1,0:T(8,128)(2,1)S(1)}, u32[]{:S(2)}, u32[]{:S(2)}) collective-permute-start(bf16[96,1024]{1,0:T(8,128)(2,1)S(1)} %pad_maximum_fusion.1), channel_id=1, source_target_pairs={{0,252},{4,8},{8,4},{12,16},{16,12},{20,24},{24,20},{28,32},{32,28... | collective-permute-start | bytes 589832 | tf_op jit(solution)/shard_map/ppermute | solution.py:27
  3.6 2.6 %collective-permute-start.1 = (bf16[16,2048]{1,0:T(8,128)(2,1)S(1)}, bf16[16,2048]{1,0:T(8,128)(2,1)S(1)}, u32[]{:S(2)}, u32[]{:S(2)}) collective-permute-start(bf16[16,2048]{1,0:T(8,128)(2,1)S(1)} %get-tuple-element.32), channel_id=1, source_target_pairs={{0,4},{4,0},{1,5},{5,1},{2,6},{6,2},{3,7},{7,3},{8,12},{12,8},{9,1... | collective-permute-start | bytes 196616 | tf_op jit(solution)/shard_map/ppermute | solution.py:389
  6.2 16.0 %collective-permute-start.2 = (bf16[64,1024]{1,0:T(8,128)(2,1)}, bf16[64,1024]{1,0:T(8,128)(2,1)S(1)}, u32[]{:S(2)}, u32[]{:S(2)}) collective-permute-start(bf16[64,1024]{1,0:T(8,128)(2,1)} %v.1), channel_id=1, source_target_pairs={{0,252},{4,8},{8,4},{12,16},{16,12},{20,24},{24,20},{28,32},{32,28... | collective-permute-start | bytes 393224 | tf_op jit(solution)/shard_map/ppermute | solution.py:27
  18.1 4.1 %collective-permute-start.3 = (f32[32,128]{1,0:T(8,128)S(1)}, f32[32,128]{1,0:T(8,128)S(1)}, u32[]{:S(2)}, u32[]{:S(2)}) collective-permute-start(f32[32,128]{1,0:T(8,128)S(1)} %head.1), channel_id=1, source_target_pairs={{0,1},{1,0},{2,3},{3,2},{4,5},{5,4},{6,7},{7,6},{8,9},{9,8},{10,11... | collective-permute-start | bytes 49160 | tf_op jit(solution)/shard_map/ppermute | solution.py:412
  22.2 13.2 %collective-permute-start.4 = (f32[32,128]{1,0:T(8,128)S(1)}, f32[32,128]{1,0:T(8,128)S(1)}, u32[]{:S(2)}, u32[]{:S(2)}) collective-permute-start(f32[32,128]{1,0:T(8,128)S(1)} %add.23.half), channel_id=1, source_target_pairs={{0,2},{1,3},{2,0},{3,1},{4,6},{5,7},{6,4},{7,5},{8,10},{9,11},{10,... | collective-permute-start | bytes 49160 | tf_op jit(solution)/shard_map/ppermute | solution.py:414
  24.8 10.6 %copy-start.9 = (bf16[64,2048]{1,0:T(8,128)(2,1)S(1)}, bf16[64,2048]{1,0:T(8,128)(2,1)}, u32[]{:S(2)}) copy-start(bf16[64,2048]{1,0:T(8,128)(2,1)} %mrpre.1) | copy-start | bytes 786436
  24.8 30.8 %all-to-all-start = ((bf16[16,288,128]{2,1,0:T(8,128)(2,1)}), bf16[16,288,128]{2,1,0:T(8,128)(2,1)S(1)}, u32[]{:S(2)}, u32[]{:S(2)}) async-start(bf16[16,288,128]{2,1,0:T(8,128)(2,1)} %pack.1), calls=%async_computation | async-start | bytes 2359296 | tf_op jit(solution)/shard_map/all_to_all | solution.py:431
  37.1 1.4 %collective-permute-start.5 = (bf16[32,2048]{1,0:T(8,128)(2,1)S(1)}, bf16[32,2048]{1,0:T(8,128)(2,1)S(1)}, u32[]{:S(2)}, u32[]{:S(2)}) collective-permute-start(bf16[32,2048]{1,0:T(8,128)(2,1)S(1)} %get-tuple-element.21.give), channel_id=1, source_target_pairs={{0,4},{4,0},{1,5},{5,1},{2,6},{6,2},{3,7},{7,3},{8,12},{12,8},{9,1... | collective-permute-start | bytes 393224 | tf_op jit(solution)/shard_map/ppermute | solution.py:426
  38.5 17.9 %collective-permute-start.7 = (bf16[64,2048]{1,0:T(8,128)(2,1)S(1)}, bf16[64,2048]{1,0:T(8,128)(2,1)S(1)}, u32[]{:S(2)}, u32[]{:S(2)}) collective-permute-start(bf16[64,2048]{1,0:T(8,128)(2,1)S(1)} %constant_dynamic-update-slice_fusion), channel_id=1, source_target_pairs={{4,16},{12,24},{16,4},{20,32},{24,12},{28,40},{32,20},{36,48},{40,... | collective-permute-start | bytes 786440 | tf_op jit(solution)/shard_map/ppermute | solution.py:27
  39.2 27.4 %collective-permute-start.6 = (bf16[64,2048]{1,0:T(8,128)(2,1)S(1)}, bf16[64,2048]{1,0:T(8,128)(2,1)S(1)}, u32[]{:S(2)}, u32[]{:S(2)}) collective-permute-start(bf16[64,2048]{1,0:T(8,128)(2,1)S(1)} %constant_dynamic-update-slice_fusion), channel_id=1, source_target_pairs={{4,8},{8,4},{12,16},{16,12},{20,24},{24,20},{28,32},{32,28},{36,40... | collective-permute-start | bytes 786440 | tf_op jit(solution)/shard_map/ppermute | solution.py:27
  55.6 2.8 %collective-permute-start.9 = (bf16[16,288,128]{2,1,0:T(8,128)(2,1)S(1)}, bf16[16,288,128]{2,1,0:T(8,128)(2,1)S(1)}, u32[]{:S(2)}, u32[]{:S(2)}) collective-permute-start(bf16[16,288,128]{2,1,0:T(8,128)(2,1)S(1)} %all-to-all-done.mine), channel_id=1, source_target_pairs={{0,4},{4,0},{1,5},{5,1},{2,6},{6,2},{3,7},{7,3},{8,12},{12,8},{9,1... | collective-permute-start | bytes 3538952 | tf_op jit(solution)/shard_map/ppermute | solution.py:439
  62.9 4.5 %copy-start.10 = (bf16[4,128]{1,0:T(4,128)(2,1)S(1)}, bf16[4,128]{1,0:T(4,128)(2,1)}, u32[]{:S(2)}) copy-start(bf16[4,128]{1,0:T(4,128)(2,1)} %param.17) | copy-start | bytes 3076
  62.9 5.9 %copy-start.4 = (bf16[64,2048]{1,0:T(8,128)(2,1)S(1)}, bf16[64,2048]{1,0:T(8,128)(2,1)}, u32[]{:S(2)}) copy-start(bf16[64,2048]{1,0:T(8,128)(2,1)} %post.7) | copy-start | bytes 786436
  62.9 17.9 %all-to-all-start.1 = ((bf16[16,160,128]{2,1,0:T(8,128)(2,1)}), bf16[16,160,128]{2,1,0:T(8,128)(2,1)S(1)}, u32[]{:S(2)}, u32[]{:S(2)}) async-start(bf16[16,160,128]{2,1,0:T(8,128)(2,1)} %attend.1), calls=%async_computation.1 | async-start | bytes 1310720 | tf_op jit(solution)/shard_map/all_to_all | solution.py:453
  66.7 2.1 %collective-permute-start.8 = (bf16[96,2048]{1,0:T(8,128)(2,1)S(1)}, bf16[96,2048]{1,0:T(8,128)(2,1)S(1)}, u32[]{:S(2)}, u32[]{:S(2)}) collective-permute-start(bf16[96,2048]{1,0:T(8,128)(2,1)S(1)} %pad_maximum_fusion), channel_id=1, source_target_pairs={{0,4},{4,0},{1,5},{5,1},{2,6},{6,2},{3,7},{7,3},{8,12},{12,8},{9,1... | collective-permute-start | bytes 1179656 | tf_op jit(solution)/shard_map/ppermute | solution.py:438
